TPU v7x, 256 devices: a whole 4x4x8 slice. The times are simulated.
256 devices in a mesh: seq: 32 (over x, z), head: 8 (over y, core).
Axes of the slice: x: 4, y: 4, z: 8, core: 2. Of those that a mesh axis runs over, the one named last changes fastest.
Arguments:
- queries: bfloat16 [8192, 64, 128], P('seq', 'head')
- keys: bfloat16 [8192, 8, 128], P('seq', 'head')
- block_order: int32 [128], P('seq'), may hold values from 0 to 127, each once
- gate_query: bfloat16 [8, 128, 128], P('head'), may hold values from -0.5 to 0.5
- gate_key: bfloat16 [8, 384, 128], P('head'), may hold values from -0.3125 to 0.3125
Outputs:
- loss: float32 [], replicated
- grad_query: float32 [8, 128, 128], P('head')
- grad_key: float32 [8, 384, 128], P('head')
Inputs may be any that keep to these rules, and one draw needn't show every extreme that they name: `block_order`: each block position appears exactly once.
All inputs are finite; a program needn't handle non-finite values.
Results may differ from a plain program's by a relative error of at most 0.0029.
Values may be sent and summed in bfloat16 or wider, within the bound.
No kernel may reach another device: no remote copies, remote signals or barrier semaphores. Data moves between devices by JAX's collectives and lax.ppermute only.
A program may use at most 64 MiB of HBM per device.

v0:
```python
import math

import jax
import jax.numpy as jnp
from jax import lax
from jax.sharding import PartitionSpec as P

BLOCK = 64


HIGH = lax.Precision.HIGHEST


def passed_along(block, axis, distance):
    devices = range(lax.axis_size(axis))
    route = [((i - distance) % len(devices), i) for i in devices]
    return lax.ppermute(block, axis, route)


def shards(queries, keys, block_order, gate_query, gate_key):
    tok, group, width = queries.shape
    local_blocks = tok // BLOCK
    seq_count = lax.axis_size("seq")
    all_blocks = local_blocks * seq_count
    rows = group * tok
    scale = width ** (-0.5)
    key_blocks = keys[:, 0, :].reshape(local_blocks, BLOCK, width)
    qmat = queries.transpose(1, 0, 2).reshape(rows, width)
    offsets = jnp.arange(BLOCK, dtype=jnp.int32)
    qpos_tok = (block_order[:, None] * BLOCK + offsets[None, :]).reshape(tok)
    qpos = jnp.tile(qpos_tok, group)
    qlast = jnp.max(qpos_tok)

    def fold(carry, piece, start):
        keyp, posp = piece
        count = keyp.shape[0]
        span = math.gcd(count, 8)

        def one(step, inner):
            kblk = keyp.reshape(span * BLOCK, width)
            kpos = (posp[:, None] * BLOCK + offsets[None, :]).reshape(span * BLOCK)

            def work(state):
                blockmax, rmax, rsum = state
                scores = (
                    lax.dot_general(
                        qmat, kblk, (((1,), (1,)), ((), ())), preferred_element_type=jnp.float32
                    )
                    * scale
                )
                scores = jnp.where(kpos[None, :] > qpos[:, None], -1e30, scores)
                bmax = jnp.max(scores.reshape(rows, span, BLOCK), axis=-1)
                column = start + step * span
                blockmax = lax.dynamic_update_slice(blockmax, bmax, (jnp.int32(0), column))
                newmax = jnp.maximum(rmax, jnp.max(scores, axis=-1))
                rsum = rsum * jnp.exp(rmax - newmax) + jnp.sum(
                    jnp.exp(scores - newmax[:, None]), axis=-1
                )
                return (blockmax, newmax, rsum)

            return lax.cond(jnp.min(posp) * BLOCK > qlast, lambda state: state, work, inner)

        return lax.fori_loop(0, count // span, one, carry)

    init = (
        jnp.full((rows, all_blocks), -1e30, jnp.float32),
        jnp.full((rows,), -1e30, jnp.float32),
        jnp.zeros((rows,), jnp.float32),
    )

    def turn(step, state):
        carry, kcur, pcur = state
        source = (lax.axis_index("seq") - step) % seq_count
        carry = fold(carry, (kcur, pcur), source * local_blocks)
        kcur, pcur = passed_along((kcur, pcur), "seq", 1)
        return (carry, kcur, pcur)

    carry, kcur, pcur = lax.fori_loop(0, seq_count - 1, turn, (init, key_blocks, block_order))
    source = (lax.axis_index("seq") - (seq_count - 1)) % seq_count
    carry = fold(carry, (kcur, pcur), source * local_blocks)
    blockmax, rmax, rsum = carry
    lse = rmax + jnp.log(rsum)
    probs = jnp.exp(blockmax - lse[:, None])
    pooled = jnp.max(probs.reshape(group, local_blocks, BLOCK, all_blocks), axis=2)
    target = pooled / jnp.sum(pooled, axis=-1, keepdims=True)
    qpool = jnp.mean(
        queries.reshape(local_blocks, BLOCK, group, width), axis=1, dtype=jnp.float32
    ).astype(jnp.bfloat16)
    kmean = jnp.mean(key_blocks, axis=1, dtype=jnp.float32).astype(jnp.bfloat16)
    kpool = jnp.concatenate(
        [jnp.max(key_blocks, axis=1), jnp.min(key_blocks, axis=1), kmean], axis=-1
    )
    qproj = jnp.einsum("bgd,de->gbe", qpool, gate_query[0], preferred_element_type=jnp.float32)
    kproj_own = jnp.dot(kpool, gate_key[0], preferred_element_type=jnp.float32)
    kproj, all_order = (
        lax.all_gather(kproj_own, "seq", axis=0, tiled=True),
        lax.all_gather(block_order, "seq", axis=0, tiled=True),
    )
    gscale = gate_query.shape[2] ** (-0.5)
    logits = jnp.einsum("gbe,ce->gbc", qproj, kproj, precision=HIGH) * gscale
    logits = jnp.where(all_order[None, None, :] > block_order[None, :, None], -1e30, logits)
    logp = jax.nn.log_softmax(logits, axis=-1)
    total = group * keys.shape[1] * lax.axis_size("head") * all_blocks
    safe = jnp.log(jnp.where(target > 0, target, 1.0))
    loss_part = jnp.sum(jnp.where(target > 0, target * (safe - logp), 0.0)) / total
    rowtot = jnp.sum(target, axis=-1, keepdims=True)
    dlogit = (jnp.exp(logp) * rowtot - target) / total
    dqproj = jnp.einsum("gbc,ce->gbe", dlogit, kproj, precision=HIGH) * gscale
    dkproj = jnp.einsum("gbc,gbe->ce", dlogit, qproj, precision=HIGH) * gscale
    grad_q = jnp.einsum("bgd,gbe->de", qpool.astype(jnp.float32), dqproj, precision=HIGH)
    dk_own = lax.psum_scatter(dkproj, "seq", scatter_dimension=0, tiled=True)
    grad_k = jnp.dot(kpool.astype(jnp.float32).T, dk_own, precision=HIGH)
    grad_q, grad_k = lax.psum((grad_q, grad_k), "seq")
    loss = lax.psum(loss_part, ("seq", "head"))
    return (loss, grad_q[None], grad_k[None])


def solution(mesh):
    return jax.shard_map(
        shards,
        mesh=mesh,
        in_specs=(
            P("seq", "head", None),
            P("seq", "head", None),
            P("seq"),
            P("head", None, None),
            P("head", None, None),
        ),
        out_specs=(P(), P("head", None, None), P("head", None, None)),
        check_vma=False,
    )
```

profile of v0, /device:TPU:1, one launch (start us, length us, event | category | flops | bytes accessed | tf_op | source)
XLA Modules:
  0.0 675.9 jit_solution(14452656746880064628)
XLA Ops:
  11.1 20.0 %all-reduce = s32[128]{0:T(128)S(1)} all-reduce(s32[128]{0:T(128)S(1)} %dynamic-update-slice), channel_id=1, replica_groups=mesh['seq'=32,'head'=8] {'seq'}, use_global_device_ids=true, to_apply=%add | all-reduce | flops 128 | bytes 1024
  33.3 34.1 %all-gather = f32[32,4,128]{2,1,0:T(4,128)S(1)} all-gather(f32[1,4,128]{2,1,0:T(4,128)S(1)} %convolution_bitcast_fusion.4), channel_id=1, replica_groups=mesh['seq'=32,'head'=8] {'seq'}, dimensions={0}, use_global_device_ids=true | all-gather | bytes 67584 | tf_op jit(solution)/shard_map/all_gather | solution.py:96
  70.9 273.4 %while.46 = (s32[]{:T(128)}, f32[2048,128]{0,1:T(8,128)S(1)}, f32[2048]{0:T(1024)S(1)}, f32[2048]{0:T(1024)S(1)}, bf16[4,64,128]{2,1,0:T(8,128)(2,1)S(1)}, /*ind...) while((s32[]{:T(128)}, f32[2048,128]{0,1:T(8,128)S(1)}, ...), condition=%wide.region_8.9_spmd.clone, body=%wide.region_1.8_spmd.clone.sunk | while | flops 137883920 | bytes 7518446 | solution.py:78
  76.3 2.9 conditional.5
  85.9 2.9 conditional.5
  110.8 2.9 conditional.5
  120.5 2.9 conditional.5
  128.4 2.9 conditional.5
  137.9 2.9 conditional.5
  174.3 2.9 conditional.5
  181.5 2.9 conditional.5
  191.1 2.9 conditional.5
  203.8 3.1 collective-permute-start.1
  227.7 2.9 conditional.5
  245.0 2.9 conditional.5
  269.5 2.9 conditional.5
  278.2 2.9 conditional.5
  288.0 2.9 conditional.5
  316.1 2.9 conditional.5
  323.4 2.9 conditional.5
  332.9 2.9 conditional.5
  353.5 166.2 %all-reduce.6.cloned.1.call-done = f32[128,128]{1,0:T(8,128)} async-done(((f32[128,128]{1,0:T(8,128)}), f32[128,128]{1,0:T(8,128)}) %all-reduce.6.cloned.1.call-update) | async-done | bytes 65552
  522.0 78.3 %psum.21 = f32[]{:T(128)} all-reduce(f32[]{:T(128)S(6)} %div.35), channel_id=1, replica_groups=mesh['seq'=32,'head'=8] {'seq','head'}, use_global_device_ids=true, to_apply=%region_24.25 | all-reduce | flops 1 | bytes 8 | tf_op jit(solution)/shard_map/psum | solution.py:114
  600.3 65.7 %all-reduce.8.cloned.1.call-done = (f32[1,128,128]{2,1,0:T(8,128)}, f32[1,384,128]{2,1,0:T(8,128)}) async-done(((f32[1,128,128]{2,1,0:T(8,128)}, f32[1,384,128]{2,1,0:T(8,128)}), (f32[1,128,128]{2,1,0:T(8,128)}, f32[1,384,128]{2,1,0:T(8,128)})) %all-reduce.8.cloned.1.call-update) | async-done | bytes 262160 | tf_op jit(solution)/shard_map/psum | solution.py:113
  (688 shorter events, 289.4 us)
Async XLA Ops:
  7.2 512.5 %all-reduce.6.cloned.1.call-start = ((), (), s32[]{:S(2)}) async-start(), calls=%async_computation | async-start | bytes 131072
  79.9 9.0 %collective-permute-start = (bf16[4,64,128]{2,1,0:T(8,128)(2,1)}, bf16[4,64,128]{2,1,0:T(8,128)(2,1)S(1)}, u32[]{:S(2)}, u32[]{:S(2)}) collective-permute-start(bf16[4,64,128]{2,1,0:T(8,128)(2,1)} %copy.56), channel_id=1, source_target_pairs={{248,0},{0,8},{8,16},{16,24},{24,32},{32,40},{40,48},{48,56},{56,6... | collective-permute-start | bytes 196616 | tf_op jit(solution)/shard_map/while/body/eval_jaxpr/ppermute | solution.py:17
  97.4 8.8 %collective-permute-start = (bf16[4,64,128]{2,1,0:T(8,128)(2,1)}, bf16[4,64,128]{2,1,0:T(8,128)(2,1)S(1)}, u32[]{:S(2)}, u32[]{:S(2)}) collective-permute-start(bf16[4,64,128]{2,1,0:T(8,128)(2,1)} %copy.56), channel_id=1, source_target_pairs={{248,0},{0,8},{8,16},{16,24},{24,32},{32,40},{40,48},{48,56},{56,6... | collective-permute-start | bytes 196616 | tf_op jit(solution)/shard_map/while/body/eval_jaxpr/ppermute | solution.py:17
  114.4 9.0 %collective-permute-start = (bf16[4,64,128]{2,1,0:T(8,128)(2,1)}, bf16[4,64,128]{2,1,0:T(8,128)(2,1)S(1)}, u32[]{:S(2)}, u32[]{:S(2)}) collective-permute-start(bf16[4,64,128]{2,1,0:T(8,128)(2,1)} %copy.56), channel_id=1, source_target_pairs={{248,0},{0,8},{8,16},{16,24},{24,32},{32,40},{40,48},{48,56},{56,6... | collective-permute-start | bytes 196616 | tf_op jit(solution)/shard_map/while/body/eval_jaxpr/ppermute | solution.py:17
  132.0 8.8 %collective-permute-start = (bf16[4,64,128]{2,1,0:T(8,128)(2,1)}, bf16[4,64,128]{2,1,0:T(8,128)(2,1)S(1)}, u32[]{:S(2)}, u32[]{:S(2)}) collective-permute-start(bf16[4,64,128]{2,1,0:T(8,128)(2,1)} %copy.56), channel_id=1, source_target_pairs={{248,0},{0,8},{8,16},{16,24},{24,32},{32,40},{40,48},{48,56},{56,6... | collective-permute-start | bytes 196616 | tf_op jit(solution)/shard_map/while/body/eval_jaxpr/ppermute | solution.py:17
  141.5 7.8 %collective-permute-start = (bf16[4,64,128]{2,1,0:T(8,128)(2,1)}, bf16[4,64,128]{2,1,0:T(8,128)(2,1)S(1)}, u32[]{:S(2)}, u32[]{:S(2)}) collective-permute-start(bf16[4,64,128]{2,1,0:T(8,128)(2,1)} %copy.56), channel_id=1, source_target_pairs={{248,0},{0,8},{8,16},{16,24},{24,32},{32,40},{40,48},{48,56},{56,6... | collective-permute-start | bytes 196616 | tf_op jit(solution)/shard_map/while/body/eval_jaxpr/ppermute | solution.py:17
  149.9 9.0 %collective-permute-start = (bf16[4,64,128]{2,1,0:T(8,128)(2,1)}, bf16[4,64,128]{2,1,0:T(8,128)(2,1)S(1)}, u32[]{:S(2)}, u32[]{:S(2)}) collective-permute-start(bf16[4,64,128]{2,1,0:T(8,128)(2,1)} %copy.56), channel_id=1, source_target_pairs={{248,0},{0,8},{8,16},{16,24},{24,32},{32,40},{40,48},{48,56},{56,6... | collective-permute-start | bytes 196616 | tf_op jit(solution)/shard_map/while/body/eval_jaxpr/ppermute | solution.py:17
  166.8 10.5 %collective-permute-start = (bf16[4,64,128]{2,1,0:T(8,128)(2,1)}, bf16[4,64,128]{2,1,0:T(8,128)(2,1)S(1)}, u32[]{:S(2)}, u32[]{:S(2)}) collective-permute-start(bf16[4,64,128]{2,1,0:T(8,128)(2,1)} %copy.56), channel_id=1, source_target_pairs={{248,0},{0,8},{8,16},{16,24},{24,32},{32,40},{40,48},{48,56},{56,6... | collective-permute-start | bytes 196616 | tf_op jit(solution)/shard_map/while/body/eval_jaxpr/ppermute | solution.py:17
  169.2 8.1 %collective-permute-start.1 = (s32[4]{0:T(128)}, s32[4]{0:T(128)S(1)}, u32[]{:S(2)}, u32[]{:S(2)}) collective-permute-start(s32[4]{0:T(128)} %copy.57), channel_id=1, source_target_pairs={{248,0},{0,8},{8,16},{16,24},{24,32},{32,40},{40,48},{48,56},{56,6... | collective-permute-start | bytes 56 | tf_op jit(solution)/shard_map/while/body/eval_jaxpr/ppermute | solution.py:17
  185.3 8.8 %collective-permute-start = (bf16[4,64,128]{2,1,0:T(8,128)(2,1)}, bf16[4,64,128]{2,1,0:T(8,128)(2,1)S(1)}, u32[]{:S(2)}, u32[]{:S(2)}) collective-permute-start(bf16[4,64,128]{2,1,0:T(8,128)(2,1)} %copy.56), channel_id=1, source_target_pairs={{248,0},{0,8},{8,16},{16,24},{24,32},{32,40},{40,48},{48,56},{56,6... | collective-permute-start | bytes 196616 | tf_op jit(solution)/shard_map/while/body/eval_jaxpr/ppermute | solution.py:17
  203.2 9.4 %collective-permute-start = (bf16[4,64,128]{2,1,0:T(8,128)(2,1)}, bf16[4,64,128]{2,1,0:T(8,128)(2,1)S(1)}, u32[]{:S(2)}, u32[]{:S(2)}) collective-permute-start(bf16[4,64,128]{2,1,0:T(8,128)(2,1)} %copy.56), channel_id=1, source_target_pairs={{248,0},{0,8},{8,16},{16,24},{24,32},{32,40},{40,48},{48,56},{56,6... | collective-permute-start | bytes 196616 | tf_op jit(solution)/shard_map/while/body/eval_jaxpr/ppermute | solution.py:17
  203.8 8.8 %collective-permute-start.1 = (s32[4]{0:T(128)}, s32[4]{0:T(128)S(1)}, u32[]{:S(2)}, u32[]{:S(2)}) collective-permute-start(s32[4]{0:T(128)} %copy.57), channel_id=1, source_target_pairs={{248,0},{0,8},{8,16},{16,24},{24,32},{32,40},{40,48},{48,56},{56,6... | collective-permute-start | bytes 56 | tf_op jit(solution)/shard_map/while/body/eval_jaxpr/ppermute | solution.py:17
  221.7 9.0 %collective-permute-start = (bf16[4,64,128]{2,1,0:T(8,128)(2,1)}, bf16[4,64,128]{2,1,0:T(8,128)(2,1)S(1)}, u32[]{:S(2)}, u32[]{:S(2)}) collective-permute-start(bf16[4,64,128]{2,1,0:T(8,128)(2,1)} %copy.56), channel_id=1, source_target_pairs={{248,0},{0,8},{8,16},{16,24},{24,32},{32,40},{40,48},{48,56},{56,6... | collective-permute-start | bytes 196616 | tf_op jit(solution)/shard_map/while/body/eval_jaxpr/ppermute | solution.py:17
  222.3 8.4 %collective-permute-start.1 = (s32[4]{0:T(128)}, s32[4]{0:T(128)S(1)}, u32[]{:S(2)}, u32[]{:S(2)}) collective-permute-start(s32[4]{0:T(128)} %copy.57), channel_id=1, source_target_pairs={{248,0},{0,8},{8,16},{16,24},{24,32},{32,40},{40,48},{48,56},{56,6... | collective-permute-start | bytes 56 | tf_op jit(solution)/shard_map/while/body/eval_jaxpr/ppermute | solution.py:17
  239.1 8.8 %collective-permute-start = (bf16[4,64,128]{2,1,0:T(8,128)(2,1)}, bf16[4,64,128]{2,1,0:T(8,128)(2,1)S(1)}, u32[]{:S(2)}, u32[]{:S(2)}) collective-permute-start(bf16[4,64,128]{2,1,0:T(8,128)(2,1)} %copy.56), channel_id=1, source_target_pairs={{248,0},{0,8},{8,16},{16,24},{24,32},{32,40},{40,48},{48,56},{56,6... | collective-permute-start | bytes 196616 | tf_op jit(solution)/shard_map/while/body/eval_jaxpr/ppermute | solution.py:17
  256.3 8.9 %collective-permute-start = (bf16[4,64,128]{2,1,0:T(8,128)(2,1)}, bf16[4,64,128]{2,1,0:T(8,128)(2,1)S(1)}, u32[]{:S(2)}, u32[]{:S(2)}) collective-permute-start(bf16[4,64,128]{2,1,0:T(8,128)(2,1)} %copy.56), channel_id=1, source_target_pairs={{248,0},{0,8},{8,16},{16,24},{24,32},{32,40},{40,48},{48,56},{56,6... | collective-permute-start | bytes 196616 | tf_op jit(solution)/shard_map/while/body/eval_jaxpr/ppermute | solution.py:17
  256.9 8.3 %collective-permute-start.1 = (s32[4]{0:T(128)}, s32[4]{0:T(128)S(1)}, u32[]{:S(2)}, u32[]{:S(2)}) collective-permute-start(s32[4]{0:T(128)} %copy.57), channel_id=1, source_target_pairs={{248,0},{0,8},{8,16},{16,24},{24,32},{32,40},{40,48},{48,56},{56,6... | collective-permute-start | bytes 56 | tf_op jit(solution)/shard_map/while/body/eval_jaxpr/ppermute | solution.py:17
  273.3 8.1 %collective-permute-start = (bf16[4,64,128]{2,1,0:T(8,128)(2,1)}, bf16[4,64,128]{2,1,0:T(8,128)(2,1)S(1)}, u32[]{:S(2)}, u32[]{:S(2)}) collective-permute-start(bf16[4,64,128]{2,1,0:T(8,128)(2,1)} %copy.56), channel_id=1, source_target_pairs={{248,0},{0,8},{8,16},{16,24},{24,32},{32,40},{40,48},{48,56},{56,6... | collective-permute-start | bytes 196616 | tf_op jit(solution)/shard_map/while/body/eval_jaxpr/ppermute | solution.py:17
  282.0 9.0 %collective-permute-start = (bf16[4,64,128]{2,1,0:T(8,128)(2,1)}, bf16[4,64,128]{2,1,0:T(8,128)(2,1)S(1)}, u32[]{:S(2)}, u32[]{:S(2)}) collective-permute-start(bf16[4,64,128]{2,1,0:T(8,128)(2,1)} %copy.56), channel_id=1, source_target_pairs={{248,0},{0,8},{8,16},{16,24},{24,32},{32,40},{40,48},{48,56},{56,6... | collective-permute-start | bytes 196616 | tf_op jit(solution)/shard_map/while/body/eval_jaxpr/ppermute | solution.py:17
  291.7 9.0 %collective-permute-start = (bf16[4,64,128]{2,1,0:T(8,128)(2,1)}, bf16[4,64,128]{2,1,0:T(8,128)(2,1)S(1)}, u32[]{:S(2)}, u32[]{:S(2)}) collective-permute-start(bf16[4,64,128]{2,1,0:T(8,128)(2,1)} %copy.56), channel_id=1, source_target_pairs={{248,0},{0,8},{8,16},{16,24},{24,32},{32,40},{40,48},{48,56},{56,6... | collective-permute-start | bytes 196616 | tf_op jit(solution)/shard_map/while/body/eval_jaxpr/ppermute | solution.py:17
  308.6 10.4 %collective-permute-start = (bf16[4,64,128]{2,1,0:T(8,128)(2,1)}, bf16[4,64,128]{2,1,0:T(8,128)(2,1)S(1)}, u32[]{:S(2)}, u32[]{:S(2)}) collective-permute-start(bf16[4,64,128]{2,1,0:T(8,128)(2,1)} %copy.56), channel_id=1, source_target_pairs={{248,0},{0,8},{8,16},{16,24},{24,32},{32,40},{40,48},{48,56},{56,6... | collective-permute-start | bytes 196616 | tf_op jit(solution)/shard_map/while/body/eval_jaxpr/ppermute | solution.py:17
  310.9 8.1 %collective-permute-start.1 = (s32[4]{0:T(128)}, s32[4]{0:T(128)S(1)}, u32[]{:S(2)}, u32[]{:S(2)}) collective-permute-start(s32[4]{0:T(128)} %copy.57), channel_id=1, source_target_pairs={{248,0},{0,8},{8,16},{16,24},{24,32},{32,40},{40,48},{48,56},{56,6... | collective-permute-start | bytes 56 | tf_op jit(solution)/shard_map/while/body/eval_jaxpr/ppermute | solution.py:17
  327.0 8.8 %collective-permute-start = (bf16[4,64,128]{2,1,0:T(8,128)(2,1)}, bf16[4,64,128]{2,1,0:T(8,128)(2,1)S(1)}, u32[]{:S(2)}, u32[]{:S(2)}) collective-permute-start(bf16[4,64,128]{2,1,0:T(8,128)(2,1)} %copy.56), channel_id=1, source_target_pairs={{248,0},{0,8},{8,16},{16,24},{24,32},{32,40},{40,48},{48,56},{56,6... | collective-permute-start | bytes 196616 | tf_op jit(solution)/shard_map/while/body/eval_jaxpr/ppermute | solution.py:17
  351.7 314.3 %all-reduce.8.cloned.1.call-start = ((), (), s32[]{:S(2)}) async-start(), calls=%async_computation.1 | async-start | bytes 524288 | tf_op jit(solution)/shard_map/psum | solution.py:113
  (41 other events, 297.9 us)
Sparse Core Ops, SparseCore 0:
  351.8 167.8 all-reduce.5
  523.9 142.1 all-reduce.7
where the time goes:
time: 682 us; the launch traced here: 676 us
  waiting for transfers between devices  234 us (34%)
  blocking collectives  132 us (19%)
  other arithmetic  85.6 us (13%)
  starting transfers between devices  56.8 us (8%)
  matrix products  54.5 us (8%)
  local copies, waits for them, and re-layouts  50.1 us (7%)
  loops' own time  45.2 us (7%)
  between operations  17.5 us (3%)
    unnamed x3, waiting for transfers between devices  166 us
    psum x1, blocking collectives, shards(): loss = lax.psum(loss_part, ('seq', 'head'))  78.3 us
    psum x1, waiting for transfers between devices, shards(): grad_q, grad_k = lax.psum((grad_q, grad_k), 'seq')  65.7 us
    ppermute x62, starting transfers between devices, passed_along(): return lax.ppermute(block, axis, route)  56.8 us
    dot_general x32, matrix products, work(): lax.dot_general(qmat, kblk, (((1,), (1,)), ((), ())), preferred_element_t...  49.5 us
    reduce_min x32, other arithmetic, one(): jnp.min(posp) * BLOCK > qlast  44.1 us
    another operation x1, loops' own time, shards(): lax.fori_loop(0, seq_count - 1, turn, (init, key_blocks, block_order))  42.7 us
    while x93, local copies, waits for them, and re-layouts  37.6 us
  transfers between devices with their start and end apart: 64, of which 9 were waited for; matrix products, arithmetic and copies ran while one was open for 22% of the time, Pallas kernels for 0%

commit v1 on v0

v1 whole, which is shorter than its diff:
```python
import functools
import math

import jax
import jax.numpy as jnp
from jax import lax
from jax.experimental import pallas as pl
from jax.experimental.pallas import tpu as pltpu
from jax.sharding import Mesh, PartitionSpec as P

BLOCK = 64
WIDTH = 128
GROUP = 8
LOCAL = 4
SEQ = 32
NB = LOCAL * SEQ
ROWS = LOCAL * BLOCK
SENT = ROWS + 16
SPAN = 8
LANES = BLOCK * GROUP
SCALE = WIDTH ** -0.5
EXP2 = SCALE * math.log2(math.e)
MASKED = -1e30 * WIDTH ** 0.5
HIGH = lax.Precision.HIGHEST
NT = (((1,), (1,)), ((), ()))
NN = (((1,), (0,)), ((), ()))
F32 = jnp.float32
BF16 = jnp.bfloat16


def dot(a, b, dims=NN, precision=None):
    return lax.dot_general(a, b, dims, precision=precision, preferred_element_type=F32)


def prepare(keys_ref, pos_ref, out_ref):
    keys = keys_ref[...]
    blocks = keys.astype(F32).reshape(LOCAL, BLOCK, WIDTH)
    kmax = jnp.max(blocks, axis=1)
    kmin = jnp.min(blocks, axis=1)
    kmean = jnp.sum(blocks, axis=1) * (1.0 / BLOCK)
    extra = jnp.concatenate([kmax, kmin, kmean, pos_ref[...]], axis=0).astype(BF16)
    for i in range(out_ref.shape[0]):
        out_ref[i, :ROWS, :] = keys
        out_ref[i, ROWS:, :] = extra


def attend(
    pos_sm, own_sm, place_ref, ownrow_ref, gathered_ref, q_ref, wq_ref, wk_ref,
    out_ref, kpool_ref, ks, bm, tgt,
):
    def put(c, _):
        block = gathered_ref[c // LOCAL, pl.ds(pl.multiple_of((c % LOCAL) * BLOCK, BLOCK), BLOCK), :]
        ks[pl.ds(pl.multiple_of(pos_sm[c] * BLOCK, BLOCK), BLOCK), :] = block
        return 0

    lax.fori_loop(0, NB, put, 0, unroll=8)

    step = SPAN * BLOCK
    sub = lax.broadcasted_iota(jnp.int32, (step, LANES), 0)
    tok = lax.broadcasted_iota(jnp.int32, (step, LANES), 1) // GROUP
    ahead = sub - tok
    lane = lax.broadcasted_iota(jnp.int32, (NB, WIDTH), 1)

    def scores(j, qb):
        rows = ks[pl.ds(pl.multiple_of(j * step, step), step), :]
        return dot(rows, qb, NT)

    def maxima(s):
        return jnp.max(jnp.max(s.reshape(SPAN, BLOCK // 8, 8, LANES), axis=1), axis=1)

    def total(s, m):
        return jnp.sum(jnp.exp2((s - m) * EXP2).reshape(step // 8, 8, LANES), axis=0)

    tgt[...] = jnp.zeros((NB, WIDTH), F32)
    for b in range(LOCAL):
        qb = q_ref[b * LANES : (b + 1) * LANES, :]
        pb = own_sm[b]
        last = pb // SPAN
        bm[...] = jnp.full((NB, LANES), MASKED, F32)

        def masked():
            s = scores(last, qb)
            return jnp.where(ahead > (pb - last * SPAN) * BLOCK, MASKED, s)

        s = masked()
        top = maxima(s)
        bm[pl.ds(pl.multiple_of(last * SPAN, SPAN), SPAN), :] = top
        ref = jnp.max(top, axis=0, keepdims=True)
        acc = total(s, ref)

        def one(j, acc):
            s = scores(j, qb)
            bm[pl.ds(pl.multiple_of(j * SPAN, SPAN), SPAN), :] = maxima(s)
            return acc + total(s, ref)

        acc = lax.fori_loop(0, last, one, acc)
        rmax = jnp.max(bm[...], axis=0, keepdims=True)
        fine = jnp.max((rmax - ref) * EXP2) <= 80.0

        def again():
            def more(j, acc):
                return acc + total(scores(j, qb), rmax)

            return lax.fori_loop(0, last, more, total(masked(), rmax)), rmax

        acc, ref = lax.cond(fine, lambda: (acc, ref), again)
        logsum = jnp.log2(jnp.sum(acc, axis=0, keepdims=True))
        d = (bm[...] - ref) * EXP2 - logsum
        e = d[:, :WIDTH]
        for i in range(1, LANES // WIDTH):
            e = jnp.maximum(e, d[:, i * WIDTH : (i + 1) * WIDTH])
        for shift in (8, 16, 32, 64):
            e = jnp.maximum(e, pltpu.roll(e, shift, 1))
        tgt[...] = jnp.where(lane // GROUP == b, jnp.exp2(e), tgt[...])

    live = lane < LOCAL * GROUP
    pooled = tgt[...]
    psum = jnp.sum(pooled, axis=0, keepdims=True)
    target = jnp.where(live, pooled / jnp.where(psum > 0, psum, 1.0), 0.0)

    extra = gathered_ref[:, ROWS:, :].reshape(SEQ * 16, WIDTH)
    place = lax.broadcasted_iota(jnp.int32, (NB, SEQ * 16), 0)
    kproj = jnp.zeros((NB, WIDTH), F32)
    for i in range(3):
        pick = jnp.where(place == place_ref[i : i + 1, :], 1.0, 0.0).astype(BF16)
        part = dot(pick, extra).astype(BF16)
        kpool_ref[:, i * WIDTH : (i + 1) * WIDTH] = part
        kproj = kproj + dot(part, wk_ref[i * WIDTH : (i + 1) * WIDTH, :])

    q = q_ref[...].astype(F32).reshape(LOCAL, BLOCK, GROUP, WIDTH)
    qpool = (jnp.sum(q, axis=1) * (1.0 / BLOCK)).reshape(LOCAL * GROUP, WIDTH)
    qpool = jnp.concatenate([qpool, jnp.zeros((WIDTH - LOCAL * GROUP, WIDTH), F32)], axis=0)
    qpool = qpool.astype(BF16)
    qproj = dot(qpool, wq_ref[...])

    logits = dot(kproj, qproj, NT, HIGH) * SCALE
    row = lax.broadcasted_iota(jnp.int32, (NB, WIDTH), 0)
    logits = jnp.where(row > ownrow_ref[0:1, :], -1e30, logits)
    shifted = logits - jnp.max(logits, axis=0, keepdims=True)
    ex = jnp.exp(shifted)
    exsum = jnp.sum(ex, axis=0, keepdims=True)
    logp = shifted - jnp.log(exsum)
    scale = 1.0 / (8 * GROUP * NB)
    safe = jnp.log(jnp.where(target > 0, target, 1.0))
    terms = jnp.where(target > 0, target * (safe - logp), 0.0)
    loss = jnp.sum(jnp.sum(terms, axis=0, keepdims=True), axis=1, keepdims=True) * scale
    rowtot = jnp.sum(target, axis=0, keepdims=True)
    dlogit = jnp.where(live, (jnp.exp(logp) * rowtot - target) * (scale * SCALE), 0.0)
    dqproj = dot(dlogit.T, kproj, NN, HIGH)
    dkproj = dot(dlogit, qproj, NN, HIGH)
    gradq = dot(qpool.astype(F32).T, dqproj, NN, HIGH)
    half = SEQ // 2
    out_ref[:half, :8, :] = gradq.reshape(half, 8, WIDTH)
    out_ref[half:, :8, :] = dkproj.reshape(half, 8, WIDTH)
    out_ref[:, 8:, :] = jnp.broadcast_to(loss.reshape(1, 1, 1), (SEQ, 8, WIDTH))


def finish(kpool_ref, dk_ref, out_ref):
    out_ref[...] = dot(kpool_ref[...].astype(F32).T, dk_ref[...], NN, HIGH)


VMEM = pl.BlockSpec(memory_space=pltpu.VMEM)
SMEM = pl.BlockSpec(memory_space=pltpu.SMEM)


def shards(queries, keys, block_order, gate_query, gate_key):
    posrows = jnp.broadcast_to(block_order.astype(F32)[:, None], (LOCAL, WIDTH))
    mine = pl.pallas_call(
        prepare,
        out_shape=jax.ShapeDtypeStruct((8, SENT, WIDTH), BF16),
        in_specs=[VMEM, VMEM],
        out_specs=VMEM,
        name="prepare",
    )(keys.reshape(ROWS, WIDTH), posrows)
    column = lax.all_to_all(mine, "z", 0, 0)
    column = jnp.broadcast_to(column[None], (4, 8, SENT, WIDTH))
    gathered = lax.all_to_all(column, "x", 0, 0).reshape(SEQ, SENT, WIDTH)

    pos = gathered[:, ROWS + 12 :, 0].astype(jnp.int32)
    place = jnp.stack(
        [jnp.pad(pos, ((0, 0), (4 * i, 12 - 4 * i)), constant_values=-1) for i in range(3)]
    ).reshape(3, SEQ * 16)
    ownrow = jnp.pad(jnp.repeat(block_order, GROUP), (0, WIDTH - LOCAL * GROUP))[None]
    sums, kpool = pl.pallas_call(
        attend,
        out_shape=(
            jax.ShapeDtypeStruct((SEQ, 16, WIDTH), F32),
            jax.ShapeDtypeStruct((NB, 3 * WIDTH), BF16),
        ),
        in_specs=[SMEM, SMEM, VMEM, VMEM, VMEM, VMEM, VMEM, VMEM],
        out_specs=(VMEM, VMEM),
        scratch_shapes=[
            pltpu.VMEM((NB * BLOCK, WIDTH), BF16),
            pltpu.VMEM((NB, LANES), F32),
            pltpu.VMEM((NB, WIDTH), F32),
        ],
        compiler_params=pltpu.CompilerParams(vmem_limit_bytes=40 << 20),
        name="attend",
    )(
        pos.reshape(NB), block_order, place, ownrow, gathered,
        queries.reshape(ROWS * GROUP, WIDTH), gate_query[0], gate_key[0],
    )
    got = jnp.sum(lax.all_to_all(sums, ("x", "z"), 0, 0), axis=0)
    loss = lax.psum(got[8, 0], ("y", "core"))
    whole = lax.all_to_all(jnp.broadcast_to(got[None, :8], (SEQ, 8, WIDTH)), ("x", "z"), 0, 0)
    whole = whole.reshape(2, NB, WIDTH)
    grad_k = pl.pallas_call(
        finish,
        out_shape=jax.ShapeDtypeStruct((3 * WIDTH, WIDTH), F32),
        in_specs=[VMEM, VMEM],
        out_specs=VMEM,
        name="finish",
    )(kpool, whole[1])
    return loss, whole[0][None], grad_k[None]


def solution(mesh):
    fine = Mesh(mesh.devices.reshape(4, 8, 4, 2), ("x", "z", "y", "core"))
    seq, head = ("x", "z"), ("y", "core")
    return jax.shard_map(
        shards,
        mesh=fine,
        in_specs=(
            P(seq, head, None),
            P(seq, head, None),
            P(seq),
            P(head, None, None),
            P(head, None, None),
        ),
        out_specs=(P(), P(head, None, None), P(head, None, None)),
        check_vma=False,
    )
```

time: 682 us -> 124 us (0.18)
  waiting for transfers between devices: 234 us -> 24.6 us
  other arithmetic: 85.6 us -> 1.36 us
  blocking collectives: 132 us -> 60.6 us
  matrix products: 54.5 us -> 0 us
  starting transfers between devices: 56.8 us -> 8.62 us
  loops' own time: 45.2 us -> 0 us
  local copies, waits for them, and re-layouts: 50.1 us -> 5.57 us
  Pallas kernels: 0 us -> 22.3 us
  between operations: 17.5 us -> 0.72 us
    unnamed x3 -> x0, waiting for transfers between devices: 166 us -> none
    psum x1 -> x0, waiting for transfers between devices: 65.7 us -> none  [shards(): grad_q, grad_k = lax.psum((grad_q, grad_k), 'seq')]
    psum x1, blocking collectives: 78.3 us -> 18.8 us  [shards(): loss = lax.psum(got[8, 0], ('y', 'core'))]
    ppermute x62 -> x0, starting transfers between devices: 56.8 us -> none  [passed_along(): return lax.ppermute(block, axis, route)]
    dot_general x39 -> x0, matrix products: 54.5 us -> none  [the longest x32 49.5 us: work(): lax.dot_general(qmat, kblk, (((1,), (1,)), ((), ())), preferred_element_t...]
    another operation x33 -> x0, loops' own time: 45.2 us -> none  [the longest x1 42.7 us: shards(): lax.fori_loop(0, seq_count - 1, turn, (init, key_blocks, block_order))]
    reduce_min x32 -> x0, other arithmetic: 44.1 us -> none  [one(): jnp.min(posp) * BLOCK > qlast]
    all_to_all x0 -> x2, blocking collectives: none -> 41.7 us  [the longest x1 25.5 us: shards(): column = lax.all_to_all(mine, 'z', 0, 0)]
  transfers between devices with their start and end apart: 64 -> 2, of which waited for: 9 -> 1; matrix products, arithmetic and copies ran while one was open for 22% -> 1% of each run, Pallas kernels for 0% -> 0%
where the time goes in v1:
time: 124 us
  blocking collectives  60.6 us (49%)
  waiting for transfers between devices  24.6 us (20%)
  Pallas kernels  22.3 us (18%)
  starting transfers between devices  8.62 us (7%)
  local copies, waits for them, and re-layouts  5.57 us (4%)
  other arithmetic  1.36 us (1%)
    all_to_all x1, blocking collectives, shards(): column = lax.all_to_all(mine, 'z', 0, 0)  25.5 us
    all_to_all x1, waiting for transfers between devices, shards(): gathered = lax.all_to_all(column, 'x', 0, 0).reshape(SEQ, SENT, WIDTH)  24.6 us
    psum x1, blocking collectives, shards(): loss = lax.psum(got[8, 0], ('y', 'core'))  18.8 us
    pallas_call x1, Pallas kernels, shards(): pl.pallas_call(attend, out_shape=(jax.ShapeDtypeStruct((SEQ, 16, WIDTH),...  18.6 us
    all_to_all x1, blocking collectives, shards(): got = jnp.sum(lax.all_to_all(sums, ('x', 'z'), 0, 0), axis=0)  16.2 us
    all_to_all x1, starting transfers between devices, shards(): lax.all_to_all(jnp.broadcast_to(got[None, :8], (SEQ, 8, WIDTH)), ('x', 'z...  4.46 us
    all_to_all x1, starting transfers between devices, shards(): gathered = lax.all_to_all(column, 'x', 0, 0).reshape(SEQ, SENT, WIDTH)  4.16 us
  transfers between devices with their start and end apart: 2, of which 1 were waited for; matrix products, arithmetic and copies ran while one was open for 1% of the time, Pallas kernels for 0%

profile of v1, /device:TPU:1, one launch (start us, length us, event | category | flops | bytes accessed | tf_op | source)
XLA Modules:
  0.0 123.7 jit_solution(5607183260015328044)
XLA Ops:
  0.6 0.7 convert_element_type.15
  1.3 0.6 broadcast_in_dim.12.pos_ref
  1.9 1.7 %prepare.1 = bf16[8,272,128]{2,1,0:T(8,128)(2,1)} custom-call(bf16[256,128]{1,0:T(8,128)(2,1)} %bitcast.21, f32[4,128]{1,0:T(4,128)} %broadcast_in_dim.12.pos_ref), custom_call_target="tpu_custom_call" | custom-call | tf_op jit(solution)/shard_map/prepare/pallas_call | solution.py:168
  3.7 25.5 %all_to_all.20 = bf16[8,272,128]{2,1,0:T(8,128)(2,1)S(1)} all-to-all(bf16[8,272,128]{2,1,0:T(8,128)(2,1)} %prepare.1), channel_id=1, replica_groups=mesh['x'=4,'z'=8,'y'=4,'core'=2] {'z'}, dimensions={0} | all-to-all | bytes 1114112 | tf_op jit(solution)/shard_map/all_to_all | solution.py:175
  29.1 1.7 %broadcast_in_dim.13 = bf16[4,8,272,128]{3,2,1,0:T(8,128)(2,1)} broadcast(bf16[8,272,128]{2,1,0:T(8,128)(2,1)S(1)} %all_to_all.20), dimensions={1,2,3} | broadcast | bytes 2785280 | tf_op jit(solution)/shard_map/broadcast_in_dim | solution.py:176
  30.8 4.2 %all-to-all-start.1 = ((bf16[4,8,272,128]{3,2,1,0:T(8,128)(2,1)}), bf16[4,8,272,128]{3,2,1,0:T(8,128)(2,1)S(1)}, u32[]{:S(2)}, u32[]{:S(2)}) async-start(bf16[4,8,272,128]{3,2,1,0:T(8,128)(2,1)} %broadcast_in_dim.13), calls=%async_computation.1 | async-start | bytes 4456448 | tf_op jit(solution)/shard_map/all_to_all | solution.py:177
  35.0 0.1 reshape.40
  35.1 24.6 %all-to-all-done.1 = bf16[4,8,272,128]{3,2,1,0:T(8,128)(2,1)S(1)} async-done(((bf16[4,8,272,128]{3,2,1,0:T(8,128)(2,1)}), bf16[4,8,272,128]{3,2,1,0:T(8,128)(2,1)S(1)}, u32[]{:S(2)}, u32[]{:S(2)}) %all-to-all-start.1) | async-done | bytes 2228256 | tf_op jit(solution)/shard_map/all_to_all | solution.py:177
  59.8 0.6 fusion
  60.4 0.1 copy.12
  60.5 0.1 copy.16
  60.6 0.1 fusion.1
  60.7 0.1 stack.12
  60.9 0.1 stack.14
  60.9 0.1 reshape.42.pos_sm
  61.1 18.6 %attend.1 = (f32[32,16,128]{2,1,0:T(8,128)S(1)}, bf16[128,384]{1,0:T(8,128)(2,1)S(1)}) custom-call(s32[128]{0:T(128)S(1)} %reshape.42.pos_sm, s32[4]{0:T(128)S(1)} %copy-done.4, s32[3,512]{1,0:T(4,128)S(1)} %pad_add_fusion.place_ref, s32[1,128]{1,0:T(1,128)S(1)} %pad_bitcast_fusion.ownrow_ref, bf16[32,272,128]{2,1,0:T(8,128)(2,1)S(1)} %bitcast.16, ...), custom_call_target="tpu_custom_call" | custom-call | tf_op jit(solution)/shard_map/attend/pallas_call | solution.py:184
  79.8 0.6 copy-done.2
  80.4 16.2 %all_to_all.21 = f32[32,16,128]{2,1,0:T(8,128)S(1)} all-to-all(f32[32,16,128]{2,1,0:T(8,128)S(1)} %get-tuple-element.5), channel_id=1, replica_groups=mesh['x'=4,'z'=8,'y'=4,'core'=2] {'x','z'}, dimensions={0} | all-to-all | bytes 524288 | tf_op jit(solution)/shard_map/all_to_all | solution.py:203
  96.7 0.7 broadcast_in_dim.31
  97.3 4.5 %all-to-all-start.3 = ((f32[32,8,128]{2,1,0:T(8,128)}), f32[32,8,128]{2,1,0:T(8,128)S(1)}, u32[]{:S(2)}, u32[]{:S(2)}) async-start(f32[32,8,128]{2,1,0:T(8,128)} %broadcast_in_dim.31), calls=%async_computation.3 | async-start | bytes 262144 | tf_op jit(solution)/shard_map/all_to_all | solution.py:205
  101.8 0.5 slice.26
  102.3 18.8 %psum.7 = f32[]{:T(128)} all-reduce(f32[]{:T(128)} %bitcast.7), channel_id=1, replica_groups=mesh['x'=4,'z'=8,'y'=4,'core'=2] {'y','core'}, use_global_device_ids=true, to_apply=%region_1.2 | all-reduce | flops 1 | bytes 8 | tf_op jit(solution)/shard_map/psum | solution.py:204
  121.2 0.7 slice_bitcast_fusion
  121.8 1.9 %finish.1 = f32[384,128]{1,0:T(8,128)} custom-call(bf16[128,384]{1,0:T(8,128)(2,1)} %copy-done.2, f32[128,128]{1,0:T(8,128)} %get-tuple-element.7.dk_ref), custom_call_target="tpu_custom_call" | custom-call | tf_op jit(solution)/shard_map/finish/pallas_call | solution.py:207
  (17 shorter events, 0.3 us)
Async XLA Ops:
  30.8 4.2 %copy-start.4 = (s32[4]{0:T(128)S(1)}, s32[4]{0:T(128)}, u32[]{:S(2)}) copy-start(s32[4]{0:T(128)} %own_sm.1) | copy-start | bytes 52
  30.8 30.3 %copy-start = (bf16[256,8,128]{2,1,0:T(8,128)(2,1)S(1)}, bf16[256,8,128]{2,1,0:T(8,128)(2,1)}, u32[]{:S(2)}) copy-start(bf16[256,8,128]{2,1,0:T(8,128)(2,1)} %param.5) | copy-start | bytes 1572868
  30.8 30.3 %copy-start.1 = (bf16[1,384,128]{2,1,0:T(8,128)(2,1)S(1)}, bf16[1,384,128]{2,1,0:T(8,128)(2,1)}, u32[]{:S(2)}) copy-start(bf16[1,384,128]{2,1,0:T(8,128)(2,1)} %param.9) | copy-start | bytes 294916
  30.8 30.3 %copy-start.3 = (bf16[1,128,128]{2,1,0:T(8,128)(2,1)S(1)}, bf16[1,128,128]{2,1,0:T(8,128)(2,1)}, u32[]{:S(2)}) copy-start(bf16[1,128,128]{2,1,0:T(8,128)(2,1)} %param.8) | copy-start | bytes 98308
  30.8 29.0 %all-to-all-start.1 = ((bf16[4,8,272,128]{3,2,1,0:T(8,128)(2,1)}), bf16[4,8,272,128]{3,2,1,0:T(8,128)(2,1)S(1)}, u32[]{:S(2)}, u32[]{:S(2)}) async-start(bf16[4,8,272,128]{3,2,1,0:T(8,128)(2,1)} %broadcast_in_dim.13), calls=%async_computation.1 | async-start | bytes 4456448 | tf_op jit(solution)/shard_map/all_to_all | solution.py:177
  79.7 0.6 copy-start.2
  97.3 23.8 %all-to-all-start.3 = ((f32[32,8,128]{2,1,0:T(8,128)}), f32[32,8,128]{2,1,0:T(8,128)S(1)}, u32[]{:S(2)}, u32[]{:S(2)}) async-start(f32[32,8,128]{2,1,0:T(8,128)} %broadcast_in_dim.31), calls=%async_computation.3 | async-start | bytes 262144 | tf_op jit(solution)/shard_map/all_to_all | solution.py:205

commit v2 on v0

v2 whole, which is shorter than its diff:
```python
import functools
import math

import jax
import jax.numpy as jnp
from jax import lax
from jax.experimental import pallas as pl
from jax.experimental.pallas import tpu as pltpu
from jax.sharding import Mesh, PartitionSpec as P

BLOCK = 64
WIDTH = 128
GROUP = 8
LOCAL = 4
NX, NZ = 4, 8
SEQ = NX * NZ
NB = LOCAL * SEQ
ROWS = LOCAL * BLOCK
MORE = ROWS + 16
SENT = MORE + LOCAL * GROUP
LANES = BLOCK * GROUP
PER = LOCAL * NX
QROWS = LOCAL * GROUP
SCALE = WIDTH ** -0.5
EXP2 = SCALE * math.log2(math.e)
MASKED = -1e30 * WIDTH ** 0.5
FAR = 1e30
SHARE = 1.0 / (8 * GROUP * NB)
HIGH = lax.Precision.HIGHEST
NT = (((1,), (1,)), ((), ()))
NN = (((1,), (0,)), ((), ()))
F32 = jnp.float32
BF16 = jnp.bfloat16
VMEM = pl.BlockSpec(memory_space=pltpu.VMEM)
SMEM = pl.BlockSpec(memory_space=pltpu.SMEM)
ANY = pl.BlockSpec(memory_space=pl.ANY)


def dot(a, b, dims=NN, precision=None):
    return lax.dot_general(a, b, dims, precision=precision, preferred_element_type=F32)


def prepare(own_sm, keys_ref, q_ref, out_ref, qpool_ref):
    keys = keys_ref[...]
    blocks = keys.astype(F32)
    kmax = jnp.max(blocks, axis=1)
    kmin = jnp.min(blocks, axis=1)
    kmean = jnp.sum(blocks, axis=1) * (1.0 / BLOCK)
    spot = lax.broadcasted_iota(jnp.int32, (LOCAL, WIDTH), 0)
    pos = jnp.zeros((LOCAL, WIDTH), F32)
    for b in range(LOCAL):
        pos = jnp.where(spot == b, own_sm[b].astype(F32), pos)
    q = q_ref[...].astype(F32).reshape(LOCAL, BLOCK, GROUP, WIDTH)
    qpool = (jnp.sum(q, axis=1) * (1.0 / BLOCK)).reshape(LOCAL * GROUP, WIDTH)
    extra = jnp.concatenate([kmax, kmin, kmean, pos], axis=0).astype(BF16)
    for i in range(NX):
        out_ref[i, :ROWS, :] = keys.reshape(ROWS, WIDTH)
        out_ref[i, ROWS:MORE, :] = extra
        out_ref[i, MORE:, :] = qpool.astype(BF16)
    qpool_ref[...] = qpool.astype(BF16)


def wide(row):
    return jnp.concatenate([row] * (LANES // WIDTH), axis=1)


def fold(rows, qb, pb, ref, acc, keep):
    for r, row in enumerate(rows):
        tops = []
        for i in range(NX):
            s = dot(row[i, :ROWS, :], qb, NT).reshape(LOCAL, BLOCK // 8, 8, LANES)
            pos = row[i, ROWS:MORE, :].astype(F32)
            for j in range(LOCAL):
                at = wide(pos[12 + j : 13 + j, :])
                top = jnp.max(jnp.max(s[j], axis=0), axis=0, keepdims=True)
                tops.append(jnp.where(at < pb, top, jnp.where(at == pb, ref, MASKED)))
                base = ref + jnp.where(at < pb, 0.0, FAR)
                acc = acc + jnp.sum(jnp.exp2((s[j] - base) * EXP2), axis=0)
            if i % 2:
                keep(r * PER + (i - 1) * LOCAL, jnp.concatenate(tops, axis=0))
                tops = []
    return acc


def first(own_sm, keys_ref, q_ref, row, bm_ref, acc_ref, ref_ref):
    sub = lax.broadcasted_iota(jnp.int32, (BLOCK, LANES), 0)
    tok = lax.broadcasted_iota(jnp.int32, (BLOCK, LANES), 1) // GROUP

    def one(b, _):
        qb = q_ref[b]
        s = jnp.where(sub > tok, MASKED, dot(keys_ref[b], qb, NT))
        ref = jnp.max(s, axis=0, keepdims=True)
        acc = jnp.sum(jnp.exp2((s - ref) * EXP2).reshape(BLOCK // 8, 8, LANES), axis=0)
        ref_ref[b] = jnp.broadcast_to(ref, (8, LANES))

        def keep(at, tops):
            bm_ref[b, at : at + 8, :] = tops

        acc_ref[b] = fold([row], qb, own_sm[b].astype(F32), ref, acc, keep)
        return 0

    lax.fori_loop(0, LOCAL, one, 0)


def middle(own_sm, q_ref, ref_ref, acc_in, back, ahead, bm_ref, acc_ref):
    def one(b, _):
        def keep(at, tops):
            bm_ref[b, at : at + 8, :] = tops

        acc_ref[b] = fold(
            [back, ahead], q_ref[b], own_sm[b].astype(F32), ref_ref[b, :1, :], acc_in[b], keep
        )
        return 0

    lax.fori_loop(0, LOCAL, one, 0)


def places(z):
    return [pl.multiple_of(lax.rem(z + off, NZ) * PER, PER) for off in (0, 7, 1, 6, 2, 5, 3, 4)]


def pooled_keys(parts, hs, z, kall):
    for h, at in zip(hs, places(z)):
        tiles = [h[i, ROWS:MORE, :].astype(F32) for i in range(NX)]
        for part in parts:
            got = jnp.concatenate([t[4 * part : 4 * part + 4, :] for t in tiles], axis=0)
            kall[part, pl.ds(at, PER), :] = got


def project(kall, wk_ref):
    kproj = jnp.zeros((NB, WIDTH), F32)
    for part in range(3):
        kproj = kproj + dot(kall[part].astype(BF16), wk_ref[part * WIDTH : (part + 1) * WIDTH, :])
    return kproj


def targets(
    own_sm, z_sm, q_ref, ref_ref, acc_in, last, bm0, bm1, bm2, bm3,
    h0, h1, h2, h3, h4, h5, h6, h7, wq_ref, wk_ref,
    own_ref, out_ref, bm4, acc_s, rmax_s, tgt, kall, held, sem,
):
    rows = (h0, h1, h2, h3, h4, h5, h6, h7)
    z = z_sm[0]

    def one(b, worst):
        def keep(at, tops):
            bm4[b, at : at + 8, :] = tops

        ref = ref_ref[b, :1, :]
        acc_s[b] = fold([last], q_ref[b], own_sm[b].astype(F32), ref, acc_in[b], keep)
        rmax = ref
        for bm in (bm0, bm1, bm2, bm3, bm4):
            rmax = jnp.maximum(rmax, jnp.max(bm[b], axis=0, keepdims=True))
        rmax_s[b] = jnp.broadcast_to(rmax, (8, LANES))
        return jnp.maximum(worst, (rmax - ref) * EXP2)

    worst = lax.fori_loop(0, LOCAL, one, jnp.zeros((1, LANES), F32))
    fine = jnp.max(worst) <= 80.0

    @pl.when(fine)
    def _():
        rmax_s[...] = ref_ref[...]

    @pl.when(jnp.logical_not(fine))
    def _():
        for i, h in enumerate(rows):
            copy = pltpu.make_async_copy(h, held.at[pl.ds(i * NX, NX)], sem)
            copy.start()
            copy.wait()
        acc_s[...] = jnp.zeros((LOCAL, 8, LANES), F32)
        sub = lax.broadcasted_iota(jnp.int32, (BLOCK, LANES), 0).astype(F32)
        tok = (lax.broadcasted_iota(jnp.int32, (BLOCK, LANES), 1) // GROUP).astype(F32)

        def again(i, _):
            pos = held[i, ROWS:MORE, :].astype(F32)
            for j in range(LOCAL):
                at = wide(pos[12 + j : 13 + j, :]) * BLOCK
                keys = held[i, j * BLOCK : (j + 1) * BLOCK, :]
                for b in range(LOCAL):
                    s = dot(keys, q_ref[b], NT)
                    late = at + sub > (own_sm[b] * BLOCK).astype(F32) + tok
                    e = jnp.where(late, 0.0, jnp.exp2((s - rmax_s[b, :1, :]) * EXP2))
                    acc_s[b] = acc_s[b] + jnp.sum(e.reshape(BLOCK // 8, 8, LANES), axis=0)
            return 0

        lax.fori_loop(0, SEQ, again, 0)

    lane = lax.broadcasted_iota(jnp.int32, (PER, WIDTH), 1)
    tgt[...] = jnp.zeros((NB, WIDTH), F32)
    at = places(z)
    parts = [(bm0, 0, at[0]), (bm4, 0, at[7])]
    for k, bm in ((1, bm1), (2, bm2), (3, bm3)):
        parts += [(bm, 0, at[2 * k - 1]), (bm, PER, at[2 * k])]
    for b in range(LOCAL):
        ref = rmax_s[b, :1, :]
        logsum = jnp.log2(jnp.sum(acc_s[b], axis=0, keepdims=True))
        for bm, start, to in parts:
            d = (bm[b, start : start + PER, :] - ref) * EXP2 - logsum
            e = d[:, :WIDTH]
            for i in range(1, LANES // WIDTH):
                e = jnp.maximum(e, d[:, i * WIDTH : (i + 1) * WIDTH])
            for shift in (8, 16, 32, 64):
                e = jnp.maximum(e, pltpu.roll(e, shift, 1))
            tgt[pl.ds(to, PER), :] = jnp.where(lane // GROUP == b, jnp.exp2(e), tgt[pl.ds(to, PER), :])
    pooled = tgt[...].T[: LOCAL * GROUP, :]
    target = pooled / jnp.sum(pooled, axis=1, keepdims=True)

    pooled_keys(range(4), rows, z, kall)
    qproj = dot(own_ref[...], wq_ref[...])
    logits = dot(qproj, project(kall, wk_ref), NT, HIGH) * SCALE
    posr = jnp.concatenate(
        [jnp.full((GROUP, WIDTH), own_sm[b].astype(F32), F32) for b in range(LOCAL)], axis=0
    )
    logits = jnp.where(kall[3].T[:1, :] > posr, -1e30, logits)
    shifted = logits - jnp.max(logits, axis=1, keepdims=True)
    ex = jnp.exp(shifted)
    exsum = jnp.sum(ex, axis=1, keepdims=True)
    logp = shifted - jnp.log(exsum)
    safe = jnp.log(jnp.where(target > 0, target, 1.0))
    terms = jnp.where(target > 0, target * (safe - logp), 0.0)
    loss = jnp.sum(jnp.sum(terms, axis=0, keepdims=True), axis=1, keepdims=True) * SHARE
    rowtot = jnp.sum(target, axis=1, keepdims=True)
    dlogit = (jnp.exp(logp) * rowtot - target) * (SHARE * SCALE)
    mine = jnp.concatenate([dlogit, jnp.broadcast_to(loss, (8, WIDTH))], axis=0)
    for i in range(SEQ):
        out_ref[i] = mine


def finish(
    z_sm, got_ref, h0, h1, h2, h3, h4, h5, h6, h7, wq_ref, wk_ref, gq_ref, gk_ref, qall, kall
):
    rows = (h0, h1, h2, h3, h4, h5, h6, h7)
    z = z_sm[0]
    for h, at in zip(rows, places(z)):
        for i in range(NX):
            to = pl.multiple_of(i * NZ * QROWS + at * (QROWS // PER), QROWS)
            qall[pl.ds(to, QROWS), :] = h[i, MORE:, :]
    pooled_keys(range(3), rows, z, kall)
    kproj = project(kall, wk_ref)
    dlogit = got_ref[:, :QROWS, :].reshape(SEQ * QROWS, WIDTH)
    both = dot(qall[...].astype(F32).T, dlogit, NN, HIGH)
    gq_ref[...] = dot(both, kproj, NN, HIGH)
    dkproj = dot(wq_ref[...].astype(F32).T, both, NN, HIGH)
    for part in range(3):
        out = dot(kall[part].T, dkproj, NT, HIGH)
        gk_ref[part * WIDTH : (part + 1) * WIDTH, :] = out


def call(kernel, out_shape, in_specs, cost, *args, scratch=()):
    return pl.pallas_call(
        kernel,
        out_shape=out_shape,
        in_specs=in_specs,
        out_specs=jax.tree.map(lambda _: VMEM, out_shape),
        scratch_shapes=scratch,
        compiler_params=pltpu.CompilerParams(vmem_limit_bytes=40 << 20),
        cost_estimate=pl.CostEstimate(flops=cost, bytes_accessed=1 << 20, transcendentals=0),
        name=kernel.__name__,
    )(*args)


def whole(shape):
    return pl.BlockSpec(shape, lambda *_: (0,) * len(shape))


def shards(queries, keys, block_order, gate_query, gate_key):
    def f32(*shape):
        return jax.ShapeDtypeStruct(shape, F32)

    own = block_order
    q4 = queries.reshape(LOCAL, LANES, WIDTH)
    k4 = keys.reshape(LOCAL, BLOCK, WIDTH)
    z = lax.axis_index("z").astype(jnp.int32).reshape(1)
    sent = jax.ShapeDtypeStruct((NX, SENT, WIDTH), BF16)
    pooled = jax.ShapeDtypeStruct((QROWS, WIDTH), BF16)
    mine, qpool = pl.pallas_call(
        prepare,
        out_shape=(sent, pooled),
        grid_spec=pltpu.PrefetchScalarGridSpec(
            num_scalar_prefetch=1,
            grid=(1,),
            in_specs=[whole(k4.shape), whole(q4.shape)],
            out_specs=(whole(sent.shape), whole(pooled.shape)),
        ),
        compiler_params=pltpu.CompilerParams(vmem_limit_bytes=40 << 20),
        name="prepare",
    )(own, k4, q4)
    row = lax.all_to_all(mine, "x", 0, 0)

    def shift(a, by):
        return lax.ppermute(a, "z", [(i, (i + by) % NZ) for i in range(NZ)])

    work = 2 * LOCAL * LANES * PER * BLOCK * WIDTH
    state = f32(LOCAL, 8, LANES)
    back, ahead = shift(row, 1), shift(row, -1)
    bm, acc, ref = call(
        first, (f32(LOCAL, PER, LANES), state, state), [SMEM, VMEM, VMEM, VMEM], work,
        own, k4, q4, row,
    )
    bms, rows = [bm], [row]
    for k in range(1, 4):
        rows += [back, ahead]
        back, ahead, acc = lax.optimization_barrier((back, ahead, acc))
        here = (back, ahead)
        back = shift(back, 1)
        ahead = shift(ahead, -1) if k < 3 else None
        bm, acc = call(
            middle, (f32(LOCAL, 2 * PER, LANES), state), [SMEM] + [VMEM] * 5, 2 * work,
            own, q4, ref, acc, *here,
        )
        bms.append(bm)
    rows.append(back)
    spread = call(
        targets, f32(SEQ, QROWS + 8, WIDTH), [SMEM] * 2 + [VMEM] * 19, work,
        own, z, q4, ref, acc, back, *bms, *rows, gate_query[0], gate_key[0], qpool,
        scratch=[
            pltpu.VMEM((LOCAL, PER, LANES), F32),
            pltpu.VMEM((LOCAL, 8, LANES), F32),
            pltpu.VMEM((LOCAL, 8, LANES), F32),
            pltpu.VMEM((NB, WIDTH), F32),
            pltpu.VMEM((4, NB, WIDTH), F32),
            pltpu.VMEM((SEQ, SENT, WIDTH), BF16),
            pltpu.SemaphoreType.DMA,
        ],
    )
    got = lax.all_to_all(spread, ("x", "z"), 0, 0)
    loss = jnp.sum(got[:, QROWS:, :], axis=0)
    loss = lax.all_to_all(jnp.broadcast_to(loss[None], (8, 8, WIDTH)), ("y", "core"), 0, 0)
    grad_q, grad_k = call(
        finish, (f32(WIDTH, WIDTH), f32(3 * WIDTH, WIDTH)), [SMEM] + [VMEM] * 11, work // 4,
        z, got, *rows, gate_query[0], gate_key[0],
        scratch=[pltpu.VMEM((SEQ * QROWS, WIDTH), BF16), pltpu.VMEM((3, NB, WIDTH), F32)],
    )
    return jnp.sum(loss[:, 0, 0]), grad_q[None], grad_k[None]


def solution(mesh):
    fine = Mesh(mesh.devices.reshape(NX, NZ, 4, 2), ("x", "z", "y", "core"))
    seq, head = ("x", "z"), ("y", "core")
    return jax.shard_map(
        shards,
        mesh=fine,
        in_specs=(
            P(seq, head, None),
            P(seq, head, None),
            P(seq),
            P(head, None, None),
            P(head, None, None),
        ),
        out_specs=(P(), P(head, None, None), P(head, None, None)),
        check_vma=False,
    )
```

time: 682 us -> 92.5 us (0.14)
  waiting for transfers between devices: 234 us -> 6.35 us
  blocking collectives: 132 us -> 29.3 us
  other arithmetic: 85.6 us -> 0.64 us
  matrix products: 54.5 us -> 0 us
  loops' own time: 45.2 us -> 0 us
  local copies, waits for them, and re-layouts: 50.1 us -> 6.79 us
  starting transfers between devices: 56.8 us -> 22.5 us
  Pallas kernels: 0 us -> 25.7 us
  between operations: 17.5 us -> 0.78 us
    unnamed x3 -> x0, waiting for transfers between devices: 166 us -> none
    psum x1 -> x0, blocking collectives: 78.3 us -> none  [shards(): loss = lax.psum(loss_part, ('seq', 'head'))]
    psum x1 -> x0, waiting for transfers between devices: 65.7 us -> none  [shards(): grad_q, grad_k = lax.psum((grad_q, grad_k), 'seq')]
    dot_general x39 -> x0, matrix products: 54.5 us -> none  [the longest x32 49.5 us: work(): lax.dot_general(qmat, kblk, (((1,), (1,)), ((), ())), preferred_element_t...]
    ppermute x62 -> x7, starting transfers between devices: 56.8 us -> 11 us  [shift(): return lax.ppermute(a, 'z', [(i, (i + by) % NZ) for i in range(NZ)])]
    another operation x33 -> x0, loops' own time: 45.2 us -> none  [the longest x1 42.7 us: shards(): lax.fori_loop(0, seq_count - 1, turn, (init, key_blocks, block_order))]
    reduce_min x32 -> x0, other arithmetic: 44.1 us -> none  [one(): jnp.min(posp) * BLOCK > qlast]
    while x93 -> x0, local copies, waits for them, and re-layouts: 37.6 us -> none
  transfers between devices with their start and end apart: 64 -> 8, of which waited for: 9 -> 4; matrix products, arithmetic and copies ran while one was open for 22% -> 0% of each run, Pallas kernels for 0% -> 23%
where the time goes in v2:
time: 92.5 us; the launch traced here: 92.1 us
  blocking collectives  29.3 us (32%)
  Pallas kernels  25.7 us (28%)
  starting transfers between devices  22.5 us (24%)
  local copies, waits for them, and re-layouts  6.79 us (7%)
  waiting for transfers between devices  6.35 us (7%)
    pallas_call x6, Pallas kernels, call(): pl.pallas_call(kernel, out_shape=out_shape, in_specs=in_specs, out_specs=...  25 us
    all_to_all x1, blocking collectives, shards(): got = lax.all_to_all(spread, ('x', 'z'), 0, 0)  18.7 us
    all_to_all x1, starting transfers between devices, shards(): lax.all_to_all(jnp.broadcast_to(loss[None], (8, 8, WIDTH)), ('y', 'core')...  11.5 us
    ppermute x7, starting transfers between devices, shift(): return lax.ppermute(a, 'z', [(i, (i + by) % NZ) for i in range(NZ)])  11 us
    all_to_all x1, blocking collectives, shards(): row = lax.all_to_all(mine, 'x', 0, 0)  10.6 us
    unnamed x28, local copies, waits for them, and re-layouts  6.18 us
    ppermute x7, waiting for transfers between devices, shift(): return lax.ppermute(a, 'z', [(i, (i + by) % NZ) for i in range(NZ)])  3.96 us
    all_to_all x1, waiting for transfers between devices, shards(): lax.all_to_all(jnp.broadcast_to(loss[None], (8, 8, WIDTH)), ('y', 'core')...  2.39 us
  transfers between devices with their start and end apart: 8, of which 4 were waited for; matrix products, arithmetic and copies ran while one was open for 0% of the time, Pallas kernels for 23%

profile of v2, /device:TPU:1, one launch (start us, length us, event | category | flops | bytes accessed | tf_op | source)
XLA Modules:
  0.0 92.1 jit_solution(12394723193849172659)
XLA Ops:
  0.6 0.6 copy-done.11
  1.3 1.0 %copy-done = bf16[256,8,128]{2,1,0:T(8,128)(2,1)S(1)} copy-done((bf16[256,8,128]{2,1,0:T(8,128)(2,1)S(1)}, bf16[256,8,128]{2,1,0:T(8,128)(2,1)}, u32[]{:S(2)}) %copy-start) | copy-done | bytes 524312
  2.3 0.8 copy-done.10
  3.2 0.7 prepare.1
  3.8 10.6 %all_to_all.15.row.h0 = bf16[4,304,128]{2,1,0:T(8,128)(2,1)S(1)} all-to-all(bf16[4,304,128]{2,1,0:T(8,128)(2,1)S(1)} %get-tuple-element.25), channel_id=1, replica_groups=mesh['x'=4,'z'=8,'y'=4,'core'=2] {'x'}, dimensions={0} | all-to-all | bytes 622592 | tf_op jit(solution)/shard_map/all_to_all | solution.py:288
  14.5 5.6 %collective-permute-start.1 = (bf16[4,304,128]{2,1,0:T(8,128)(2,1)S(1)}, bf16[4,304,128]{2,1,0:T(8,128)(2,1)S(1)}, u32[]{:S(2)}, u32[]{:S(2)}) collective-permute-start(bf16[4,304,128]{2,1,0:T(8,128)(2,1)S(1)} %all_to_all.15.row.h0), channel_id=1, source_target_pairs={{0,56},{8,0},{16,8},{24,16},{32,24},{40,32},{48,40},{56,48},{1,57}... | collective-permute-start | bytes 933896 | tf_op jit(solution)/shard_map/ppermute | solution.py:291
  20.1 3.1 %first.1 = (f32[4,16,512]{2,1,0:T(8,128)S(1)}, f32[4,8,512]{2,1,0:T(8,128)S(1)}, f32[4,8,512]{2,1,0:T(8,128)S(1)}) custom-call(s32[4]{0:T(128)S(1)} %copy-done.11, bf16[4,64,128]{2,1,0:T(8,128)(2,1)S(1)} %bitcast.18, bf16[4,512,128]{2,1,0:T(8,128)(2,1)S(1)} %bitcast.8, bf16[4,304,128]{2,1,0:T(8,128)(2,1)S(1)} %all_to_all.15.row.h0), custom_call_target="tpu_custom_call" | custom-call | flops 536870912 | bytes 1048576 | tf_op jit(solution)/shard_map/first/pallas_call | solution.py:250
  23.2 0.6 copy-done.6
  23.8 0.7 collective-permute-done.1.ahead.h2
  24.5 3.1 %collective-permute-done.back.h1 = bf16[4,304,128]{2,1,0:T(8,128)(2,1)S(1)} collective-permute-done((bf16[4,304,128]{2,1,0:T(8,128)(2,1)S(1)}, bf16[4,304,128]{2,1,0:T(8,128)(2,1)S(1)}, u32[]{:S(2)}, u32[]{:S(2)}) %collective-permute-start) | collective-permute-done | bytes 311328 | tf_op jit(solution)/shard_map/ppermute | solution.py:291
  27.7 2.7 %collective-permute-start.3 = (bf16[4,304,128]{2,1,0:T(8,128)(2,1)S(1)}, bf16[4,304,128]{2,1,0:T(8,128)(2,1)S(1)}, u32[]{:S(2)}, u32[]{:S(2)}) collective-permute-start(bf16[4,304,128]{2,1,0:T(8,128)(2,1)S(1)} %collective-permute-done.1.ahead.h2), channel_id=1, source_target_pairs={{0,56},{8,0},{16,8},{24,16},{32,24},{40,32},{48,40},{56,48},{1,57}... | collective-permute-start | bytes 933896 | tf_op jit(solution)/shard_map/ppermute | solution.py:291
  30.4 5.2 %middle.3 = (f32[4,32,512]{2,1,0:T(8,128)S(1)}, f32[4,8,512]{2,1,0:T(8,128)S(1)}) custom-call(s32[4]{0:T(128)S(1)} %copy-done.11, bf16[4,512,128]{2,1,0:T(8,128)(2,1)S(1)} %bitcast.9, f32[4,8,512]{2,1,0:T(8,128)S(1)} %get-tuple-element.26.ref_ref, f32[4,8,512]{2,1,0:T(8,128)S(1)} %get-tuple-element.30.acc_in, ...), custom_call_target="tpu_custom_call" | custom-call | flops 1073741824 | bytes 1048576 | tf_op jit(solution)/shard_map/middle/pallas_call | solution.py:250
  35.6 2.7 %collective-permute-start.5 = (bf16[4,304,128]{2,1,0:T(8,128)(2,1)S(1)}, bf16[4,304,128]{2,1,0:T(8,128)(2,1)S(1)}, u32[]{:S(2)}, u32[]{:S(2)}) collective-permute-start(bf16[4,304,128]{2,1,0:T(8,128)(2,1)S(1)} %collective-permute-done.3.ahead.h4), channel_id=1, source_target_pairs={{0,56},{8,0},{16,8},{24,16},{32,24},{40,32},{48,40},{56,48},{1,57}... | collective-permute-start | bytes 933896 | tf_op jit(solution)/shard_map/ppermute | solution.py:291
  38.3 5.2 %middle.4 = (f32[4,32,512]{2,1,0:T(8,128)S(1)}, f32[4,8,512]{2,1,0:T(8,128)S(1)}) custom-call(s32[4]{0:T(128)S(1)} %copy-done.11, bf16[4,512,128]{2,1,0:T(8,128)(2,1)S(1)} %bitcast.10, f32[4,8,512]{2,1,0:T(8,128)S(1)} %get-tuple-element.26.ref_ref, f32[4,8,512]{2,1,0:T(8,128)S(1)} %get-tuple-element.34.acc_in, ...), custom_call_target="tpu_custom_call" | custom-call | flops 1073741824 | bytes 1048576 | tf_op jit(solution)/shard_map/middle/pallas_call | solution.py:250
  43.5 0.7 copy-done.3
  44.2 0.6 copy-done.12
  44.8 0.8 copy-done.9
  45.6 0.8 copy-done.13
  46.5 5.2 %middle.5 = (f32[4,32,512]{2,1,0:T(8,128)S(1)}, f32[4,8,512]{2,1,0:T(8,128)S(1)}) custom-call(s32[4]{0:T(128)S(1)} %copy-done.11, bf16[4,512,128]{2,1,0:T(8,128)(2,1)S(1)} %bitcast.11, f32[4,8,512]{2,1,0:T(8,128)S(1)} %copy-done.9, f32[4,8,512]{2,1,0:T(8,128)S(1)} %copy-done.13, bf16[4,304,128]{2,1,0:T(8,128)(2,1)S(1)} %collective-permute-done.4.back.h5, ...), custom_call_target="tpu_custom_call" | custom-call | flops 1073741824 | bytes 1048576 | tf_op jit(solution)/shard_map/middle/pallas_call | solution.py:250
  51.8 4.1 %targets.1 = f32[32,40,128]{2,1,0:T(8,128)S(1)} custom-call(s32[4]{0:T(128)S(1)} %copy-done.11, s32[1]{0:T(128)} %bitcast.z_sm, bf16[4,512,128]{2,1,0:T(8,128)(2,1)S(1)} %bitcast.12, f32[4,8,512]{2,1,0:T(8,128)S(1)} %copy-done.9, f32[4,8,512]{2,1,0:T(8,128)S(1)} %get-tuple-element.39.acc_in, bf16[4,304,128]{2,1,0:T(8,128)(2,1)S(1)} %collective-permute-done.6.last.h7, ...), custom_call_target="tpu_custom_call" | custom-call | flops 536870912 | bytes 1048576 | tf_op jit(solution)/shard_map/targets/pallas_call | solution.py:250
  55.9 18.7 %all_to_all.16.got_ref = f32[32,40,128]{2,1,0:T(8,128)S(1)} all-to-all(f32[32,40,128]{2,1,0:T(8,128)S(1)} %targets.1), channel_id=1, replica_groups=mesh['x'=4,'z'=8,'y'=4,'core'=2] {'x','z'}, dimensions={0} | all-to-all | bytes 1310720 | tf_op jit(solution)/shard_map/all_to_all | solution.py:326
  75.3 11.5 %all-to-all-start.2 = ((f32[8,8,128]{2,1,0:T(8,128)}), f32[8,8,128]{2,1,0:T(8,128)S(1)}, u32[]{:S(2)}, u32[]{:S(2)}) async-start(f32[8,8,128]{2,1,0:T(8,128)} %broadcast_in_dim.12), calls=%async_computation.2 | async-start | bytes 65536 | tf_op jit(solution)/shard_map/all_to_all | solution.py:328
  86.8 2.3 %finish.1 = (f32[128,128]{1,0:T(8,128)}, f32[384,128]{1,0:T(8,128)}) custom-call(s32[1]{0:T(128)} %bitcast.z_sm, f32[32,40,128]{2,1,0:T(8,128)S(1)} %all_to_all.16.got_ref, bf16[4,304,128]{2,1,0:T(8,128)(2,1)S(1)} %all_to_all.15.row.h0, bf16[4,304,128]{2,1,0:T(8,128)(2,1)S(1)} %collective-permute-done.back.h1, ...), custom_call_target="tpu_custom_call" | custom-call | flops 134217728 | bytes 1048576 | tf_op jit(solution)/shard_map/finish/pallas_call | solution.py:250
  89.1 2.4 %all-to-all-done.2 = f32[8,8,128]{2,1,0:T(8,128)S(1)} async-done(((f32[8,8,128]{2,1,0:T(8,128)}), f32[8,8,128]{2,1,0:T(8,128)S(1)}, u32[]{:S(2)}, u32[]{:S(2)}) %all-to-all-start.2) | async-done | bytes 32800 | tf_op jit(solution)/shard_map/all_to_all | solution.py:328
  (32 shorter events, 1.5 us)
Async XLA Ops:
  0.6 0.7 copy-start.11
  1.3 1.0 %copy-start = (bf16[256,8,128]{2,1,0:T(8,128)(2,1)S(1)}, bf16[256,8,128]{2,1,0:T(8,128)(2,1)}, u32[]{:S(2)}) copy-start(bf16[256,8,128]{2,1,0:T(8,128)(2,1)} %param.5) | copy-start | bytes 1572868
  2.3 0.8 copy-start.10
  14.5 15.9 %copy-start.1 = (bf16[256,8,128]{2,1,0:T(8,128)(2,1)S(1)}, bf16[256,8,128]{2,1,0:T(8,128)(2,1)}, u32[]{:S(2)}) copy-start(bf16[256,8,128]{2,1,0:T(8,128)(2,1)} %param.5) | copy-start | bytes 1572868
  14.5 10.1 %collective-permute-start.1 = (bf16[4,304,128]{2,1,0:T(8,128)(2,1)S(1)}, bf16[4,304,128]{2,1,0:T(8,128)(2,1)S(1)}, u32[]{:S(2)}, u32[]{:S(2)}) collective-permute-start(bf16[4,304,128]{2,1,0:T(8,128)(2,1)S(1)} %all_to_all.15.row.h0), channel_id=1, source_target_pairs={{0,56},{8,0},{16,8},{24,16},{32,24},{40,32},{48,40},{56,48},{1,57}... | collective-permute-start | bytes 933896 | tf_op jit(solution)/shard_map/ppermute | solution.py:291
  20.1 7.6 %collective-permute-start = (bf16[4,304,128]{2,1,0:T(8,128)(2,1)S(1)}, bf16[4,304,128]{2,1,0:T(8,128)(2,1)S(1)}, u32[]{:S(2)}, u32[]{:S(2)}) collective-permute-start(bf16[4,304,128]{2,1,0:T(8,128)(2,1)S(1)} %all_to_all.15.row.h0), channel_id=1, source_target_pairs={{0,8},{8,16},{16,24},{24,32},{32,40},{40,48},{48,56},{56,0},{1,9},... | collective-permute-start | bytes 933896 | tf_op jit(solution)/shard_map/ppermute | solution.py:291
  23.2 0.7 copy-start.6
  23.8 14.5 %copy-start.8 = (f32[4,8,512]{2,1,0:T(8,128)}, f32[4,8,512]{2,1,0:T(8,128)S(1)}, u32[]{:S(2)}) copy-start(f32[4,8,512]{2,1,0:T(8,128)S(1)} %get-tuple-element.26.ref_ref) | copy-start | bytes 196612
  27.7 7.8 %collective-permute-start.2 = (bf16[4,304,128]{2,1,0:T(8,128)(2,1)S(1)}, bf16[4,304,128]{2,1,0:T(8,128)(2,1)S(1)}, u32[]{:S(2)}, u32[]{:S(2)}) collective-permute-start(bf16[4,304,128]{2,1,0:T(8,128)(2,1)S(1)} %collective-permute-done.back.h1), channel_id=1, source_target_pairs={{0,8},{8,16},{16,24},{24,32},{32,40},{40,48},{48,56},{56,0},{1,9},... | collective-permute-start | bytes 933896 | tf_op jit(solution)/shard_map/ppermute | solution.py:291
  27.7 7.8 %collective-permute-start.3 = (bf16[4,304,128]{2,1,0:T(8,128)(2,1)S(1)}, bf16[4,304,128]{2,1,0:T(8,128)(2,1)S(1)}, u32[]{:S(2)}, u32[]{:S(2)}) collective-permute-start(bf16[4,304,128]{2,1,0:T(8,128)(2,1)S(1)} %collective-permute-done.1.ahead.h2), channel_id=1, source_target_pairs={{0,56},{8,0},{16,8},{24,16},{32,24},{40,32},{48,40},{56,48},{1,57}... | collective-permute-start | bytes 933896 | tf_op jit(solution)/shard_map/ppermute | solution.py:291
  35.5 9.2 %collective-permute-start.4 = (bf16[4,304,128]{2,1,0:T(8,128)(2,1)S(1)}, bf16[4,304,128]{2,1,0:T(8,128)(2,1)S(1)}, u32[]{:S(2)}, u32[]{:S(2)}) collective-permute-start(bf16[4,304,128]{2,1,0:T(8,128)(2,1)S(1)} %collective-permute-done.2.back.h3), channel_id=1, source_target_pairs={{0,8},{8,16},{16,24},{24,32},{32,40},{40,48},{48,56},{56,0},{1,9},... | collective-permute-start | bytes 933896 | tf_op jit(solution)/shard_map/ppermute | solution.py:291
  35.6 9.2 %collective-permute-start.5 = (bf16[4,304,128]{2,1,0:T(8,128)(2,1)S(1)}, bf16[4,304,128]{2,1,0:T(8,128)(2,1)S(1)}, u32[]{:S(2)}, u32[]{:S(2)}) collective-permute-start(bf16[4,304,128]{2,1,0:T(8,128)(2,1)S(1)} %collective-permute-done.3.ahead.h4), channel_id=1, source_target_pairs={{0,56},{8,0},{16,8},{24,16},{32,24},{40,32},{48,40},{56,48},{1,57}... | collective-permute-start | bytes 933896 | tf_op jit(solution)/shard_map/ppermute | solution.py:291
  43.5 0.7 copy-start.3
  44.2 0.6 copy-start.12
  44.8 7.0 %collective-permute-start.6 = (bf16[4,304,128]{2,1,0:T(8,128)(2,1)S(1)}, bf16[4,304,128]{2,1,0:T(8,128)(2,1)S(1)}, u32[]{:S(2)}, u32[]{:S(2)}) collective-permute-start(bf16[4,304,128]{2,1,0:T(8,128)(2,1)S(1)} %collective-permute-done.4.back.h5), channel_id=1, source_target_pairs={{0,8},{8,16},{16,24},{24,32},{32,40},{40,48},{48,56},{56,0},{1,9},... | collective-permute-start | bytes 933896 | tf_op jit(solution)/shard_map/ppermute | solution.py:291
  44.8 0.8 copy-start.9
  45.6 0.8 copy-start.13
  46.5 5.3 %copy-start.2 = (bf16[1,384,128]{2,1,0:T(8,128)(2,1)S(1)}, bf16[1,384,128]{2,1,0:T(8,128)(2,1)}, u32[]{:S(2)}) copy-start(bf16[1,384,128]{2,1,0:T(8,128)(2,1)} %param.9) | copy-start | bytes 294916
  46.5 5.3 %copy-start.4 = (f32[4,32,512]{2,1,0:T(8,128)S(1)}, f32[4,32,512]{2,1,0:T(8,128)}, u32[]{:S(2)}) copy-start(f32[4,32,512]{2,1,0:T(8,128)} %copy-done.3) | copy-start | bytes 786436
  46.5 5.3 %copy-start.5 = (bf16[1,128,128]{2,1,0:T(8,128)(2,1)S(1)}, bf16[1,128,128]{2,1,0:T(8,128)(2,1)}, u32[]{:S(2)}) copy-start(bf16[1,128,128]{2,1,0:T(8,128)(2,1)} %param.8) | copy-start | bytes 98308
  46.5 5.3 %copy-start.7 = (f32[4,16,512]{2,1,0:T(8,128)S(1)}, f32[4,16,512]{2,1,0:T(8,128)}, u32[]{:S(2)}) copy-start(f32[4,16,512]{2,1,0:T(8,128)} %copy-done.6) | copy-start | bytes 393220
  75.3 16.2 %all-to-all-start.2 = ((f32[8,8,128]{2,1,0:T(8,128)}), f32[8,8,128]{2,1,0:T(8,128)S(1)}, u32[]{:S(2)}, u32[]{:S(2)}) async-start(f32[8,8,128]{2,1,0:T(8,128)} %broadcast_in_dim.12), calls=%async_computation.2 | async-start | bytes 65536 | tf_op jit(solution)/shard_map/all_to_all | solution.py:328

commit v3 on v2

v3 whole, which is shorter than its diff:
```python
import functools
import math

import jax
import jax.numpy as jnp
from jax import lax
from jax.experimental import pallas as pl
from jax.experimental.pallas import tpu as pltpu
from jax.sharding import Mesh, PartitionSpec as P

BLOCK = 64
WIDTH = 128
GROUP = 8
LOCAL = 4
NX, NZ = 4, 8
SEQ = NX * NZ
NB = LOCAL * SEQ
ROWS = LOCAL * BLOCK
MORE = ROWS + 16
SENT = MORE + LOCAL * GROUP
LANES = BLOCK * GROUP
PER = LOCAL * NX
QROWS = LOCAL * GROUP
SCALE = WIDTH ** -0.5
EXP2 = SCALE * math.log2(math.e)
MASKED = -1e30 * WIDTH ** 0.5
FAR = 1e30
SHARE = 1.0 / (8 * GROUP * NB)
LIFT = 2.0 ** 14
PIECES = 8
HIGH = lax.Precision.HIGHEST
NT = (((1,), (1,)), ((), ()))
NN = (((1,), (0,)), ((), ()))
F32 = jnp.float32
BF16 = jnp.bfloat16
VMEM = pl.BlockSpec(memory_space=pltpu.VMEM)
HBM = pl.BlockSpec(memory_space=pltpu.HBM)


def dot(a, b, dims=NN, precision=None):
    return lax.dot_general(a, b, dims, precision=precision, preferred_element_type=F32)


def prepare(own_hbm, keys_hbm, q_hbm, out_ref, qpool_ref, own_ref, own_sm, keys_ref, q_ref, sems):
    copies = [
        pltpu.make_async_copy(own_hbm, own_sm, sems.at[0]),
        pltpu.make_async_copy(keys_hbm, keys_ref, sems.at[1]),
        pltpu.make_async_copy(q_hbm, q_ref, sems.at[2]),
    ]
    for copy in copies:
        copy.start()
    for copy in copies:
        copy.wait()
    keys = keys_ref[...]
    blocks = keys.astype(F32)
    kmax = jnp.max(blocks, axis=1)
    kmin = jnp.min(blocks, axis=1)
    kmean = jnp.sum(blocks, axis=1) * (1.0 / BLOCK)
    for b in range(LOCAL):
        own_ref[b] = jnp.full((8, WIDTH), own_sm[b].astype(F32), F32)
    pos = jnp.concatenate([own_ref[b, :1, :] for b in range(LOCAL)], axis=0)
    q = q_ref[...].astype(F32).reshape(LOCAL, BLOCK, GROUP, WIDTH)
    qpool = (jnp.sum(q, axis=1) * (1.0 / BLOCK)).reshape(QROWS, WIDTH).astype(BF16)
    extra = jnp.concatenate([kmax, kmin, kmean, pos], axis=0).astype(BF16)
    for i in range(NX):
        out_ref[i, :ROWS, :] = keys.reshape(ROWS, WIDTH)
        out_ref[i, ROWS:MORE, :] = extra
        out_ref[i, MORE:, :] = qpool
    qpool_ref[...] = qpool


def wide(row):
    return jnp.concatenate([row] * (LANES // WIDTH), axis=1)


def maxima(parts):
    row = lax.broadcasted_iota(jnp.int32, parts[0].shape, 0)
    step = 1
    while len(parts) > 1:
        low = (row // step) % 2 == 0
        parts = [
            jnp.maximum(jnp.where(low, a, b), pltpu.roll(jnp.where(low, b, a), 8 - step, 0))
            for a, b in zip(parts[::2], parts[1::2])
        ]
        step *= 2
    return parts[0]


def fold(rows, qb, pb, ref, acc, keep):
    for r, row in enumerate(rows):
        for i0 in range(0, NX, 2):
            tiles = [row[i, ROWS:MORE, :].astype(F32)[12:, :] for i in (i0, i0 + 1)]
            pos = jnp.concatenate(tiles, axis=0)
            early, same = pos < pb, pos == pb
            off = jnp.where(early, 0.0, FAR)
            offs = [jnp.broadcast_to(off[j : j + 1, :], (8, WIDTH)) for j in range(8)]
            kept, sums = [], []
            for at in range(0, LANES, 256):
                n = 256 // WIDTH
                base = ref[:, at : at + 256]
                tops = []
                total = acc[:, at : at + 256]
                for i in (0, 1):
                    s = dot(row[i0 + i, :ROWS, :], qb[at : at + 256, :], NT)
                    s = s.reshape(LOCAL, BLOCK // 8, 8, 256)
                    for j in range(LOCAL):
                        tops.append(jnp.max(s[j], axis=0))
                        shift = base + jnp.concatenate([offs[i * LOCAL + j]] * n, axis=1)
                        total = total + jnp.sum(jnp.exp2((s[j] - shift) * EXP2), axis=0)
                sums.append(total)
                top = maxima(tops)
                own = jnp.where(jnp.concatenate([same] * n, axis=1), base, MASKED)
                kept.append(jnp.where(jnp.concatenate([early] * n, axis=1), top, own))
            acc = jnp.concatenate(sums, axis=1)
            keep(r * PER + i0 * LOCAL, jnp.concatenate(kept, axis=1))
    return acc


def first(own_ref, keys_ref, q_ref, row, bm_ref, acc_ref, ref_ref):
    sub = lax.broadcasted_iota(jnp.int32, (BLOCK, LANES), 0)
    tok = lax.broadcasted_iota(jnp.int32, (BLOCK, LANES), 1) // GROUP

    def one(b, _):
        qb = q_ref[b]
        s = jnp.where(sub > tok, MASKED, dot(keys_ref[b], qb, NT))
        ref = jnp.broadcast_to(jnp.max(s, axis=0, keepdims=True), (8, LANES))
        acc = jnp.sum(jnp.exp2((s.reshape(BLOCK // 8, 8, LANES) - ref) * EXP2), axis=0)
        ref_ref[b] = ref

        def keep(at, tops):
            bm_ref[b, at : at + 8, :] = tops

        acc_ref[b] = fold([row], qb, own_ref[b], ref, acc, keep)
        return 0

    lax.fori_loop(0, LOCAL, one, 0, unroll=4)


def middle(own_ref, q_ref, ref_ref, acc_in, back, ahead, bm_ref, acc_ref):
    def one(b, _):
        def keep(at, tops):
            bm_ref[b, at : at + 8, :] = tops

        acc_ref[b] = fold(
            [back, ahead], q_ref[b], own_ref[b], ref_ref[b], acc_in[b], keep
        )
        return 0

    lax.fori_loop(0, LOCAL, one, 0, unroll=4)


def places(z):
    return [pl.multiple_of(lax.rem(z + off, NZ) * PER, PER) for off in (0, 7, 1, 6, 2, 5, 3, 4)]


def pooled_keys(parts, hs, z, kall):
    for h, at in zip(hs, places(z)):
        tiles = [h[i, ROWS:MORE, :].astype(F32) for i in range(NX)]
        for part in parts:
            got = jnp.concatenate([t[4 * part : 4 * part + 4, :] for t in tiles], axis=0)
            kall[part, pl.ds(at, PER), :] = got


def project(kall, wk_ref):
    kproj = jnp.zeros((NB, WIDTH), F32)
    for part in range(3):
        kproj = kproj + dot(kall[part].astype(BF16), wk_ref[part * WIDTH : (part + 1) * WIDTH, :])
    return kproj


def places_in(shape):
    row = lax.broadcasted_iota(jnp.int32, shape, len(shape) - 2)
    return row, lax.broadcasted_iota(jnp.int32, shape, len(shape) - 1)


def piece_scale(r):
    return 2.0 ** (12 * r - 64)


def targets(
    own_ref, q_ref, ref_ref, acc_in, last, bm0, bm1, bm2, bm3,
    h0, h1, h2, h3, h4, h5, h6, h7, wq_ref, wk_ref,
    qpool_ref, out_ref, bm4, acc_s, rmax_s, tgt, kall, held, sem,
):
    rows = (h0, h1, h2, h3, h4, h5, h6, h7)
    z = lax.axis_index("z")

    def one(b, worst):
        def keep(at, tops):
            bm4[b, at : at + 8, :] = tops

        ref = ref_ref[b]
        acc_s[b] = fold([last], q_ref[b], own_ref[b], ref, acc_in[b], keep)
        rmax = ref
        for bm in (bm0, bm1, bm2, bm3, bm4):
            rmax = jnp.maximum(rmax, jnp.max(bm[b], axis=0, keepdims=True))
        rmax_s[b] = rmax
        return jnp.maximum(worst, (rmax - ref) * EXP2)

    worst = lax.fori_loop(0, LOCAL, one, jnp.zeros((8, LANES), F32))
    fine = jnp.max(worst) <= 80.0

    @pl.when(fine)
    def _():
        rmax_s[...] = ref_ref[...]

    @pl.when(jnp.logical_not(fine))
    def _():
        for i, h in enumerate(rows):
            copy = pltpu.make_async_copy(h, held.at[pl.ds(i * NX, NX)], sem)
            copy.start()
            copy.wait()
        acc_s[...] = jnp.zeros((LOCAL, 8, LANES), F32)
        sub = lax.broadcasted_iota(jnp.int32, (BLOCK, LANES), 0).astype(F32)
        tok = (lax.broadcasted_iota(jnp.int32, (BLOCK, LANES), 1) // GROUP).astype(F32)

        def again(i, _):
            pos = held[i, ROWS:MORE, :].astype(F32)
            for j in range(LOCAL):
                at = wide(pos[12 + j : 13 + j, :]) * BLOCK
                keys = held[i, j * BLOCK : (j + 1) * BLOCK, :]
                for b in range(LOCAL):
                    s = dot(keys, q_ref[b], NT)
                    late = at + sub > wide(own_ref[b, :1, :]) * BLOCK + tok
                    e = jnp.where(late, 0.0, jnp.exp2((s - rmax_s[b, :1, :]) * EXP2))
                    acc_s[b] = acc_s[b] + jnp.sum(e.reshape(BLOCK // 8, 8, LANES), axis=0)
            return 0

        lax.fori_loop(0, SEQ, again, 0)

    lane = lax.broadcasted_iota(jnp.int32, (PER, WIDTH), 1)
    tgt[...] = jnp.zeros((NB, WIDTH), F32)
    at = places(z)
    parts = [(bm0, 0, at[0]), (bm4, 0, at[7])]
    for k, bm in ((1, bm1), (2, bm2), (3, bm3)):
        parts += [(bm, 0, at[2 * k - 1]), (bm, PER, at[2 * k])]
    for b in range(LOCAL):
        ref = rmax_s[b, :1, :]
        logsum = jnp.log2(jnp.sum(acc_s[b], axis=0, keepdims=True))
        for bm, start, to in parts:
            d = (bm[b, start : start + PER, :] - ref) * EXP2 - logsum
            e = d[:, :WIDTH]
            for i in range(1, LANES // WIDTH):
                e = jnp.maximum(e, d[:, i * WIDTH : (i + 1) * WIDTH])
            for shift in (8, 16, 32, 64):
                e = jnp.maximum(e, pltpu.roll(e, shift, 1))
            tgt[pl.ds(to, PER), :] = jnp.where(lane // GROUP == b, jnp.exp2(e), tgt[pl.ds(to, PER), :])
    pooled = tgt[...].T[: LOCAL * GROUP, :]
    target = pooled / jnp.sum(pooled, axis=1, keepdims=True)

    pooled_keys(range(4), rows, z, kall)
    qproj = dot(qpool_ref[...], wq_ref[...])
    logits = dot(qproj, project(kall, wk_ref), NT, HIGH) * SCALE
    posr = own_ref[...].reshape(QROWS, WIDTH)
    logits = jnp.where(kall[3].T[:1, :] > posr, -1e30, logits)
    shifted = logits - jnp.max(logits, axis=1, keepdims=True)
    ex = jnp.exp(shifted)
    exsum = jnp.sum(ex, axis=1, keepdims=True)
    logp = shifted - jnp.log(exsum)
    safe = jnp.log(jnp.where(target > 0, target, 1.0))
    terms = jnp.where(target > 0, target * (safe - logp), 0.0)
    loss = jnp.sum(jnp.sum(terms, axis=0, keepdims=True), axis=1, keepdims=True) * SHARE
    rowtot = jnp.sum(target, axis=1, keepdims=True)
    dlogit = jnp.exp(logp) * rowtot - target
    dlogit = dlogit * LIFT
    row, col = places_in(dlogit.shape)
    for r in range(PIECES):
        scaled = loss * piece_scale(r)
        piece = jnp.where(jnp.abs(scaled) >= 2.0 ** -14, scaled.astype(BF16).astype(F32), 0.0)
        loss = loss - piece * (1.0 / piece_scale(r))
        dlogit = jnp.where((row == r) & (col == 0), piece, dlogit)
    out_ref[...] = dlogit


def head_loss(got_ref, out_ref):
    got = jnp.sum(got_ref[:, :PIECES, :], axis=0)
    row, col = places_in(got.shape)
    total = jnp.zeros(got.shape, F32)
    for r in range(PIECES):
        total = jnp.where((row == r) & (col == 0), got * (1.0 / piece_scale(r)), total)
    total = jnp.sum(jnp.sum(total, axis=0, keepdims=True), axis=1, keepdims=True)
    out_ref[...] = jnp.broadcast_to(total.reshape(1, 1, 1), out_ref.shape)


def finish(
    got_ref, h0, h1, h2, h3, h4, h5, h6, h7, wq_ref, wk_ref, gq_ref, gk_ref, qall, kall
):
    rows = (h0, h1, h2, h3, h4, h5, h6, h7)
    z = lax.axis_index("z")
    for h, at in zip(rows, places(z)):
        for i in range(NX):
            to = pl.multiple_of(i * NZ * QROWS + at * (QROWS // PER), QROWS)
            qall[pl.ds(to, QROWS), :] = h[i, MORE:, :]
    pooled_keys(range(3), rows, z, kall)
    kproj = project(kall, wk_ref)
    row, col = places_in(got_ref.shape)
    held = (row < PIECES) & (col == 0)
    dlogit = jnp.where(held, 0.0, got_ref[...])
    rest = jnp.sum(dlogit, axis=2, keepdims=True)
    dlogit = jnp.where(held, -rest, dlogit)
    rest = jnp.sum(dlogit, axis=2, keepdims=True)
    size = jnp.sum(jnp.abs(dlogit), axis=2, keepdims=True)
    dlogit = dlogit - jnp.abs(dlogit) * (rest / jnp.where(size > 0, size, 1.0))
    dlogit = dlogit.reshape(SEQ * QROWS, WIDTH) * (SHARE * SCALE / LIFT)
    both = dot(qall[...].astype(F32).T, dlogit, NN, HIGH)
    gq_ref[...] = dot(both, kproj, NN, HIGH)
    dkproj = dot(wq_ref[...].astype(F32).T, both, NN, HIGH)
    for part in range(3):
        out = dot(kall[part].T, dkproj, NT, HIGH)
        gk_ref[part * WIDTH : (part + 1) * WIDTH, :] = out


def call(kernel, out_shape, in_specs, cost, *args, scratch=()):
    return pl.pallas_call(
        kernel,
        out_shape=out_shape,
        in_specs=in_specs,
        out_specs=jax.tree.map(lambda _: VMEM, out_shape),
        scratch_shapes=scratch,
        compiler_params=pltpu.CompilerParams(vmem_limit_bytes=40 << 20),
        cost_estimate=pl.CostEstimate(flops=cost, bytes_accessed=1 << 20, transcendentals=0),
        name=kernel.__name__,
    )(*args)


def shards(queries, keys, block_order, gate_query, gate_key):
    def f32(*shape):
        return jax.ShapeDtypeStruct(shape, F32)

    q4 = queries.reshape(LOCAL, LANES, WIDTH)
    k4 = keys.reshape(LOCAL, BLOCK, WIDTH)
    mine, qpool, own = pl.pallas_call(
        prepare,
        out_shape=(
            jax.ShapeDtypeStruct((NX, SENT, WIDTH), BF16),
            jax.ShapeDtypeStruct((QROWS, WIDTH), BF16),
            f32(LOCAL, 8, WIDTH),
        ),
        in_specs=[HBM] * 3,
        out_specs=(VMEM, VMEM, VMEM),
        scratch_shapes=[
            pltpu.SMEM((LOCAL,), jnp.int32),
            pltpu.VMEM(k4.shape, BF16),
            pltpu.VMEM(q4.shape, BF16),
            pltpu.SemaphoreType.DMA((3,)),
        ],
        name="prepare",
    )(block_order, k4, q4)
    row = lax.all_to_all(mine, "x", 0, 0)

    def shift(a, by):
        return lax.ppermute(a, "z", [(i, (i + by) % NZ) for i in range(NZ)])

    work = 2 * LOCAL * LANES * PER * BLOCK * WIDTH
    state = f32(LOCAL, 8, LANES)
    back, ahead = shift(row, 1), shift(row, -1)
    bm, acc, ref = call(
        first, (f32(LOCAL, PER, LANES), state, state), [VMEM] * 4, work,
        own, k4, q4, row,
    )
    bms, rows = [bm], [row]
    for k in range(1, 4):
        rows += [back, ahead]
        back, ahead, acc = lax.optimization_barrier((back, ahead, acc))
        here = (back, ahead)
        back = shift(back, 1)
        ahead = shift(ahead, -1) if k < 3 else None
        bm, acc = call(
            middle, (f32(LOCAL, 2 * PER, LANES), state), [VMEM] * 6, 2 * work,
            own, q4, ref, acc, *here,
        )
        bms.append(bm)
    rows.append(back)
    dlogit = call(
        targets, f32(QROWS, WIDTH), [VMEM] * 20, work,
        own, q4, ref, acc, back, *bms, *rows, gate_query[0], gate_key[0], qpool,
        scratch=[
            pltpu.VMEM((LOCAL, PER, LANES), F32),
            pltpu.VMEM((LOCAL, 8, LANES), F32),
            pltpu.VMEM((LOCAL, 8, LANES), F32),
            pltpu.VMEM((NB, WIDTH), F32),
            pltpu.VMEM((4, NB, WIDTH), F32),
            pltpu.VMEM((SEQ, SENT, WIDTH), BF16),
            pltpu.SemaphoreType.DMA,
        ],
    )
    spread = jnp.broadcast_to(dlogit.astype(jnp.float16)[None], (SEQ, QROWS, WIDTH))
    got = lax.all_to_all(spread, ("x", "z"), 0, 0).astype(F32)
    loss = call(head_loss, f32(8, 8, WIDTH), [VMEM], 1 << 16, got)
    loss = lax.all_to_all(loss, ("y", "core"), 0, 0)
    grad_q, grad_k = call(
        finish, (f32(WIDTH, WIDTH), f32(3 * WIDTH, WIDTH)), [VMEM] * 11, work // 4,
        got, *rows, gate_query[0], gate_key[0],
        scratch=[pltpu.VMEM((SEQ * QROWS, WIDTH), BF16), pltpu.VMEM((3, NB, WIDTH), F32)],
    )
    return jnp.sum(loss[:, 0, 0]), grad_q[None], grad_k[None]


def solution(mesh):
    fine = Mesh(mesh.devices.reshape(NX, NZ, 4, 2), ("x", "z", "y", "core"))
    seq, head = ("x", "z"), ("y", "core")
    return jax.shard_map(
        shards,
        mesh=fine,
        in_specs=(
            P(seq, head, None),
            P(seq, head, None),
            P(seq),
            P(head, None, None),
            P(head, None, None),
        ),
        out_specs=(P(), P(head, None, None), P(head, None, None)),
        check_vma=False,
    )
```

time: 92.5 us -> 84.8 us (0.917)
  waiting for transfers between devices: 6.35 us -> 14.3 us
  local copies, waits for them, and re-layouts: 6.79 us -> 0.07 us
  blocking collectives: 29.3 us -> 24.2 us
  Pallas kernels: 25.7 us -> 21.4 us
    ppermute x7, waiting for transfers between devices: 3.96 us -> 12.1 us  [shift(): return lax.ppermute(a, 'z', [(i, (i + by) % NZ) for i in range(NZ)])]
    unnamed x28 -> x12, local copies, waits for them, and re-layouts: 6.18 us -> 0.03 us
    pallas_call x6 -> x7, Pallas kernels: 25 us -> 19.4 us  [call(): pl.pallas_call(kernel, out_shape=out_shape, in_specs=in_specs, out_specs=...]
    all_to_all x1, blocking collectives: 18.7 us -> 13.5 us  [shards(): got = lax.all_to_all(spread, ('x', 'z'), 0, 0).astype(F32)]
    pallas_call x1, Pallas kernels: 0.67 us -> 2.04 us  [shards(): pl.pallas_call(prepare, out_shape=(jax.ShapeDtypeStruct((NX, SENT, WIDTH)...]
  transfers between devices with their start and end apart: 8 -> 8, of which waited for: 4 -> 6; matrix products, arithmetic and copies ran while one was open for 0% -> 0% of each run, Pallas kernels for 23% -> 18%
where the time goes in v3:
time: 84.8 us; the launch traced here: 84.5 us
  blocking collectives  24.2 us (29%)
  starting transfers between devices  23 us (27%)
  Pallas kernels  21.4 us (25%)
  waiting for transfers between devices  14.3 us (17%)
    pallas_call x7, Pallas kernels, call(): pl.pallas_call(kernel, out_shape=out_shape, in_specs=in_specs, out_specs=...  19.4 us
    all_to_all x1, blocking collectives, shards(): got = lax.all_to_all(spread, ('x', 'z'), 0, 0).astype(F32)  13.5 us
    ppermute x7, waiting for transfers between devices, shift(): return lax.ppermute(a, 'z', [(i, (i + by) % NZ) for i in range(NZ)])  12.1 us
    all_to_all x1, starting transfers between devices, shards(): loss = lax.all_to_all(loss, ('y', 'core'), 0, 0)  11.8 us
    ppermute x7, starting transfers between devices, shift(): return lax.ppermute(a, 'z', [(i, (i + by) % NZ) for i in range(NZ)])  11.1 us
    all_to_all x1, blocking collectives, shards(): row = lax.all_to_all(mine, 'x', 0, 0)  10.8 us
    all_to_all x1, waiting for transfers between devices, shards(): loss = lax.all_to_all(loss, ('y', 'core'), 0, 0)  2.26 us
    pallas_call x1, Pallas kernels, shards(): pl.pallas_call(prepare, out_shape=(jax.ShapeDtypeStruct((NX, SENT, WIDTH)...  2.04 us
  transfers between devices with their start and end apart: 8, of which 6 were waited for; matrix products, arithmetic and copies ran while one was open for 0% of the time, Pallas kernels for 18%

profile of v3, /device:TPU:1, one launch (start us, length us, event | category | flops | bytes accessed | tf_op | source)
XLA Modules:
  0.0 84.5 jit_solution(17633924803827786212)
XLA Ops:
  0.6 2.0 %prepare.1 = (bf16[4,304,128]{2,1,0:T(8,128)(2,1)}, bf16[32,128]{1,0:T(8,128)(2,1)}, f32[4,8,128]{2,1,0:T(8,128)}) custom-call(s32[4]{0:T(128)} %own_hbm.1, bf16[4,64,128]{2,1,0:T(8,128)(2,1)} %bitcast.16, bf16[4,512,128]{2,1,0:T(8,128)(2,1)} %bitcast.6), custom_call_target="tpu_custom_call" | custom-call | tf_op jit(solution)/shard_map/prepare/pallas_call | solution.py:332
  2.7 0.0 copy-start.3
  2.7 0.0 copy-start.4
  2.7 10.8 %all_to_all.15.row.h0 = bf16[4,304,128]{2,1,0:T(8,128)(2,1)S(1)} all-to-all(bf16[4,304,128]{2,1,0:T(8,128)(2,1)} %get-tuple-element.27), channel_id=1, replica_groups=mesh['x'=4,'z'=8,'y'=4,'core'=2] {'x'}, dimensions={0} | all-to-all | bytes 622592 | tf_op jit(solution)/shard_map/all_to_all | solution.py:349
  13.5 5.8 %collective-permute-start.1 = (bf16[4,304,128]{2,1,0:T(8,128)(2,1)S(1)}, bf16[4,304,128]{2,1,0:T(8,128)(2,1)S(1)}, u32[]{:S(2)}, u32[]{:S(2)}) collective-permute-start(bf16[4,304,128]{2,1,0:T(8,128)(2,1)S(1)} %all_to_all.15.row.h0), channel_id=1, source_target_pairs={{0,56},{8,0},{16,8},{24,16},{32,24},{40,32},{48,40},{56,48},{1,57}... | collective-permute-start | bytes 933896 | tf_op jit(solution)/shard_map/ppermute | solution.py:352
  19.3 2.0 %first.1 = (f32[4,16,512]{2,1,0:T(8,128)S(1)}, f32[4,8,512]{2,1,0:T(8,128)S(1)}, f32[4,8,512]{2,1,0:T(8,128)S(1)}) custom-call(f32[4,8,128]{2,1,0:T(8,128)S(1)} %copy-done.4, bf16[4,64,128]{2,1,0:T(8,128)(2,1)S(1)} %bitcast.17, bf16[4,512,128]{2,1,0:T(8,128)(2,1)S(1)} %bitcast.7, bf16[4,304,128]{2,1,0:T(8,128)(2,1)S(1)} %all_to_all.15.row.h0), custom_call_target="tpu_custom_call" | custom-call | flops 536870912 | bytes 1048576 | tf_op jit(solution)/shard_map/first/pallas_call | solution.py:314
  21.3 2.4 %collective-permute-done.1.ahead.h2 = bf16[4,304,128]{2,1,0:T(8,128)(2,1)S(1)} collective-permute-done((bf16[4,304,128]{2,1,0:T(8,128)(2,1)S(1)}, bf16[4,304,128]{2,1,0:T(8,128)(2,1)S(1)}, u32[]{:S(2)}, u32[]{:S(2)}) %collective-permute-start.1) | collective-permute-done | bytes 311328 | tf_op jit(solution)/shard_map/ppermute | solution.py:352
  23.8 3.1 %collective-permute-done.back.h1 = bf16[4,304,128]{2,1,0:T(8,128)(2,1)S(1)} collective-permute-done((bf16[4,304,128]{2,1,0:T(8,128)(2,1)S(1)}, bf16[4,304,128]{2,1,0:T(8,128)(2,1)S(1)}, u32[]{:S(2)}, u32[]{:S(2)}) %collective-permute-start) | collective-permute-done | bytes 311328 | tf_op jit(solution)/shard_map/ppermute | solution.py:352
  26.9 2.7 %collective-permute-start.3 = (bf16[4,304,128]{2,1,0:T(8,128)(2,1)S(1)}, bf16[4,304,128]{2,1,0:T(8,128)(2,1)S(1)}, u32[]{:S(2)}, u32[]{:S(2)}) collective-permute-start(bf16[4,304,128]{2,1,0:T(8,128)(2,1)S(1)} %collective-permute-done.1.ahead.h2), channel_id=1, source_target_pairs={{0,56},{8,0},{16,8},{24,16},{32,24},{40,32},{48,40},{56,48},{1,57}... | collective-permute-start | bytes 933896 | tf_op jit(solution)/shard_map/ppermute | solution.py:352
  29.6 3.6 %middle.3 = (f32[4,32,512]{2,1,0:T(8,128)S(1)}, f32[4,8,512]{2,1,0:T(8,128)S(1)}) custom-call(f32[4,8,128]{2,1,0:T(8,128)S(1)} %copy-done.4, bf16[4,512,128]{2,1,0:T(8,128)(2,1)S(1)} %bitcast.8, f32[4,8,512]{2,1,0:T(8,128)S(1)} %get-tuple-element.28.ref_ref, f32[4,8,512]{2,1,0:T(8,128)S(1)} %get-tuple-element.32.acc_in, ...), custom_call_target="tpu_custom_call" | custom-call | flops 1073741824 | bytes 1048576 | tf_op jit(solution)/shard_map/middle/pallas_call | solution.py:314
  33.1 0.7 collective-permute-done.2.back.h3
  33.9 2.7 %collective-permute-start.5 = (bf16[4,304,128]{2,1,0:T(8,128)(2,1)S(1)}, bf16[4,304,128]{2,1,0:T(8,128)(2,1)S(1)}, u32[]{:S(2)}, u32[]{:S(2)}) collective-permute-start(bf16[4,304,128]{2,1,0:T(8,128)(2,1)S(1)} %collective-permute-done.3.ahead.h4), channel_id=1, source_target_pairs={{0,56},{8,0},{16,8},{24,16},{32,24},{40,32},{48,40},{56,48},{1,57}... | collective-permute-start | bytes 933896 | tf_op jit(solution)/shard_map/ppermute | solution.py:352
  36.5 3.6 %middle.4 = (f32[4,32,512]{2,1,0:T(8,128)S(1)}, f32[4,8,512]{2,1,0:T(8,128)S(1)}) custom-call(f32[4,8,128]{2,1,0:T(8,128)S(1)} %copy-done.4, bf16[4,512,128]{2,1,0:T(8,128)(2,1)S(1)} %bitcast.9, f32[4,8,512]{2,1,0:T(8,128)S(1)} %get-tuple-element.28.ref_ref, f32[4,8,512]{2,1,0:T(8,128)S(1)} %get-tuple-element.36.acc_in, ...), custom_call_target="tpu_custom_call" | custom-call | flops 1073741824 | bytes 1048576 | tf_op jit(solution)/shard_map/middle/pallas_call | solution.py:314
  40.1 0.9 %collective-permute-done.4.back.h5 = bf16[4,304,128]{2,1,0:T(8,128)(2,1)S(1)} collective-permute-done((bf16[4,304,128]{2,1,0:T(8,128)(2,1)S(1)}, bf16[4,304,128]{2,1,0:T(8,128)(2,1)S(1)}, u32[]{:S(2)}, u32[]{:S(2)}) %collective-permute-start.4) | collective-permute-done | bytes 311328 | tf_op jit(solution)/shard_map/ppermute | solution.py:352
  41.0 3.6 %middle.5 = (f32[4,32,512]{2,1,0:T(8,128)S(1)}, f32[4,8,512]{2,1,0:T(8,128)S(1)}) custom-call(f32[4,8,128]{2,1,0:T(8,128)S(1)} %copy-done.4, bf16[4,512,128]{2,1,0:T(8,128)(2,1)S(1)} %bitcast.10, f32[4,8,512]{2,1,0:T(8,128)S(1)} %get-tuple-element.28.ref_ref, f32[4,8,512]{2,1,0:T(8,128)S(1)} %get-tuple-element.38.acc_in, ...), custom_call_target="tpu_custom_call" | custom-call | flops 1073741824 | bytes 1048576 | tf_op jit(solution)/shard_map/middle/pallas_call | solution.py:314
  44.6 4.9 %collective-permute-done.6.last.h7 = bf16[4,304,128]{2,1,0:T(8,128)(2,1)S(1)} collective-permute-done((bf16[4,304,128]{2,1,0:T(8,128)(2,1)S(1)}, bf16[4,304,128]{2,1,0:T(8,128)(2,1)S(1)}, u32[]{:S(2)}, u32[]{:S(2)}) %collective-permute-start.6) | collective-permute-done | bytes 311328 | tf_op jit(solution)/shard_map/ppermute | solution.py:352
  49.5 3.4 %targets.1 = f32[32,128]{1,0:T(8,128)S(1)} custom-call(f32[4,8,128]{2,1,0:T(8,128)S(1)} %copy-done.4, bf16[4,512,128]{2,1,0:T(8,128)(2,1)S(1)} %bitcast.11, f32[4,8,512]{2,1,0:T(8,128)S(1)} %get-tuple-element.28.ref_ref, f32[4,8,512]{2,1,0:T(8,128)S(1)} %get-tuple-element.41.acc_in, bf16[4,304,128]{2,1,0:T(8,128)(2,1)S(1)} %collective-permute-done.6.last.h7, ...), custom_call_target="tpu_custom_call" | custom-call | flops 536870912 | bytes 1048576 | tf_op jit(solution)/shard_map/targets/pallas_call | solution.py:314
  53.0 13.5 %all_to_all.16 = f16[32,32,128]{2,1,0:T(8,128)(2,1)S(1)} all-to-all(f16[32,32,128]{2,1,0:T(8,128)(2,1)S(1)} %broadcast_in_dim.12), channel_id=1, replica_groups=mesh['x'=4,'z'=8,'y'=4,'core'=2] {'x','z'}, dimensions={0} | all-to-all | bytes 524288 | tf_op jit(solution)/shard_map/all_to_all | solution.py:388
  66.5 0.1 convert_element_type.7.got_ref
  66.6 0.7 head_loss.1
  67.3 11.8 %all-to-all-start.2 = ((f32[8,8,128]{2,1,0:T(8,128)}), f32[8,8,128]{2,1,0:T(8,128)S(1)}, u32[]{:S(2)}, u32[]{:S(2)}) async-start(f32[8,8,128]{2,1,0:T(8,128)} %head_loss.1), calls=%async_computation.2 | async-start | bytes 65536 | tf_op jit(solution)/shard_map/all_to_all | solution.py:390
  79.1 2.5 %finish.1 = (f32[128,128]{1,0:T(8,128)}, f32[384,128]{1,0:T(8,128)}) custom-call(f32[32,32,128]{2,1,0:T(8,128)S(1)} %convert_element_type.7.got_ref, bf16[4,304,128]{2,1,0:T(8,128)(2,1)S(1)} %all_to_all.15.row.h0, bf16[4,304,128]{2,1,0:T(8,128)(2,1)S(1)} %collective-permute-done.back.h1, bf16[4,304,128]{2,1,0:T(8,128)(2,1)S(1)} %collective-permute-done.1.ahead.h2, ...), custom_call_target="tpu_custom_call" | custom-call | flops 134217728 | bytes 1048576 | tf_op jit(solution)/shard_map/finish/pallas_call | solution.py:314
  81.6 2.3 %all-to-all-done.2 = f32[8,8,128]{2,1,0:T(8,128)S(1)} async-done(((f32[8,8,128]{2,1,0:T(8,128)}), f32[8,8,128]{2,1,0:T(8,128)S(1)}, u32[]{:S(2)}, u32[]{:S(2)}) %all-to-all-start.2) | async-done | bytes 32800 | tf_op jit(solution)/shard_map/all_to_all | solution.py:390
  83.9 0.6 slice_reduce_fusion
  (18 shorter events, 0.1 us)
Async XLA Ops:
  0.6 18.6 %copy-start = (bf16[256,8,128]{2,1,0:T(8,128)(2,1)S(1)}, bf16[256,8,128]{2,1,0:T(8,128)(2,1)}, u32[]{:S(2)}) copy-start(bf16[256,8,128]{2,1,0:T(8,128)(2,1)} %param.5) | copy-start | bytes 1572868
  2.7 16.6 %copy-start.3 = (bf16[256,1,128]{2,0,1:T(8,128)(2,1)S(1)}, bf16[256,1,128]{2,0,1:T(8,128)(2,1)}, u32[]{:S(2)}) copy-start(bf16[256,1,128]{2,0,1:T(8,128)(2,1)} %param.6) | copy-start | bytes 196612
  2.7 16.6 %copy-start.4 = (f32[4,8,128]{2,1,0:T(8,128)S(1)}, f32[4,8,128]{2,1,0:T(8,128)}, u32[]{:S(2)}) copy-start(f32[4,8,128]{2,1,0:T(8,128)} %get-tuple-element.26.own_ref) | copy-start | bytes 49156
  13.5 10.3 %collective-permute-start.1 = (bf16[4,304,128]{2,1,0:T(8,128)(2,1)S(1)}, bf16[4,304,128]{2,1,0:T(8,128)(2,1)S(1)}, u32[]{:S(2)}, u32[]{:S(2)}) collective-permute-start(bf16[4,304,128]{2,1,0:T(8,128)(2,1)S(1)} %all_to_all.15.row.h0), channel_id=1, source_target_pairs={{0,56},{8,0},{16,8},{24,16},{32,24},{40,32},{48,40},{56,48},{1,57}... | collective-permute-start | bytes 933896 | tf_op jit(solution)/shard_map/ppermute | solution.py:352
  19.3 7.6 %collective-permute-start = (bf16[4,304,128]{2,1,0:T(8,128)(2,1)S(1)}, bf16[4,304,128]{2,1,0:T(8,128)(2,1)S(1)}, u32[]{:S(2)}, u32[]{:S(2)}) collective-permute-start(bf16[4,304,128]{2,1,0:T(8,128)(2,1)S(1)} %all_to_all.15.row.h0), channel_id=1, source_target_pairs={{0,8},{8,16},{16,24},{24,32},{32,40},{40,48},{48,56},{56,0},{1,9},... | collective-permute-start | bytes 933896 | tf_op jit(solution)/shard_map/ppermute | solution.py:352
  26.9 7.0 %collective-permute-start.2 = (bf16[4,304,128]{2,1,0:T(8,128)(2,1)S(1)}, bf16[4,304,128]{2,1,0:T(8,128)(2,1)S(1)}, u32[]{:S(2)}, u32[]{:S(2)}) collective-permute-start(bf16[4,304,128]{2,1,0:T(8,128)(2,1)S(1)} %collective-permute-done.back.h1), channel_id=1, source_target_pairs={{0,8},{8,16},{16,24},{24,32},{32,40},{40,48},{48,56},{56,0},{1,9},... | collective-permute-start | bytes 933896 | tf_op jit(solution)/shard_map/ppermute | solution.py:352
  26.9 7.0 %collective-permute-start.3 = (bf16[4,304,128]{2,1,0:T(8,128)(2,1)S(1)}, bf16[4,304,128]{2,1,0:T(8,128)(2,1)S(1)}, u32[]{:S(2)}, u32[]{:S(2)}) collective-permute-start(bf16[4,304,128]{2,1,0:T(8,128)(2,1)S(1)} %collective-permute-done.1.ahead.h2), channel_id=1, source_target_pairs={{0,56},{8,0},{16,8},{24,16},{32,24},{40,32},{48,40},{56,48},{1,57}... | collective-permute-start | bytes 933896 | tf_op jit(solution)/shard_map/ppermute | solution.py:352
  33.9 7.2 %collective-permute-start.4 = (bf16[4,304,128]{2,1,0:T(8,128)(2,1)S(1)}, bf16[4,304,128]{2,1,0:T(8,128)(2,1)S(1)}, u32[]{:S(2)}, u32[]{:S(2)}) collective-permute-start(bf16[4,304,128]{2,1,0:T(8,128)(2,1)S(1)} %collective-permute-done.2.back.h3), channel_id=1, source_target_pairs={{0,8},{8,16},{16,24},{24,32},{32,40},{40,48},{48,56},{56,0},{1,9},... | collective-permute-start | bytes 933896 | tf_op jit(solution)/shard_map/ppermute | solution.py:352
  33.9 7.2 %collective-permute-start.5 = (bf16[4,304,128]{2,1,0:T(8,128)(2,1)S(1)}, bf16[4,304,128]{2,1,0:T(8,128)(2,1)S(1)}, u32[]{:S(2)}, u32[]{:S(2)}) collective-permute-start(bf16[4,304,128]{2,1,0:T(8,128)(2,1)S(1)} %collective-permute-done.3.ahead.h4), channel_id=1, source_target_pairs={{0,56},{8,0},{16,8},{24,16},{32,24},{40,32},{48,40},{56,48},{1,57}... | collective-permute-start | bytes 933896 | tf_op jit(solution)/shard_map/ppermute | solution.py:352
  41.0 8.5 %copy-start.1 = (bf16[1,384,128]{2,1,0:T(8,128)(2,1)S(1)}, bf16[1,384,128]{2,1,0:T(8,128)(2,1)}, u32[]{:S(2)}) copy-start(bf16[1,384,128]{2,1,0:T(8,128)(2,1)} %param.9) | copy-start | bytes 294916
  41.0 8.5 %collective-permute-start.6 = (bf16[4,304,128]{2,1,0:T(8,128)(2,1)S(1)}, bf16[4,304,128]{2,1,0:T(8,128)(2,1)S(1)}, u32[]{:S(2)}, u32[]{:S(2)}) collective-permute-start(bf16[4,304,128]{2,1,0:T(8,128)(2,1)S(1)} %collective-permute-done.4.back.h5), channel_id=1, source_target_pairs={{0,8},{8,16},{16,24},{24,32},{32,40},{40,48},{48,56},{56,0},{1,9},... | collective-permute-start | bytes 933896 | tf_op jit(solution)/shard_map/ppermute | solution.py:352
  41.0 8.5 %copy-start.2 = (bf16[1,128,128]{2,1,0:T(8,128)(2,1)S(1)}, bf16[1,128,128]{2,1,0:T(8,128)(2,1)}, u32[]{:S(2)}) copy-start(bf16[1,128,128]{2,1,0:T(8,128)(2,1)} %param.8) | copy-start | bytes 98308
  44.6 4.9 %copy-start.5 = (bf16[32,128]{1,0:T(8,128)(2,1)S(1)}, bf16[32,128]{1,0:T(8,128)(2,1)}, u32[]{:S(2)}) copy-start(bf16[32,128]{1,0:T(8,128)(2,1)} %get-tuple-element.46.qpool_ref) | copy-start | bytes 24580
  67.3 16.5 %all-to-all-start.2 = ((f32[8,8,128]{2,1,0:T(8,128)}), f32[8,8,128]{2,1,0:T(8,128)S(1)}, u32[]{:S(2)}, u32[]{:S(2)}) async-start(f32[8,8,128]{2,1,0:T(8,128)} %head_loss.1), calls=%async_computation.2 | async-start | bytes 65536 | tf_op jit(solution)/shard_map/all_to_all | solution.py:390

commit v4 on v3

v4 whole, which is shorter than its diff:
```python
import functools
import math

import jax
import jax.numpy as jnp
from jax import lax
from jax.experimental import pallas as pl
from jax.experimental.pallas import tpu as pltpu
from jax.sharding import Mesh, PartitionSpec as P

BLOCK = 64
WIDTH = 128
GROUP = 8
LOCAL = 4
NX, NZ = 4, 8
SEQ = NX * NZ
NB = LOCAL * SEQ
ROWS = LOCAL * BLOCK
MORE = ROWS + 16
SENT = MORE + LOCAL * GROUP
LANES = BLOCK * GROUP
HX = NX // 2
HALF = LOCAL * HX
EXTRA = SENT - ROWS
STATS = 4 * LOCAL
CUT = HX * EXTRA * WIDTH // LANES
QSENT = LANES + 16
QROWS = LOCAL * GROUP
SCALE = WIDTH ** -0.5
EXP2 = SCALE * math.log2(math.e)
MASKED = -1e30 * WIDTH ** 0.5
FAR = 1e30
SHARE = 1.0 / (8 * GROUP * NB)
LIFT = 2.0 ** 14
HIGH = lax.Precision.HIGHEST
NT = (((1,), (1,)), ((), ()))
NN = (((1,), (0,)), ((), ()))
F32 = jnp.float32
BF16 = jnp.bfloat16
VMEM = pl.BlockSpec(memory_space=pltpu.VMEM)
HBM = pl.BlockSpec(memory_space=pltpu.HBM)


def dot(a, b, dims=NN, precision=None):
    return lax.dot_general(a, b, dims, precision=precision, preferred_element_type=F32)


def prepare(own_hbm, keys_hbm, q_hbm, out_ref, qx_ref, own_sm, keys_ref, q_ref, sems):
    copies = [
        pltpu.make_async_copy(own_hbm, own_sm, sems.at[0]),
        pltpu.make_async_copy(keys_hbm, keys_ref, sems.at[1]),
        pltpu.make_async_copy(q_hbm, q_ref, sems.at[2]),
    ]
    for copy in copies:
        copy.start()
    for copy in copies:
        copy.wait()
    keys = keys_ref[...]
    blocks = keys.astype(F32)
    kmax = jnp.max(blocks, axis=1)
    kmin = jnp.min(blocks, axis=1)
    kmean = jnp.sum(blocks, axis=1) * (1.0 / BLOCK)
    pos = [jnp.full((1, WIDTH), own_sm[b].astype(F32), F32) for b in range(LOCAL)]
    sub = lax.broadcasted_iota(jnp.int32, (BLOCK, LANES), 0)
    tok = lax.broadcasted_iota(jnp.int32, (BLOCK, LANES), 1) // GROUP
    for b in range(LOCAL):
        s = jnp.where(sub > tok, MASKED, dot(keys[b], q_ref[b], NT))
        ref = jnp.max(s, axis=0, keepdims=True)
        rows = [ref[:, i * WIDTH : (i + 1) * WIDTH] for i in range(LANES // WIDTH)]
        rows += [pos[b], jnp.zeros((11, WIDTH), F32)]
        qx_ref[b, :LANES, :] = q_ref[b]
        qx_ref[b, LANES:, :] = jnp.concatenate(rows, axis=0).astype(BF16)
    pos = jnp.concatenate(pos, axis=0)
    q = q_ref[...].astype(F32).reshape(LOCAL, BLOCK, GROUP, WIDTH)
    qpool = (jnp.sum(q, axis=1) * (1.0 / BLOCK)).reshape(QROWS, WIDTH).astype(BF16)
    extra = jnp.concatenate([kmax, kmin, kmean, pos], axis=0).astype(BF16)
    out_ref[:ROWS, :] = keys.reshape(ROWS, WIDTH)
    out_ref[ROWS:MORE, :] = extra
    out_ref[MORE:, :] = qpool


def maxima(parts):
    row = lax.broadcasted_iota(jnp.int32, parts[0].shape, 0)
    step = 1
    while len(parts) > 1:
        low = (row // step) % 2 == 0
        parts = [
            jnp.maximum(jnp.where(low, a, b), pltpu.roll(jnp.where(low, b, a), 8 - step, 0))
            for a, b in zip(parts[::2], parts[1::2])
        ]
        step *= 2
    return parts[0]


def fold(rows, qb, pb, ref, acc, keep, diag=None):
    for r, row in enumerate(rows):
        for i0 in range(0, HX, 2):
            tiles = [row[i, ROWS:MORE, :].astype(F32)[12:, :] for i in (i0, i0 + 1)]
            pos = jnp.concatenate(tiles, axis=0)
            early, same = pos < pb, pos == pb
            off = jnp.where(early, 0.0, FAR)
            offs = [jnp.broadcast_to(off[j : j + 1, :], (8, WIDTH)) for j in range(8)]
            kept, sums = [], []
            for at in range(0, LANES, 512):
                n = 512 // WIDTH
                base = ref[:, at : at + 512]
                tops = []
                total = acc[:, at : at + 512]
                for i in (0, 1):
                    s = dot(row[i0 + i, :ROWS, :], qb[at : at + 512, :], NT)
                    s = s.reshape(LOCAL, BLOCK // 8, 8, 512)
                    for j in range(LOCAL):
                        tops.append(jnp.max(s[j], axis=0))
                        shift = base + jnp.concatenate([offs[i * LOCAL + j]] * n, axis=1)
                        total = total + jnp.sum(jnp.exp2((s[j] - shift) * EXP2), axis=0)
                sums.append(total)
                top = maxima(tops)
                own = MASKED
                if diag is not None:
                    own = jnp.where(jnp.concatenate([same] * n, axis=1), diag[:, at : at + 512], MASKED)
                kept.append(jnp.where(jnp.concatenate([early] * n, axis=1), top, own))
            acc = jnp.concatenate(sums, axis=1)
            keep(r * HALF, jnp.concatenate(kept, axis=1))
    return acc


def stage(mine, q, mine_ref, q_ref):
    mine_ref[...] = mine[...]
    q_ref[...] = q[...]


def join(mine, beside, out_ref):
    odd = lax.axis_index("x") % 2
    out_ref[odd] = mine[...]
    out_ref[1 - odd] = beside[...]


def start_of(q_ref, b):
    extra = q_ref[b, LANES:, :].astype(F32)
    spread = [jnp.broadcast_to(extra[i : i + 1, :], (8, WIDTH)) for i in range(5)]
    return spread[4], jnp.concatenate(spread[:4], axis=1)


def sweep(*jobs):
    def run(job, b, ref, acc, store):
        rows, q_ref, _, bm_ref, acc_ref, ref_ref, diags = job
        pos, _ = start_of(q_ref, b)
        best = [ref]

        def keep(at, tops):
            best.append(jnp.maximum(best[-1], tops))
            if store:
                bm_ref[b, at : at + 8, :] = tops

        diag = diags[b] if diags is not None else None
        acc_ref[b] = fold(rows, q_ref[b, :LANES, :], pos, ref, acc, keep, diag)
        ref_ref[b] = ref
        return (best[-1] - ref) * EXP2

    worst = jnp.zeros((8, LANES), F32)
    for job in jobs:

        def one(b, worst, job=job):
            return jnp.maximum(worst, run(job, b, *job[2](b), True))

        worst = lax.fori_loop(0, LOCAL, one, worst, unroll=4)

    @pl.when(jnp.max(worst) > 80.0)
    def _():
        for job in jobs:

            def again(b, _, job=job):
                ref, acc = job[2](b)
                high = jnp.maximum(ref, jnp.max(job[3][b], axis=0, keepdims=True))
                run(job, b, high, acc * jnp.exp2((ref - high) * EXP2), False)
                return 0

            lax.fori_loop(0, LOCAL, again, 0)


def held(ref_in, acc_in):
    return lambda b: (ref_in[b], acc_in[b])


def first(q_ref, mine_ref, half, bm_ref, acc_ref, ref_ref, diags):
    sub = lax.broadcasted_iota(jnp.int32, (BLOCK, LANES), 0)
    tok = lax.broadcasted_iota(jnp.int32, (BLOCK, LANES), 1) // GROUP

    def state(b):
        _, ref = start_of(q_ref, b)
        s = jnp.where(sub > tok, MASKED, dot(mine_ref[pl.ds(pl.multiple_of(b * BLOCK, BLOCK), BLOCK), :], q_ref[b, :LANES, :], NT))
        diags[b] = jnp.broadcast_to(jnp.max(s, axis=0, keepdims=True), (8, LANES))
        e = jnp.exp2((s.reshape(BLOCK // 8, 8, LANES) - ref) * EXP2)
        return ref, jnp.sum(e, axis=0)

    sweep(([half], q_ref, state, bm_ref, acc_ref, ref_ref, diags))


def partner_first(q_ref, half, back, ahead, bm_ref, acc_ref, ref_ref):
    def state(b):
        return start_of(q_ref, b)[1], jnp.zeros((8, LANES), F32)

    sweep(([half, back, ahead], q_ref, state, bm_ref, acc_ref, ref_ref, None))


def middle(q_ref, acc_in, ref_in, back, ahead, bm_ref, acc_ref, ref_ref):
    sweep(([back, ahead], q_ref, held(ref_in, acc_in), bm_ref, acc_ref, ref_ref, None))


def both(q0, acc0, ref0, q1, acc1, ref1, back, ahead, bm0, acc0_out, ref0_out, bm1, acc1_out, ref1_out):
    sweep(
        ([back, ahead], q0, held(ref0, acc0), bm0, acc0_out, ref0_out, None),
        ([back, ahead], q1, held(ref1, acc1), bm1, acc1_out, ref1_out, None),
    )


def last_rows(q0, acc0, ref0, q1, acc1, ref1, row, bm0, bm1, stat_ref, a0, r0, a1, r1):
    sweep(
        ([row], q0, held(ref0, acc0), bm0, a0, r0, None),
        ([row], q1, held(ref1, acc1), bm1, a1, r1, None),
    )
    for n, (acc, ref) in enumerate(((a0, r0), (a1, r1))):
        for b in range(LOCAL):
            pair = [jnp.sum(acc[b], axis=0, keepdims=True), ref[b, :1, :]]
            at = (n * LOCAL + b) * 2
            stat_ref[at : at + 2, :] = jnp.concatenate(pair, axis=0)
    extra = row[:, ROWS:, :].astype(F32).reshape(HX * EXTRA, WIDTH)
    wide_rows = [extra[i * CUT : (i + 1) * CUT, :] for i in range(LANES // WIDTH)]
    stat_ref[STATS:, :] = jnp.concatenate(wide_rows, axis=1)


OFFSETS = (0, 7, 1, 6, 2, 5, 3, 4)


def pool(stat, other, *refs):
    bms, (out_ref, tgt) = (refs[:5], refs[5:9]), refs[11:]
    z = lax.axis_index("z")
    lane = lax.broadcasted_iota(jnp.int32, (HALF, WIDTH), 1)
    tgt[...] = jnp.zeros(tgt.shape, F32)
    for n in range(2):
        for b in range(LOCAL):
            here, there = (n * LOCAL + b) * 2, ((1 - n) * LOCAL + b) * 2
            ref0, ref1 = stat[here + 1 : here + 2, :], other[there + 1 : there + 2, :]
            ref = jnp.maximum(ref0, ref1)
            total = stat[here : here + 1, :] * jnp.exp2((ref0 - ref) * EXP2)
            total = total + other[there : there + 1, :] * jnp.exp2((ref1 - ref) * EXP2)
            logsum = jnp.log2(total)
            k = 0
            for bm in bms[n]:
                d = (bm[b] - ref) * EXP2 - logsum
                e = d[:, :WIDTH]
                for i in range(1, LANES // WIDTH):
                    e = jnp.maximum(e, d[:, i * WIDTH : (i + 1) * WIDTH])
                for shift in (8, 16, 32, 64):
                    e = jnp.maximum(e, pltpu.roll(e, shift, 1))
                e = jnp.exp2(e)
                for i in range(bm.shape[1] // HALF):
                    at = pl.multiple_of(lax.rem(z + OFFSETS[k], NZ) * HALF + n * NB // 2, HALF)
                    part = e[i * HALF : (i + 1) * HALF, :]
                    tgt[pl.ds(at, HALF), :] += jnp.where(lane // GROUP == b, part, 0.0)
                    k += 1
    out_ref[...] = tgt[...].T[:QROWS, :] * LIFT


def collect(mine, other, row, stat, qall, kall, posr=None):
    x, z = lax.axis_index("x"), lax.axis_index("z")

    def extra(far, k, i):
        if k < NZ - 1:
            ex = other if far else mine
            return ex[k * HX + i, :16, :].astype(F32), ex[k * HX + i, 16:, :]
        if not far:
            return row[i, ROWS:MORE, :].astype(F32), row[i, MORE:, :]
        low = stat[STATS:, 2 * i * WIDTH : (2 * i + 1) * WIDTH]
        high = stat[STATS:, (2 * i + 1) * WIDTH : (2 * i + 2) * WIDTH]
        return low[:16, :], jnp.concatenate([low[16:, :], high], axis=0).astype(BF16)

    for far, side in ((False, x // 2), (True, 1 - x // 2)):
        for k, off in enumerate(OFFSETS):
            at = lax.rem(z + off, NZ)
            pieces = [extra(far, k, i) for i in range(HX)]
            for part in range(4):
                got = jnp.concatenate([t[4 * part : 4 * part + 4, :] for t, _ in pieces], axis=0)
                to = pl.multiple_of(side * (NB // 2) + at * HALF, HALF)
                kall[part, pl.ds(to, HALF), :] = got
            for i, (tile, queries) in enumerate(pieces):
                to = pl.multiple_of(((side * HX + i) * NZ + at) * QROWS, QROWS)
                qall[pl.ds(to, QROWS), :] = queries
                if posr is not None:
                    rows = [jnp.broadcast_to(tile[12 + b : 13 + b, :], (GROUP, WIDTH)) for b in range(LOCAL)]
                    posr[pl.ds(to, QROWS), :] = jnp.concatenate(rows, axis=0)


def project(kall, wk_ref):
    kproj = jnp.zeros((NB, WIDTH), F32)
    for part in range(3):
        kproj = kproj + dot(kall[part].astype(BF16), wk_ref[part * WIDTH : (part + 1) * WIDTH, :])
    return kproj


def all_targets(got_ref):
    lane = lax.broadcasted_iota(jnp.int32, (NZ * QROWS, WIDTH), 1)
    parts = []
    for x in range(NX):
        own = got_ref[x * NZ : (x + 1) * NZ].reshape(NZ * QROWS, WIDTH)
        far = got_ref[(NX - 1 - x) * NZ : (NX - x) * NZ].reshape(NZ * QROWS, WIDTH)
        row = jnp.where(lane < NB // 2, own, far)
        parts.append(row if x < HX else pltpu.roll(row, NB // 2, 1))
    pooled = jnp.concatenate(parts, axis=0)
    return pooled / jnp.sum(pooled, axis=1, keepdims=True)


def head_loss(got_ref, mine, other, row, stat, wq_ref, wk_ref, out_ref, logp_ref, qall, kall, posr):
    collect(mine, other, row, stat, qall, kall, posr)
    qproj = dot(qall[...], wq_ref[...])
    logits = dot(qproj, project(kall, wk_ref), NT, HIGH) * SCALE
    logits = jnp.where(kall[3].T[:1, :] > posr[...], -1e30, logits)
    shifted = logits - jnp.max(logits, axis=1, keepdims=True)
    logp = shifted - jnp.log(jnp.sum(jnp.exp(shifted), axis=1, keepdims=True))
    logp_ref[...] = logp
    target = all_targets(got_ref)
    safe = jnp.log(jnp.where(target > 0, target, 1.0))
    terms = jnp.where(target > 0, target * (safe - logp), 0.0)
    loss = jnp.sum(jnp.sum(terms, axis=0, keepdims=True), axis=1, keepdims=True) * SHARE
    out_ref[...] = jnp.broadcast_to(loss.reshape(1, 1, 1), out_ref.shape)


def finish(got_ref, logp_ref, mine, other, row, stat, wq_ref, wk_ref, gq_ref, gk_ref, qall, kall):
    collect(mine, other, row, stat, qall, kall)
    target = all_targets(got_ref)
    rowtot = jnp.sum(target, axis=1, keepdims=True)
    dlogit = (jnp.exp(logp_ref[...]) * rowtot - target) * (SHARE * SCALE)
    both = dot(qall[...].astype(F32).T, dlogit, NN, HIGH)
    gq_ref[...] = dot(both, project(kall, wk_ref), NN, HIGH)
    dkproj = dot(wq_ref[...].astype(F32).T, both, NN, HIGH)
    for part in range(3):
        gk_ref[part * WIDTH : (part + 1) * WIDTH, :] = dot(kall[part].T, dkproj, NT, HIGH)


def call(kernel, out_shape, cost, *args, scratch=()):
    return pl.pallas_call(
        kernel,
        out_shape=out_shape,
        in_specs=[VMEM] * len(args),
        out_specs=jax.tree.map(lambda _: VMEM, out_shape),
        scratch_shapes=scratch,
        compiler_params=pltpu.CompilerParams(vmem_limit_bytes=40 << 20),
        cost_estimate=pl.CostEstimate(flops=cost, bytes_accessed=1 << 20, transcendentals=0),
        name=kernel.__name__,
    )(*args)


def shards(queries, keys, block_order, gate_query, gate_key):
    def f32(*shape):
        return jax.ShapeDtypeStruct(shape, F32)

    q4 = queries.reshape(LOCAL, LANES, WIDTH)
    k4 = keys.reshape(LOCAL, BLOCK, WIDTH)
    mine, q0 = pl.pallas_call(
        prepare,
        out_shape=(
            jax.ShapeDtypeStruct((SENT, WIDTH), BF16),
            jax.ShapeDtypeStruct((LOCAL, QSENT, WIDTH), BF16),
        ),
        in_specs=[HBM] * 3,
        out_specs=(VMEM, VMEM),
        scratch_shapes=[
            pltpu.SMEM((LOCAL,), jnp.int32),
            pltpu.VMEM(k4.shape, BF16),
            pltpu.VMEM(q4.shape, BF16),
            pltpu.SemaphoreType.DMA((3,)),
        ],
        name="prepare",
    )(block_order, k4, q4)

    def as_one(a):
        return jax.ShapeDtypeStruct(a.shape, a.dtype)

    def partner(a):
        return lax.ppermute(a, "x", [(i, NX - 1 - i) for i in range(NX)])

    def shift(a, by):
        return lax.ppermute(a, "z", [(i, (i + by) % NZ) for i in range(NZ)])

    beside = lax.ppermute(mine, "x", [(i, i ^ 1) for i in range(NX)])
    q1 = partner(q0)
    mine, q0 = call(stage, (as_one(mine), as_one(q0)), 1 << 10, mine, q0)
    half = call(join, jax.ShapeDtypeStruct((HX, SENT, WIDTH), BF16), 1 << 10, mine, beside)
    unit = LOCAL * LANES * HALF * BLOCK * WIDTH * 2
    state = (f32(LOCAL, 8, LANES),) * 2

    def maxima_of(n):
        return f32(LOCAL, n * HALF, LANES)

    rows = [half]
    back, ahead = shift(half, 1), shift(half, -1)
    bm, acc, ref = call(
        first, (maxima_of(1),) + state, unit, q0, mine, half,
        scratch=[pltpu.VMEM((LOCAL, 8, LANES), F32)],
    )
    own, other = [bm], []
    for k in range(1, 4):
        back, ahead, acc = lax.optimization_barrier((back, ahead, acc))
        here = (back, ahead)
        rows += here
        back = shift(back, 1)
        ahead = shift(ahead, -1) if k < 3 else None
        if k == 3:
            extras = jnp.concatenate([row[:, ROWS:, :] for row in rows], axis=0)
            far_extras = partner(extras)
        if k == 1:
            bm, acc, ref = call(middle, (maxima_of(2),) + state, 2 * unit, q0, acc, ref, *here)
            q1, acc = lax.optimization_barrier((q1, acc))
            bm1, acc1, ref1 = call(partner_first, (maxima_of(3),) + state, 3 * unit, q1, *rows)
        else:
            bm, acc, ref, bm1, acc1, ref1 = call(
                both, ((maxima_of(2),) + state) * 2, 4 * unit, q0, acc, ref, q1, acc1, ref1, *here
            )
        own.append(bm)
        other.append(bm1)
        acc, acc1 = lax.optimization_barrier((acc, acc1))
    bm0, bm1, stat = call(
        last_rows, (maxima_of(1), maxima_of(1), f32(STATS + CUT, LANES)), 2 * unit,
        q0, acc, ref, q1, acc1, ref1, back,
        scratch=[pltpu.VMEM((LOCAL, 8, LANES), F32)] * 4,
    )
    far_stat, far_extras = lax.optimization_barrier((partner(stat), far_extras))
    pooled = call(
        pool, f32(QROWS, WIDTH), unit // 4, stat, far_stat, *own, bm0, *other, bm1,
        gate_query[0], gate_key[0],
        scratch=[pltpu.VMEM((NB, WIDTH), F32)],
    )
    spread = jnp.broadcast_to(pooled.astype(jnp.float16)[None], (SEQ, QROWS, WIDTH))
    given = (extras, far_extras, back, far_stat, gate_query[0], gate_key[0])
    got = lax.all_to_all(spread, ("x", "z"), 0, 0).astype(F32)
    gathered = [pltpu.VMEM((SEQ * QROWS, WIDTH), BF16), pltpu.VMEM((4, NB, WIDTH), F32)]
    loss, logp = call(
        head_loss, (f32(8, 8, WIDTH), f32(SEQ * QROWS, WIDTH)), unit, got, *given,
        scratch=gathered + [pltpu.VMEM((SEQ * QROWS, WIDTH), F32)],
    )
    loss = lax.all_to_all(loss, ("y", "core"), 0, 0)
    grad_q, grad_k = call(
        finish, (f32(WIDTH, WIDTH), f32(3 * WIDTH, WIDTH)), unit,
        got, logp, *given, scratch=gathered,
    )
    return jnp.sum(loss[:, 0, 0]), grad_q[None], grad_k[None]


def solution(mesh):
    fine = Mesh(mesh.devices.reshape(NX, NZ, 4, 2), ("x", "z", "y", "core"))
    seq, head = ("x", "z"), ("y", "core")
    return jax.shard_map(
        shards,
        mesh=fine,
        in_specs=(
            P(seq, head, None),
            P(seq, head, None),
            P(seq),
            P(head, None, None),
            P(head, None, None),
        ),
        out_specs=(P(), P(head, None, None), P(head, None, None)),
        check_vma=False,
    )
```

time: 84.8 us -> 81.6 us (0.962)
  blocking collectives: 24.2 us -> 14.7 us
  starting transfers between devices: 23 us -> 29.3 us
  waiting for transfers between devices: 14.3 us -> 10.3 us
  Pallas kernels: 21.4 us -> 23.4 us
  local copies, waits for them, and re-layouts: 0.07 us -> 2.07 us
    all_to_all x1 -> x0, blocking collectives: 10.8 us -> none  [shards(): row = lax.all_to_all(mine, 'x', 0, 0)]
    ppermute x7, waiting for transfers between devices: 12.1 us -> 4.9 us  [shift(): return lax.ppermute(a, 'z', [(i, (i + by) % NZ) for i in range(NZ)])]
    ppermute x0 -> x4, starting transfers between devices: none -> 6.19 us  [the longest x3 4.07 us: partner(): return lax.ppermute(a, 'x', [(i, NX - 1 - i) for i in range(NX)])]
    ppermute x0 -> x4, waiting for transfers between devices: none -> 3.3 us  [the longest x3 3.3 us: partner(): return lax.ppermute(a, 'x', [(i, NX - 1 - i) for i in range(NX)])]
    pallas_call x8 -> x12, Pallas kernels: 21.4 us -> 23.4 us  [the longest x11 21.1 us: call(): pl.pallas_call(kernel, out_shape=out_shape, in_specs=[VMEM] * len(args),...]
    unnamed x12 -> x14, local copies, waits for them, and re-layouts: 0.03 us -> 2.02 us
    all_to_all x1, blocking collectives: 13.5 us -> 14.7 us  [shards(): got = lax.all_to_all(spread, ('x', 'z'), 0, 0).astype(F32)]
  transfers between devices with their start and end apart: 8 -> 12, of which waited for: 6 -> 5; matrix products, arithmetic and copies ran while one was open for 0% -> 0% of each run, Pallas kernels for 18% -> 23%
where the time goes in v4:
time: 81.6 us; the launch traced here: 81.3 us
  starting transfers between devices  29.3 us (36%)
  Pallas kernels  23.4 us (29%)
  blocking collectives  14.7 us (18%)
  waiting for transfers between devices  10.3 us (13%)
  local copies, waits for them, and re-layouts  2.07 us (3%)
  between operations  0.82 us (1%)
    pallas_call x11, Pallas kernels, call(): pl.pallas_call(kernel, out_shape=out_shape, in_specs=[VMEM] * len(args),...  21.1 us
    all_to_all x1, blocking collectives, shards(): got = lax.all_to_all(spread, ('x', 'z'), 0, 0).astype(F32)  14.7 us
    all_to_all x1, starting transfers between devices, shards(): loss = lax.all_to_all(loss, ('y', 'core'), 0, 0)  12 us
    ppermute x7, starting transfers between devices, shift(): return lax.ppermute(a, 'z', [(i, (i + by) % NZ) for i in range(NZ)])  11.2 us
    ppermute x7, waiting for transfers between devices, shift(): return lax.ppermute(a, 'z', [(i, (i + by) % NZ) for i in range(NZ)])  4.9 us
    ppermute x3, starting transfers between devices, partner(): return lax.ppermute(a, 'x', [(i, NX - 1 - i) for i in range(NX)])  4.07 us
    ppermute x3, waiting for transfers between devices, partner(): return lax.ppermute(a, 'x', [(i, NX - 1 - i) for i in range(NX)])  3.3 us
    pallas_call x1, Pallas kernels, shards(): pl.pallas_call(prepare, out_shape=(jax.ShapeDtypeStruct((SENT, WIDTH), BF...  2.31 us
  transfers between devices with their start and end apart: 12, of which 5 were waited for; matrix products, arithmetic and copies ran while one was open for 0% of the time, Pallas kernels for 23%

profile of v4, /device:TPU:1, one launch (start us, length us, event | category | flops | bytes accessed | tf_op | source)
XLA Modules:
  0.0 81.3 jit_solution(11836856629382353260)
XLA Ops:
  0.6 2.3 %prepare.1 = (bf16[304,128]{1,0:T(8,128)(2,1)}, bf16[4,528,128]{2,1,0:T(8,128)(2,1)}) custom-call(s32[4]{0:T(128)} %own_hbm.1, bf16[4,64,128]{2,1,0:T(8,128)(2,1)} %bitcast.13, bf16[4,512,128]{2,1,0:T(8,128)(2,1)} %bitcast.12), custom_call_target="tpu_custom_call" | custom-call | tf_op jit(solution)/shard_map/prepare/pallas_call | solution.py:359
  2.9 2.1 %collective-permute-start = (bf16[304,128]{1,0:T(8,128)(2,1)}, bf16[304,128]{1,0:T(8,128)(2,1)S(1)}, u32[]{:S(2)}, u32[]{:S(2)}) collective-permute-start(bf16[304,128]{1,0:T(8,128)(2,1)} %get-tuple-element.54.mine), channel_id=1, source_target_pairs={{0,64},{64,0},{128,192},{192,128},{1,65},{65,1},{129,193},{193,129... | collective-permute-start | bytes 233480 | tf_op jit(solution)/shard_map/ppermute | solution.py:385
  5.1 1.8 %collective-permute-start.5 = (bf16[4,528,128]{2,1,0:T(8,128)(2,1)}, bf16[4,528,128]{2,1,0:T(8,128)(2,1)S(1)}, u32[]{:S(2)}, u32[]{:S(2)}) collective-permute-start(bf16[4,528,128]{2,1,0:T(8,128)(2,1)} %get-tuple-element.55.q), channel_id=1, source_target_pairs={{0,192},{64,128},{128,64},{192,0},{1,193},{65,129},{129,65},{193,1... | collective-permute-start | bytes 1622024 | tf_op jit(solution)/shard_map/ppermute | solution.py:380
  6.9 1.1 %copy-done.1 = bf16[4,528,128]{2,1,0:T(8,128)(2,1)S(1)} copy-done((bf16[4,528,128]{2,1,0:T(8,128)(2,1)S(1)}, bf16[4,528,128]{2,1,0:T(8,128)(2,1)}, u32[]{:S(2)}) %copy-start.1) | copy-done | bytes 540696
  8.0 0.9 %copy-done.3 = bf16[304,128]{1,0:T(8,128)(2,1)S(1)} copy-done((bf16[304,128]{1,0:T(8,128)(2,1)S(1)}, bf16[304,128]{1,0:T(8,128)(2,1)}, u32[]{:S(2)}) %copy-start.3) | copy-done | bytes 77848
  8.9 5.7 %collective-permute-start.2 = (bf16[2,304,128]{2,1,0:T(8,128)(2,1)S(1)}, bf16[2,304,128]{2,1,0:T(8,128)(2,1)S(1)}, u32[]{:S(2)}, u32[]{:S(2)}) collective-permute-start(bf16[2,304,128]{2,1,0:T(8,128)(2,1)S(1)} %join.1.half), channel_id=1, source_target_pairs={{0,56},{8,0},{16,8},{24,16},{32,24},{40,32},{48,40},{56,48},{1,57}... | collective-permute-start | bytes 466952 | tf_op jit(solution)/shard_map/ppermute | solution.py:383
  14.6 1.3 %first.1 = (f32[4,8,512]{2,1,0:T(8,128)S(1)}, f32[4,8,512]{2,1,0:T(8,128)S(1)}, f32[4,8,512]{2,1,0:T(8,128)S(1)}) custom-call(bf16[4,528,128]{2,1,0:T(8,128)(2,1)S(1)} %get-tuple-element.56.q_ref.q0, bf16[304,128]{1,0:T(8,128)(2,1)S(1)} %get-tuple-element.57.mine.mine_ref, bf16[2,304,128]{2,1,0:T(8,128)(2,1)S(1)} %join.1.half), custom_call_target="tpu_custom_call" | custom-call | flops 268435456 | bytes 1048576 | tf_op jit(solution)/shard_map/first/pallas_call | solution.py:341
  16.8 3.4 %collective-permute-done.1.back = bf16[2,304,128]{2,1,0:T(8,128)(2,1)S(1)} collective-permute-done((bf16[2,304,128]{2,1,0:T(8,128)(2,1)S(1)}, bf16[2,304,128]{2,1,0:T(8,128)(2,1)S(1)}, u32[]{:S(2)}, u32[]{:S(2)}) %collective-permute-start.1) | collective-permute-done | bytes 155680 | tf_op jit(solution)/shard_map/ppermute | solution.py:383
  20.2 2.7 %collective-permute-start.4 = (bf16[2,304,128]{2,1,0:T(8,128)(2,1)S(1)}, bf16[2,304,128]{2,1,0:T(8,128)(2,1)S(1)}, u32[]{:S(2)}, u32[]{:S(2)}) collective-permute-start(bf16[2,304,128]{2,1,0:T(8,128)(2,1)S(1)} %collective-permute-done.2.ahead), channel_id=1, source_target_pairs={{0,56},{8,0},{16,8},{24,16},{32,24},{40,32},{48,40},{56,48},{1,57}... | collective-permute-start | bytes 466952 | tf_op jit(solution)/shard_map/ppermute | solution.py:383
  22.9 2.0 %middle.1 = (f32[4,16,512]{2,1,0:T(8,128)S(1)}, f32[4,8,512]{2,1,0:T(8,128)S(1)}, f32[4,8,512]{2,1,0:T(8,128)S(1)}) custom-call(bf16[4,528,128]{2,1,0:T(8,128)(2,1)S(1)} %get-tuple-element.56.q_ref.q0, f32[4,8,512]{2,1,0:T(8,128)S(1)} %get-tuple-element.61.acc_in, f32[4,8,512]{2,1,0:T(8,128)S(1)} %get-tuple-element.62.ref_in, ...), custom_call_target="tpu_custom_call" | custom-call | flops 536870912 | bytes 1048576 | tf_op jit(solution)/shard_map/middle/pallas_call | solution.py:341
  24.9 2.8 %partner_first.1 = (f32[4,24,512]{2,1,0:T(8,128)S(1)}, f32[4,8,512]{2,1,0:T(8,128)S(1)}, f32[4,8,512]{2,1,0:T(8,128)S(1)}) custom-call(bf16[4,528,128]{2,1,0:T(8,128)(2,1)S(1)} %collective-permute-done.5.q_ref.q1, bf16[2,304,128]{2,1,0:T(8,128)(2,1)S(1)} %join.1.half, bf16[2,304,128]{2,1,0:T(8,128)(2,1)S(1)} %collective-permute-done.1.back, ...), custom_call_target="tpu_custom_call" | custom-call | flops 805306368 | bytes 1048576 | tf_op jit(solution)/shard_map/partner_first/pallas_call | solution.py:341
  27.8 2.7 %collective-permute-start.7 = (bf16[2,304,128]{2,1,0:T(8,128)(2,1)S(1)}, bf16[2,304,128]{2,1,0:T(8,128)(2,1)S(1)}, u32[]{:S(2)}, u32[]{:S(2)}) collective-permute-start(bf16[2,304,128]{2,1,0:T(8,128)(2,1)S(1)} %collective-permute-done.4.ahead), channel_id=1, source_target_pairs={{0,56},{8,0},{16,8},{24,16},{32,24},{40,32},{48,40},{56,48},{1,57}... | collective-permute-start | bytes 466952 | tf_op jit(solution)/shard_map/ppermute | solution.py:383
  30.4 3.6 %both.2 = (f32[4,16,512]{2,1,0:T(8,128)S(1)}, f32[4,8,512]{2,1,0:T(8,128)S(1)}, f32[4,8,512]{2,1,0:T(8,128)S(1)}, f32[4,16,512]{2,1,0:T(8,128)S(1)}, f32[4,8,512]{2,1,0:T(8,128)S(1)}, /*index=5*/f32[4,8,512]{2,1,0:T(8,128)S(1)}) custom-call(bf16[4,528,128]{2,1,0:T(8,128)(2,1)S(1)} %get-tuple-element.56.q_ref.q0, f32[4,8,512]{2,1,0:T(8,128)S(1)} %get-tuple-element.70.acc0, ...), custom_call_target="tpu_custom_call" | custom-call | flops 1073741824 | bytes 1048576 | tf_op jit(solution)/shard_map/both/pallas_call | solution.py:341
  34.3 1.0 %collective-permute-start.10 = (bf16[14,48,128]{2,1,0:T(8,128)(2,1)S(1)}, bf16[14,48,128]{2,1,0:T(8,128)(2,1)S(1)}, u32[]{:S(2)}, u32[]{:S(2)}) collective-permute-start(bf16[14,48,128]{2,1,0:T(8,128)(2,1)S(1)} %slice_dynamic-update-slice_fusion.1.mine), channel_id=1, source_target_pairs={{0,192},{64,128},{128,64},{192,0},{1,193},{65,129},{129,65},{193,1... | collective-permute-start | bytes 516104 | tf_op jit(solution)/shard_map/ppermute | solution.py:380
  35.2 3.7 %both.3 = (f32[4,16,512]{2,1,0:T(8,128)S(1)}, f32[4,8,512]{2,1,0:T(8,128)S(1)}, f32[4,8,512]{2,1,0:T(8,128)S(1)}, f32[4,16,512]{2,1,0:T(8,128)S(1)}, f32[4,8,512]{2,1,0:T(8,128)S(1)}, /*index=5*/f32[4,8,512]{2,1,0:T(8,128)S(1)}) custom-call(bf16[4,528,128]{2,1,0:T(8,128)(2,1)S(1)} %get-tuple-element.56.q_ref.q0, f32[4,8,512]{2,1,0:T(8,128)S(1)} %get-tuple-element.77.acc0, ...), custom_call_target="tpu_custom_call" | custom-call | flops 1073741824 | bytes 1048576 | tf_op jit(solution)/shard_map/both/pallas_call | solution.py:341
  39.5 2.2 %last_rows.1 = (f32[4,8,512]{2,1,0:T(8,128)S(1)}, f32[4,8,512]{2,1,0:T(8,128)S(1)}, f32[40,512]{1,0:T(8,128)S(1)}) custom-call(bf16[4,528,128]{2,1,0:T(8,128)(2,1)S(1)} %get-tuple-element.56.q_ref.q0, f32[4,8,512]{2,1,0:T(8,128)S(1)} %get-tuple-element.85.acc0, f32[4,8,512]{2,1,0:T(8,128)S(1)} %get-tuple-element.86.ref0, ...), custom_call_target="tpu_custom_call" | custom-call | flops 536870912 | bytes 1048576 | tf_op jit(solution)/shard_map/last_rows/pallas_call | solution.py:341
  41.7 1.3 %collective-permute-start.9 = (f32[40,512]{1,0:T(8,128)S(1)}, f32[40,512]{1,0:T(8,128)S(1)}, u32[]{:S(2)}, u32[]{:S(2)}) collective-permute-start(f32[40,512]{1,0:T(8,128)S(1)} %get-tuple-element.89.stat), channel_id=1, source_target_pairs={{0,192},{64,128},{128,64},{192,0},{1,193},{65,129},{129,65},{193,1... | collective-permute-start | bytes 245768 | tf_op jit(solution)/shard_map/ppermute | solution.py:380
  43.0 3.3 %collective-permute-done.9.other.stat = f32[40,512]{1,0:T(8,128)S(1)} collective-permute-done((f32[40,512]{1,0:T(8,128)S(1)}, f32[40,512]{1,0:T(8,128)S(1)}, u32[]{:S(2)}, u32[]{:S(2)}) %collective-permute-start.9) | collective-permute-done | bytes 81952 | tf_op jit(solution)/shard_map/ppermute | solution.py:380
  46.3 0.9 %pool.1 = f32[32,128]{1,0:T(8,128)S(1)} custom-call(f32[40,512]{1,0:T(8,128)S(1)} %get-tuple-element.89.stat, f32[40,512]{1,0:T(8,128)S(1)} %collective-permute-done.9.other.stat, f32[4,8,512]{2,1,0:T(8,128)S(1)} %get-tuple-element.91.refs_0_, f32[4,16,512]{2,1,0:T(8,128)S(1)} %get-tuple-element.92.refs_1_, f32[4,16,512]{2,1,0:T(8,128)S(1)} %get-tuple-element.93.refs_2_, ...), custom_call_target="tpu_custom_call" | custom-call | flops 67108864 | bytes 1048576 | tf_op jit(solution)/shard_map/pool/pallas_call | solution.py:341
  47.4 14.7 %all_to_all.10 = f16[32,32,128]{2,1,0:T(8,128)(2,1)S(1)} all-to-all(f16[32,32,128]{2,1,0:T(8,128)(2,1)S(1)} %broadcast_in_dim.12), channel_id=1, replica_groups=mesh['x'=4,'z'=8,'y'=4,'core'=2] {'x','z'}, dimensions={0} | all-to-all | bytes 524288 | tf_op jit(solution)/shard_map/all_to_all | solution.py:435
  62.1 1.9 %head_loss.1 = (f32[8,8,128]{2,1,0:T(8,128)}, f32[1024,128]{1,0:T(8,128)S(1)}) custom-call(f32[32,32,128]{2,1,0:T(8,128)S(1)} %convert_element_type.7.got_ref, bf16[14,48,128]{2,1,0:T(8,128)(2,1)S(1)} %slice_dynamic-update-slice_fusion.1.mine, bf16[14,48,128]{2,1,0:T(8,128)(2,1)S(1)} %collective-permute-done.10.other, ...), custom_call_target="tpu_custom_call" | custom-call | flops 268435456 | bytes 1048576 | tf_op jit(solution)/shard_map/head_loss/pallas_call | solution.py:341
  64.0 12.0 %all-to-all-start.1 = ((f32[8,8,128]{2,1,0:T(8,128)}), f32[8,8,128]{2,1,0:T(8,128)S(1)}, u32[]{:S(2)}, u32[]{:S(2)}) async-start(f32[8,8,128]{2,1,0:T(8,128)} %get-tuple-element.101), calls=%async_computation.1 | async-start | bytes 65536 | tf_op jit(solution)/shard_map/all_to_all | solution.py:441
  76.0 2.7 %finish.1 = (f32[128,128]{1,0:T(8,128)}, f32[384,128]{1,0:T(8,128)}) custom-call(f32[32,32,128]{2,1,0:T(8,128)S(1)} %convert_element_type.7.got_ref, f32[1024,128]{1,0:T(8,128)S(1)} %get-tuple-element.102.logp_ref, bf16[14,48,128]{2,1,0:T(8,128)(2,1)S(1)} %slice_dynamic-update-slice_fusion.1.mine, bf16[14,48,128]{2,1,0:T(8,128)(2,1)S(1)} %collective-permute-done.10.other, ...), custom_call_target="tpu_custom_call" | custom-call | flops 268435456 | bytes 1048576 | tf_op jit(solution)/shard_map/finish/pallas_call | solution.py:341
  78.6 2.1 %all-to-all-done.1 = f32[8,8,128]{2,1,0:T(8,128)S(1)} async-done(((f32[8,8,128]{2,1,0:T(8,128)}), f32[8,8,128]{2,1,0:T(8,128)S(1)}, u32[]{:S(2)}, u32[]{:S(2)}) %all-to-all-start.1) | async-done | bytes 32800 | tf_op jit(solution)/shard_map/all_to_all | solution.py:441
  (32 shorter events, 2.5 us)
Async XLA Ops:
  2.9 6.0 %collective-permute-start = (bf16[304,128]{1,0:T(8,128)(2,1)}, bf16[304,128]{1,0:T(8,128)(2,1)S(1)}, u32[]{:S(2)}, u32[]{:S(2)}) collective-permute-start(bf16[304,128]{1,0:T(8,128)(2,1)} %get-tuple-element.54.mine), channel_id=1, source_target_pairs={{0,64},{64,0},{128,192},{192,128},{1,65},{65,1},{129,193},{193,129... | collective-permute-start | bytes 233480 | tf_op jit(solution)/shard_map/ppermute | solution.py:385
  5.1 19.8 %collective-permute-start.5 = (bf16[4,528,128]{2,1,0:T(8,128)(2,1)}, bf16[4,528,128]{2,1,0:T(8,128)(2,1)S(1)}, u32[]{:S(2)}, u32[]{:S(2)}) collective-permute-start(bf16[4,528,128]{2,1,0:T(8,128)(2,1)} %get-tuple-element.55.q), channel_id=1, source_target_pairs={{0,192},{64,128},{128,64},{192,0},{1,193},{65,129},{129,65},{193,1... | collective-permute-start | bytes 1622024 | tf_op jit(solution)/shard_map/ppermute | solution.py:380
  6.9 1.1 %copy-start.1 = (bf16[4,528,128]{2,1,0:T(8,128)(2,1)S(1)}, bf16[4,528,128]{2,1,0:T(8,128)(2,1)}, u32[]{:S(2)}) copy-start(bf16[4,528,128]{2,1,0:T(8,128)(2,1)} %get-tuple-element.55.q) | copy-start | bytes 1622020
  8.0 0.9 %copy-start.3 = (bf16[304,128]{1,0:T(8,128)(2,1)S(1)}, bf16[304,128]{1,0:T(8,128)(2,1)}, u32[]{:S(2)}) copy-start(bf16[304,128]{1,0:T(8,128)(2,1)} %get-tuple-element.54.mine) | copy-start | bytes 233476
  8.9 7.8 %collective-permute-start.2 = (bf16[2,304,128]{2,1,0:T(8,128)(2,1)S(1)}, bf16[2,304,128]{2,1,0:T(8,128)(2,1)S(1)}, u32[]{:S(2)}, u32[]{:S(2)}) collective-permute-start(bf16[2,304,128]{2,1,0:T(8,128)(2,1)S(1)} %join.1.half), channel_id=1, source_target_pairs={{0,56},{8,0},{16,8},{24,16},{32,24},{40,32},{48,40},{56,48},{1,57}... | collective-permute-start | bytes 466952 | tf_op jit(solution)/shard_map/ppermute | solution.py:383
  14.6 5.6 %collective-permute-start.1 = (bf16[2,304,128]{2,1,0:T(8,128)(2,1)S(1)}, bf16[2,304,128]{2,1,0:T(8,128)(2,1)S(1)}, u32[]{:S(2)}, u32[]{:S(2)}) collective-permute-start(bf16[2,304,128]{2,1,0:T(8,128)(2,1)S(1)} %join.1.half), channel_id=1, source_target_pairs={{0,8},{8,16},{16,24},{24,32},{32,40},{40,48},{48,56},{56,0},{1,9},... | collective-permute-start | bytes 466952 | tf_op jit(solution)/shard_map/ppermute | solution.py:383
  20.2 7.5 %collective-permute-start.3 = (bf16[2,304,128]{2,1,0:T(8,128)(2,1)S(1)}, bf16[2,304,128]{2,1,0:T(8,128)(2,1)S(1)}, u32[]{:S(2)}, u32[]{:S(2)}) collective-permute-start(bf16[2,304,128]{2,1,0:T(8,128)(2,1)S(1)} %collective-permute-done.1.back), channel_id=1, source_target_pairs={{0,8},{8,16},{16,24},{24,32},{32,40},{40,48},{48,56},{56,0},{1,9},... | collective-permute-start | bytes 466952 | tf_op jit(solution)/shard_map/ppermute | solution.py:383
  20.2 7.5 %collective-permute-start.4 = (bf16[2,304,128]{2,1,0:T(8,128)(2,1)S(1)}, bf16[2,304,128]{2,1,0:T(8,128)(2,1)S(1)}, u32[]{:S(2)}, u32[]{:S(2)}) collective-permute-start(bf16[2,304,128]{2,1,0:T(8,128)(2,1)S(1)} %collective-permute-done.2.ahead), channel_id=1, source_target_pairs={{0,56},{8,0},{16,8},{24,16},{32,24},{40,32},{48,40},{56,48},{1,57}... | collective-permute-start | bytes 466952 | tf_op jit(solution)/shard_map/ppermute | solution.py:383
  27.7 6.4 %collective-permute-start.6 = (bf16[2,304,128]{2,1,0:T(8,128)(2,1)S(1)}, bf16[2,304,128]{2,1,0:T(8,128)(2,1)S(1)}, u32[]{:S(2)}, u32[]{:S(2)}) collective-permute-start(bf16[2,304,128]{2,1,0:T(8,128)(2,1)S(1)} %collective-permute-done.3.back), channel_id=1, source_target_pairs={{0,8},{8,16},{16,24},{24,32},{32,40},{40,48},{48,56},{56,0},{1,9},... | collective-permute-start | bytes 466952 | tf_op jit(solution)/shard_map/ppermute | solution.py:383
  27.8 6.3 %collective-permute-start.7 = (bf16[2,304,128]{2,1,0:T(8,128)(2,1)S(1)}, bf16[2,304,128]{2,1,0:T(8,128)(2,1)S(1)}, u32[]{:S(2)}, u32[]{:S(2)}) collective-permute-start(bf16[2,304,128]{2,1,0:T(8,128)(2,1)S(1)} %collective-permute-done.4.ahead), channel_id=1, source_target_pairs={{0,56},{8,0},{16,8},{24,16},{32,24},{40,32},{48,40},{56,48},{1,57}... | collective-permute-start | bytes 466952 | tf_op jit(solution)/shard_map/ppermute | solution.py:383
  34.1 5.4 %collective-permute-start.8 = (bf16[2,304,128]{2,1,0:T(8,128)(2,1)S(1)}, bf16[2,304,128]{2,1,0:T(8,128)(2,1)S(1)}, u32[]{:S(2)}, u32[]{:S(2)}) collective-permute-start(bf16[2,304,128]{2,1,0:T(8,128)(2,1)S(1)} %collective-permute-done.6.back), channel_id=1, source_target_pairs={{0,8},{8,16},{16,24},{24,32},{32,40},{40,48},{48,56},{56,0},{1,9},... | collective-permute-start | bytes 466952 | tf_op jit(solution)/shard_map/ppermute | solution.py:383
  34.3 8.8 %collective-permute-start.10 = (bf16[14,48,128]{2,1,0:T(8,128)(2,1)S(1)}, bf16[14,48,128]{2,1,0:T(8,128)(2,1)S(1)}, u32[]{:S(2)}, u32[]{:S(2)}) collective-permute-start(bf16[14,48,128]{2,1,0:T(8,128)(2,1)S(1)} %slice_dynamic-update-slice_fusion.1.mine), channel_id=1, source_target_pairs={{0,192},{64,128},{128,64},{192,0},{1,193},{65,129},{129,65},{193,1... | collective-permute-start | bytes 516104 | tf_op jit(solution)/shard_map/ppermute | solution.py:380
  39.5 6.8 %copy-start = (bf16[1,384,128]{2,1,0:T(8,128)(2,1)S(1)}, bf16[1,384,128]{2,1,0:T(8,128)(2,1)}, u32[]{:S(2)}) copy-start(bf16[1,384,128]{2,1,0:T(8,128)(2,1)} %param.9) | copy-start | bytes 294916
  39.5 6.8 %copy-start.2 = (bf16[1,128,128]{2,1,0:T(8,128)(2,1)S(1)}, bf16[1,128,128]{2,1,0:T(8,128)(2,1)}, u32[]{:S(2)}) copy-start(bf16[1,128,128]{2,1,0:T(8,128)(2,1)} %param.8) | copy-start | bytes 98308
  41.7 4.6 %collective-permute-start.9 = (f32[40,512]{1,0:T(8,128)S(1)}, f32[40,512]{1,0:T(8,128)S(1)}, u32[]{:S(2)}, u32[]{:S(2)}) collective-permute-start(f32[40,512]{1,0:T(8,128)S(1)} %get-tuple-element.89.stat), channel_id=1, source_target_pairs={{0,192},{64,128},{128,64},{192,0},{1,193},{65,129},{129,65},{193,1... | collective-permute-start | bytes 245768 | tf_op jit(solution)/shard_map/ppermute | solution.py:380
  64.0 16.7 %all-to-all-start.1 = ((f32[8,8,128]{2,1,0:T(8,128)}), f32[8,8,128]{2,1,0:T(8,128)S(1)}, u32[]{:S(2)}, u32[]{:S(2)}) async-start(f32[8,8,128]{2,1,0:T(8,128)} %get-tuple-element.101), calls=%async_computation.1 | async-start | bytes 65536 | tf_op jit(solution)/shard_map/all_to_all | solution.py:441

commit v5 on v4

--- a/solution.py
+++ b/solution.py
@@ -359,8 +359,8 @@
     mine, q0 = pl.pallas_call(
         prepare,
         out_shape=(
-            jax.ShapeDtypeStruct((SENT, WIDTH), BF16),
-            jax.ShapeDtypeStruct((LOCAL, QSENT, WIDTH), BF16),
+            pltpu.VMEM((SENT, WIDTH), BF16),
+            pltpu.VMEM((LOCAL, QSENT, WIDTH), BF16),
         ),
         in_specs=[HBM] * 3,
         out_specs=(VMEM, VMEM),
@@ -384,7 +384,6 @@
 
     beside = lax.ppermute(mine, "x", [(i, i ^ 1) for i in range(NX)])
     q1 = partner(q0)
-    mine, q0 = call(stage, (as_one(mine), as_one(q0)), 1 << 10, mine, q0)
     half = call(join, jax.ShapeDtypeStruct((HX, SENT, WIDTH), BF16), 1 << 10, mine, beside)
     unit = LOCAL * LANES * HALF * BLOCK * WIDTH * 2
     state = (f32(LOCAL, 8, LANES),) * 2

time: 81.6 us -> 79.7 us (0.977)
  local copies, waits for them, and re-layouts: 2.07 us -> 0.11 us
  starting transfers between devices: 29.3 us -> 30.9 us
  waiting for transfers between devices: 10.3 us -> 9.36 us
    unnamed x14 -> x10, local copies, waits for them, and re-layouts: 2.02 us -> 0.06 us
    ppermute x3, starting transfers between devices: 4.07 us -> 5.91 us  [partner(): return lax.ppermute(a, 'x', [(i, NX - 1 - i) for i in range(NX)])]
    pallas_call x11 -> x10, Pallas kernels: 21.1 us -> 21.1 us  [call(): pl.pallas_call(kernel, out_shape=out_shape, in_specs=[VMEM] * len(args),...]
  transfers between devices with their start and end apart: 12 -> 12, of which waited for: 5 -> 4; matrix products, arithmetic and copies ran while one was open for 0% -> 0% of each run, Pallas kernels for 23% -> 23%
where the time goes in v5:
time: 79.7 us; the launch traced here: 79.5 us
  starting transfers between devices  30.9 us (39%)
  Pallas kernels  22.7 us (28%)
  blocking collectives  14.9 us (19%)
  waiting for transfers between devices  9.36 us (12%)
  between operations  0.83 us (1%)
    pallas_call x10, Pallas kernels, call(): pl.pallas_call(kernel, out_shape=out_shape, in_specs=[VMEM] * len(args),...  21.1 us
    all_to_all x1, blocking collectives, shards(): got = lax.all_to_all(spread, ('x', 'z'), 0, 0).astype(F32)  14.9 us
    all_to_all x1, starting transfers between devices, shards(): loss = lax.all_to_all(loss, ('y', 'core'), 0, 0)  11.5 us
    ppermute x7, starting transfers between devices, shift(): return lax.ppermute(a, 'z', [(i, (i + by) % NZ) for i in range(NZ)])  11.4 us
    ppermute x3, starting transfers between devices, partner(): return lax.ppermute(a, 'x', [(i, NX - 1 - i) for i in range(NX)])  5.91 us
    ppermute x7, waiting for transfers between devices, shift(): return lax.ppermute(a, 'z', [(i, (i + by) % NZ) for i in range(NZ)])  4.27 us
    ppermute x3, waiting for transfers between devices, partner(): return lax.ppermute(a, 'x', [(i, NX - 1 - i) for i in range(NX)])  3.03 us
    ppermute x1, starting transfers between devices, shards(): beside = lax.ppermute(mine, 'x', [(i, i ^ 1) for i in range(NX)])  2.13 us
  transfers between devices with their start and end apart: 12, of which 4 were waited for; matrix products, arithmetic and copies ran while one was open for 0% of the time, Pallas kernels for 23%

profile of v5, /device:TPU:1, one launch (start us, length us, event | category | flops | bytes accessed | tf_op | source)
XLA Modules:
  0.0 79.5 jit_solution(171528647444346136)
XLA Ops:
  0.6 1.6 %prepare.1 = (bf16[304,128]{1,0:T(8,128)(2,1)S(1)}, bf16[4,528,128]{2,1,0:T(8,128)(2,1)S(1)}) custom-call(s32[4]{0:T(128)} %own_hbm.1, bf16[4,64,128]{2,1,0:T(8,128)(2,1)} %bitcast.13, bf16[4,512,128]{2,1,0:T(8,128)(2,1)} %bitcast.12), custom_call_target="tpu_custom_call" | custom-call | tf_op jit(solution)/shard_map/prepare/pallas_call | solution.py:359
  2.2 2.1 %collective-permute-start = (bf16[304,128]{1,0:T(8,128)(2,1)S(1)}, bf16[304,128]{1,0:T(8,128)(2,1)S(1)}, u32[]{:S(2)}, u32[]{:S(2)}) collective-permute-start(bf16[304,128]{1,0:T(8,128)(2,1)S(1)} %get-tuple-element.53.mine.mine_ref), channel_id=1, source_target_pairs={{0,64},{64,0},{128,192},{192,128},{1,65},{65,1},{129,193},{193,129... | collective-permute-start | bytes 233480 | tf_op jit(solution)/shard_map/ppermute | solution.py:385
  4.3 1.8 %collective-permute-start.5 = (bf16[4,528,128]{2,1,0:T(8,128)(2,1)S(1)}, bf16[4,528,128]{2,1,0:T(8,128)(2,1)S(1)}, u32[]{:S(2)}, u32[]{:S(2)}) collective-permute-start(bf16[4,528,128]{2,1,0:T(8,128)(2,1)S(1)} %get-tuple-element.52.q_ref.q0), channel_id=1, source_target_pairs={{0,192},{64,128},{128,64},{192,0},{1,193},{65,129},{129,65},{193,1... | collective-permute-start | bytes 1622024 | tf_op jit(solution)/shard_map/ppermute | solution.py:380
  6.2 5.9 %collective-permute-start.2 = (bf16[2,304,128]{2,1,0:T(8,128)(2,1)S(1)}, bf16[2,304,128]{2,1,0:T(8,128)(2,1)S(1)}, u32[]{:S(2)}, u32[]{:S(2)}) collective-permute-start(bf16[2,304,128]{2,1,0:T(8,128)(2,1)S(1)} %join.1.half), channel_id=1, source_target_pairs={{0,56},{8,0},{16,8},{24,16},{32,24},{40,32},{48,40},{56,48},{1,57}... | collective-permute-start | bytes 466952 | tf_op jit(solution)/shard_map/ppermute | solution.py:383
  12.1 1.3 %first.1 = (f32[4,8,512]{2,1,0:T(8,128)S(1)}, f32[4,8,512]{2,1,0:T(8,128)S(1)}, f32[4,8,512]{2,1,0:T(8,128)S(1)}) custom-call(bf16[4,528,128]{2,1,0:T(8,128)(2,1)S(1)} %get-tuple-element.52.q_ref.q0, bf16[304,128]{1,0:T(8,128)(2,1)S(1)} %get-tuple-element.53.mine.mine_ref, bf16[2,304,128]{2,1,0:T(8,128)(2,1)S(1)} %join.1.half), custom_call_target="tpu_custom_call" | custom-call | flops 268435456 | bytes 1048576 | tf_op jit(solution)/shard_map/first/pallas_call | solution.py:341
  13.4 0.8 %collective-permute-done.2.ahead = bf16[2,304,128]{2,1,0:T(8,128)(2,1)S(1)} collective-permute-done((bf16[2,304,128]{2,1,0:T(8,128)(2,1)S(1)}, bf16[2,304,128]{2,1,0:T(8,128)(2,1)S(1)}, u32[]{:S(2)}, u32[]{:S(2)}) %collective-permute-start.2) | collective-permute-done | bytes 155680 | tf_op jit(solution)/shard_map/ppermute | solution.py:383
  14.2 3.4 %collective-permute-done.1.back = bf16[2,304,128]{2,1,0:T(8,128)(2,1)S(1)} collective-permute-done((bf16[2,304,128]{2,1,0:T(8,128)(2,1)S(1)}, bf16[2,304,128]{2,1,0:T(8,128)(2,1)S(1)}, u32[]{:S(2)}, u32[]{:S(2)}) %collective-permute-start.1) | collective-permute-done | bytes 155680 | tf_op jit(solution)/shard_map/ppermute | solution.py:383
  17.6 2.7 %collective-permute-start.4 = (bf16[2,304,128]{2,1,0:T(8,128)(2,1)S(1)}, bf16[2,304,128]{2,1,0:T(8,128)(2,1)S(1)}, u32[]{:S(2)}, u32[]{:S(2)}) collective-permute-start(bf16[2,304,128]{2,1,0:T(8,128)(2,1)S(1)} %collective-permute-done.2.ahead), channel_id=1, source_target_pairs={{0,56},{8,0},{16,8},{24,16},{32,24},{40,32},{48,40},{56,48},{1,57}... | collective-permute-start | bytes 466952 | tf_op jit(solution)/shard_map/ppermute | solution.py:383
  20.3 2.0 %middle.1 = (f32[4,16,512]{2,1,0:T(8,128)S(1)}, f32[4,8,512]{2,1,0:T(8,128)S(1)}, f32[4,8,512]{2,1,0:T(8,128)S(1)}) custom-call(bf16[4,528,128]{2,1,0:T(8,128)(2,1)S(1)} %get-tuple-element.52.q_ref.q0, f32[4,8,512]{2,1,0:T(8,128)S(1)} %get-tuple-element.57.acc_in, f32[4,8,512]{2,1,0:T(8,128)S(1)} %get-tuple-element.58.ref_in, ...), custom_call_target="tpu_custom_call" | custom-call | flops 536870912 | bytes 1048576 | tf_op jit(solution)/shard_map/middle/pallas_call | solution.py:341
  22.3 2.8 %partner_first.1 = (f32[4,24,512]{2,1,0:T(8,128)S(1)}, f32[4,8,512]{2,1,0:T(8,128)S(1)}, f32[4,8,512]{2,1,0:T(8,128)S(1)}) custom-call(bf16[4,528,128]{2,1,0:T(8,128)(2,1)S(1)} %collective-permute-done.5.q_ref.q1, bf16[2,304,128]{2,1,0:T(8,128)(2,1)S(1)} %join.1.half, bf16[2,304,128]{2,1,0:T(8,128)(2,1)S(1)} %collective-permute-done.1.back, ...), custom_call_target="tpu_custom_call" | custom-call | flops 805306368 | bytes 1048576 | tf_op jit(solution)/shard_map/partner_first/pallas_call | solution.py:341
  25.3 2.7 %collective-permute-start.7 = (bf16[2,304,128]{2,1,0:T(8,128)(2,1)S(1)}, bf16[2,304,128]{2,1,0:T(8,128)(2,1)S(1)}, u32[]{:S(2)}, u32[]{:S(2)}) collective-permute-start(bf16[2,304,128]{2,1,0:T(8,128)(2,1)S(1)} %collective-permute-done.4.ahead), channel_id=1, source_target_pairs={{0,56},{8,0},{16,8},{24,16},{32,24},{40,32},{48,40},{56,48},{1,57}... | collective-permute-start | bytes 466952 | tf_op jit(solution)/shard_map/ppermute | solution.py:383
  27.9 3.6 %both.2 = (f32[4,16,512]{2,1,0:T(8,128)S(1)}, f32[4,8,512]{2,1,0:T(8,128)S(1)}, f32[4,8,512]{2,1,0:T(8,128)S(1)}, f32[4,16,512]{2,1,0:T(8,128)S(1)}, f32[4,8,512]{2,1,0:T(8,128)S(1)}, /*index=5*/f32[4,8,512]{2,1,0:T(8,128)S(1)}) custom-call(bf16[4,528,128]{2,1,0:T(8,128)(2,1)S(1)} %get-tuple-element.52.q_ref.q0, f32[4,8,512]{2,1,0:T(8,128)S(1)} %get-tuple-element.66.acc0, ...), custom_call_target="tpu_custom_call" | custom-call | flops 1073741824 | bytes 1048576 | tf_op jit(solution)/shard_map/both/pallas_call | solution.py:341
  31.7 2.5 %collective-permute-start.10 = (bf16[14,48,128]{2,1,0:T(8,128)(2,1)S(1)}, bf16[14,48,128]{2,1,0:T(8,128)(2,1)S(1)}, u32[]{:S(2)}, u32[]{:S(2)}) collective-permute-start(bf16[14,48,128]{2,1,0:T(8,128)(2,1)S(1)} %slice_dynamic-update-slice_fusion.1.mine), channel_id=1, source_target_pairs={{0,192},{64,128},{128,64},{192,0},{1,193},{65,129},{129,65},{193,1... | collective-permute-start | bytes 516104 | tf_op jit(solution)/shard_map/ppermute | solution.py:380
  34.3 3.7 %both.3 = (f32[4,16,512]{2,1,0:T(8,128)S(1)}, f32[4,8,512]{2,1,0:T(8,128)S(1)}, f32[4,8,512]{2,1,0:T(8,128)S(1)}, f32[4,16,512]{2,1,0:T(8,128)S(1)}, f32[4,8,512]{2,1,0:T(8,128)S(1)}, /*index=5*/f32[4,8,512]{2,1,0:T(8,128)S(1)}) custom-call(bf16[4,528,128]{2,1,0:T(8,128)(2,1)S(1)} %get-tuple-element.52.q_ref.q0, f32[4,8,512]{2,1,0:T(8,128)S(1)} %get-tuple-element.73.acc0, ...), custom_call_target="tpu_custom_call" | custom-call | flops 1073741824 | bytes 1048576 | tf_op jit(solution)/shard_map/both/pallas_call | solution.py:341
  38.0 2.2 %last_rows.1 = (f32[4,8,512]{2,1,0:T(8,128)S(1)}, f32[4,8,512]{2,1,0:T(8,128)S(1)}, f32[40,512]{1,0:T(8,128)S(1)}) custom-call(bf16[4,528,128]{2,1,0:T(8,128)(2,1)S(1)} %get-tuple-element.52.q_ref.q0, f32[4,8,512]{2,1,0:T(8,128)S(1)} %get-tuple-element.81.acc0, f32[4,8,512]{2,1,0:T(8,128)S(1)} %get-tuple-element.82.ref0, ...), custom_call_target="tpu_custom_call" | custom-call | flops 536870912 | bytes 1048576 | tf_op jit(solution)/shard_map/last_rows/pallas_call | solution.py:341
  40.2 1.6 %collective-permute-start.9 = (f32[40,512]{1,0:T(8,128)S(1)}, f32[40,512]{1,0:T(8,128)S(1)}, u32[]{:S(2)}, u32[]{:S(2)}) collective-permute-start(f32[40,512]{1,0:T(8,128)S(1)} %get-tuple-element.85.stat), channel_id=1, source_target_pairs={{0,192},{64,128},{128,64},{192,0},{1,193},{65,129},{129,65},{193,1... | collective-permute-start | bytes 245768 | tf_op jit(solution)/shard_map/ppermute | solution.py:380
  41.8 3.0 %collective-permute-done.9.other.stat = f32[40,512]{1,0:T(8,128)S(1)} collective-permute-done((f32[40,512]{1,0:T(8,128)S(1)}, f32[40,512]{1,0:T(8,128)S(1)}, u32[]{:S(2)}, u32[]{:S(2)}) %collective-permute-start.9) | collective-permute-done | bytes 81952 | tf_op jit(solution)/shard_map/ppermute | solution.py:380
  44.8 0.9 %pool.1 = f32[32,128]{1,0:T(8,128)S(1)} custom-call(f32[40,512]{1,0:T(8,128)S(1)} %get-tuple-element.85.stat, f32[40,512]{1,0:T(8,128)S(1)} %collective-permute-done.9.other.stat, f32[4,8,512]{2,1,0:T(8,128)S(1)} %get-tuple-element.87.refs_0_, f32[4,16,512]{2,1,0:T(8,128)S(1)} %get-tuple-element.88.refs_1_, f32[4,16,512]{2,1,0:T(8,128)S(1)} %get-tuple-element.89.refs_2_, ...), custom_call_target="tpu_custom_call" | custom-call | flops 67108864 | bytes 1048576 | tf_op jit(solution)/shard_map/pool/pallas_call | solution.py:341
  45.8 14.9 %all_to_all.10 = f16[32,32,128]{2,1,0:T(8,128)(2,1)S(1)} all-to-all(f16[32,32,128]{2,1,0:T(8,128)(2,1)S(1)} %broadcast_in_dim.12), channel_id=1, replica_groups=mesh['x'=4,'z'=8,'y'=4,'core'=2] {'x','z'}, dimensions={0} | all-to-all | bytes 524288 | tf_op jit(solution)/shard_map/all_to_all | solution.py:434
  60.7 1.9 %head_loss.1 = (f32[8,8,128]{2,1,0:T(8,128)}, f32[1024,128]{1,0:T(8,128)S(1)}) custom-call(f32[32,32,128]{2,1,0:T(8,128)S(1)} %convert_element_type.7.got_ref, bf16[14,48,128]{2,1,0:T(8,128)(2,1)S(1)} %slice_dynamic-update-slice_fusion.1.mine, bf16[14,48,128]{2,1,0:T(8,128)(2,1)S(1)} %collective-permute-done.10.other, ...), custom_call_target="tpu_custom_call" | custom-call | flops 268435456 | bytes 1048576 | tf_op jit(solution)/shard_map/head_loss/pallas_call | solution.py:341
  62.6 11.5 %all-to-all-start.1 = ((f32[8,8,128]{2,1,0:T(8,128)}), f32[8,8,128]{2,1,0:T(8,128)S(1)}, u32[]{:S(2)}, u32[]{:S(2)}) async-start(f32[8,8,128]{2,1,0:T(8,128)} %get-tuple-element.97), calls=%async_computation.1 | async-start | bytes 65536 | tf_op jit(solution)/shard_map/all_to_all | solution.py:440
  74.1 2.7 %finish.1 = (f32[128,128]{1,0:T(8,128)}, f32[384,128]{1,0:T(8,128)}) custom-call(f32[32,32,128]{2,1,0:T(8,128)S(1)} %convert_element_type.7.got_ref, f32[1024,128]{1,0:T(8,128)S(1)} %get-tuple-element.98.logp_ref, bf16[14,48,128]{2,1,0:T(8,128)(2,1)S(1)} %slice_dynamic-update-slice_fusion.1.mine, bf16[14,48,128]{2,1,0:T(8,128)(2,1)S(1)} %collective-permute-done.10.other, ...), custom_call_target="tpu_custom_call" | custom-call | flops 268435456 | bytes 1048576 | tf_op jit(solution)/shard_map/finish/pallas_call | solution.py:341
  76.8 2.1 %all-to-all-done.1 = f32[8,8,128]{2,1,0:T(8,128)S(1)} async-done(((f32[8,8,128]{2,1,0:T(8,128)}), f32[8,8,128]{2,1,0:T(8,128)S(1)}, u32[]{:S(2)}, u32[]{:S(2)}) %all-to-all-start.1) | async-done | bytes 32800 | tf_op jit(solution)/shard_map/all_to_all | solution.py:440
  78.8 0.6 slice_reduce_fusion
  (27 shorter events, 0.4 us)
Async XLA Ops:
  2.2 3.9 %collective-permute-start = (bf16[304,128]{1,0:T(8,128)(2,1)S(1)}, bf16[304,128]{1,0:T(8,128)(2,1)S(1)}, u32[]{:S(2)}, u32[]{:S(2)}) collective-permute-start(bf16[304,128]{1,0:T(8,128)(2,1)S(1)} %get-tuple-element.53.mine.mine_ref), channel_id=1, source_target_pairs={{0,64},{64,0},{128,192},{192,128},{1,65},{65,1},{129,193},{193,129... | collective-permute-start | bytes 233480 | tf_op jit(solution)/shard_map/ppermute | solution.py:385
  4.3 18.0 %collective-permute-start.5 = (bf16[4,528,128]{2,1,0:T(8,128)(2,1)S(1)}, bf16[4,528,128]{2,1,0:T(8,128)(2,1)S(1)}, u32[]{:S(2)}, u32[]{:S(2)}) collective-permute-start(bf16[4,528,128]{2,1,0:T(8,128)(2,1)S(1)} %get-tuple-element.52.q_ref.q0), channel_id=1, source_target_pairs={{0,192},{64,128},{128,64},{192,0},{1,193},{65,129},{129,65},{193,1... | collective-permute-start | bytes 1622024 | tf_op jit(solution)/shard_map/ppermute | solution.py:380
  6.2 8.0 %collective-permute-start.2 = (bf16[2,304,128]{2,1,0:T(8,128)(2,1)S(1)}, bf16[2,304,128]{2,1,0:T(8,128)(2,1)S(1)}, u32[]{:S(2)}, u32[]{:S(2)}) collective-permute-start(bf16[2,304,128]{2,1,0:T(8,128)(2,1)S(1)} %join.1.half), channel_id=1, source_target_pairs={{0,56},{8,0},{16,8},{24,16},{32,24},{40,32},{48,40},{56,48},{1,57}... | collective-permute-start | bytes 466952 | tf_op jit(solution)/shard_map/ppermute | solution.py:383
  12.1 5.6 %collective-permute-start.1 = (bf16[2,304,128]{2,1,0:T(8,128)(2,1)S(1)}, bf16[2,304,128]{2,1,0:T(8,128)(2,1)S(1)}, u32[]{:S(2)}, u32[]{:S(2)}) collective-permute-start(bf16[2,304,128]{2,1,0:T(8,128)(2,1)S(1)} %join.1.half), channel_id=1, source_target_pairs={{0,8},{8,16},{16,24},{24,32},{32,40},{40,48},{48,56},{56,0},{1,9},... | collective-permute-start | bytes 466952 | tf_op jit(solution)/shard_map/ppermute | solution.py:383
  17.6 7.5 %collective-permute-start.3 = (bf16[2,304,128]{2,1,0:T(8,128)(2,1)S(1)}, bf16[2,304,128]{2,1,0:T(8,128)(2,1)S(1)}, u32[]{:S(2)}, u32[]{:S(2)}) collective-permute-start(bf16[2,304,128]{2,1,0:T(8,128)(2,1)S(1)} %collective-permute-done.1.back), channel_id=1, source_target_pairs={{0,8},{8,16},{16,24},{24,32},{32,40},{40,48},{48,56},{56,0},{1,9},... | collective-permute-start | bytes 466952 | tf_op jit(solution)/shard_map/ppermute | solution.py:383
  17.6 7.5 %collective-permute-start.4 = (bf16[2,304,128]{2,1,0:T(8,128)(2,1)S(1)}, bf16[2,304,128]{2,1,0:T(8,128)(2,1)S(1)}, u32[]{:S(2)}, u32[]{:S(2)}) collective-permute-start(bf16[2,304,128]{2,1,0:T(8,128)(2,1)S(1)} %collective-permute-done.2.ahead), channel_id=1, source_target_pairs={{0,56},{8,0},{16,8},{24,16},{32,24},{40,32},{48,40},{56,48},{1,57}... | collective-permute-start | bytes 466952 | tf_op jit(solution)/shard_map/ppermute | solution.py:383
  25.2 6.4 %collective-permute-start.6 = (bf16[2,304,128]{2,1,0:T(8,128)(2,1)S(1)}, bf16[2,304,128]{2,1,0:T(8,128)(2,1)S(1)}, u32[]{:S(2)}, u32[]{:S(2)}) collective-permute-start(bf16[2,304,128]{2,1,0:T(8,128)(2,1)S(1)} %collective-permute-done.3.back), channel_id=1, source_target_pairs={{0,8},{8,16},{16,24},{24,32},{32,40},{40,48},{48,56},{56,0},{1,9},... | collective-permute-start | bytes 466952 | tf_op jit(solution)/shard_map/ppermute | solution.py:383
  25.3 6.3 %collective-permute-start.7 = (bf16[2,304,128]{2,1,0:T(8,128)(2,1)S(1)}, bf16[2,304,128]{2,1,0:T(8,128)(2,1)S(1)}, u32[]{:S(2)}, u32[]{:S(2)}) collective-permute-start(bf16[2,304,128]{2,1,0:T(8,128)(2,1)S(1)} %collective-permute-done.4.ahead), channel_id=1, source_target_pairs={{0,56},{8,0},{16,8},{24,16},{32,24},{40,32},{48,40},{56,48},{1,57}... | collective-permute-start | bytes 466952 | tf_op jit(solution)/shard_map/ppermute | solution.py:383
  31.6 6.3 %collective-permute-start.8 = (bf16[2,304,128]{2,1,0:T(8,128)(2,1)S(1)}, bf16[2,304,128]{2,1,0:T(8,128)(2,1)S(1)}, u32[]{:S(2)}, u32[]{:S(2)}) collective-permute-start(bf16[2,304,128]{2,1,0:T(8,128)(2,1)S(1)} %collective-permute-done.6.back), channel_id=1, source_target_pairs={{0,8},{8,16},{16,24},{24,32},{32,40},{40,48},{48,56},{56,0},{1,9},... | collective-permute-start | bytes 466952 | tf_op jit(solution)/shard_map/ppermute | solution.py:383
  31.7 10.0 %collective-permute-start.10 = (bf16[14,48,128]{2,1,0:T(8,128)(2,1)S(1)}, bf16[14,48,128]{2,1,0:T(8,128)(2,1)S(1)}, u32[]{:S(2)}, u32[]{:S(2)}) collective-permute-start(bf16[14,48,128]{2,1,0:T(8,128)(2,1)S(1)} %slice_dynamic-update-slice_fusion.1.mine), channel_id=1, source_target_pairs={{0,192},{64,128},{128,64},{192,0},{1,193},{65,129},{129,65},{193,1... | collective-permute-start | bytes 516104 | tf_op jit(solution)/shard_map/ppermute | solution.py:380
  37.9 6.8 %copy-start = (bf16[1,384,128]{2,1,0:T(8,128)(2,1)S(1)}, bf16[1,384,128]{2,1,0:T(8,128)(2,1)}, u32[]{:S(2)}) copy-start(bf16[1,384,128]{2,1,0:T(8,128)(2,1)} %param.9) | copy-start | bytes 294916
  38.0 6.8 %copy-start.1 = (bf16[1,128,128]{2,1,0:T(8,128)(2,1)S(1)}, bf16[1,128,128]{2,1,0:T(8,128)(2,1)}, u32[]{:S(2)}) copy-start(bf16[1,128,128]{2,1,0:T(8,128)(2,1)} %param.8) | copy-start | bytes 98308
  40.2 4.6 %collective-permute-start.9 = (f32[40,512]{1,0:T(8,128)S(1)}, f32[40,512]{1,0:T(8,128)S(1)}, u32[]{:S(2)}, u32[]{:S(2)}) collective-permute-start(f32[40,512]{1,0:T(8,128)S(1)} %get-tuple-element.85.stat), channel_id=1, source_target_pairs={{0,192},{64,128},{128,64},{192,0},{1,193},{65,129},{129,65},{193,1... | collective-permute-start | bytes 245768 | tf_op jit(solution)/shard_map/ppermute | solution.py:380
  62.6 16.2 %all-to-all-start.1 = ((f32[8,8,128]{2,1,0:T(8,128)}), f32[8,8,128]{2,1,0:T(8,128)S(1)}, u32[]{:S(2)}, u32[]{:S(2)}) async-start(f32[8,8,128]{2,1,0:T(8,128)} %get-tuple-element.97), calls=%async_computation.1 | async-start | bytes 65536 | tf_op jit(solution)/shard_map/all_to_all | solution.py:440

commit v6 on v5

--- a/solution.py
+++ b/solution.py
@@ -53,8 +53,8 @@
     ]
     for copy in copies:
         copy.start()
-    for copy in copies:
-        copy.wait()
+    copies[0].wait()
+    copies[1].wait()
     keys = keys_ref[...]
     blocks = keys.astype(F32)
     kmax = jnp.max(blocks, axis=1)
@@ -63,9 +63,11 @@
     pos = [jnp.full((1, WIDTH), own_sm[b].astype(F32), F32) for b in range(LOCAL)]
     sub = lax.broadcasted_iota(jnp.int32, (BLOCK, LANES), 0)
     tok = lax.broadcasted_iota(jnp.int32, (BLOCK, LANES), 1) // GROUP
+    copies[2].wait()
     for b in range(LOCAL):
         s = jnp.where(sub > tok, MASKED, dot(keys[b], q_ref[b], NT))
         ref = jnp.max(s, axis=0, keepdims=True)
+        ref = ref - jnp.abs(ref) * (1.0 / 128)
         rows = [ref[:, i * WIDTH : (i + 1) * WIDTH] for i in range(LANES // WIDTH)]
         rows += [pos[b], jnp.zeros((11, WIDTH), F32)]
         qx_ref[b, :LANES, :] = q_ref[b]
@@ -170,24 +172,28 @@
         for job in jobs:
 
             def again(b, _, job=job):
-                ref, acc = job[2](b)
+                ref, _ = job[2](b)
                 high = jnp.maximum(ref, jnp.max(job[3][b], axis=0, keepdims=True))
-                run(job, b, high, acc * jnp.exp2((ref - high) * EXP2), False)
+                run(job, b, *job[2](b, high), False)
                 return 0
 
             lax.fori_loop(0, LOCAL, again, 0)
 
 
 def held(ref_in, acc_in):
-    return lambda b: (ref_in[b], acc_in[b])
+    def state(b, high=None):
+        ref, acc = ref_in[b], acc_in[b]
+        return (ref, acc) if high is None else (high, acc * jnp.exp2((ref - high) * EXP2))
+
+    return state
 
 
 def first(q_ref, mine_ref, half, bm_ref, acc_ref, ref_ref, diags):
     sub = lax.broadcasted_iota(jnp.int32, (BLOCK, LANES), 0)
     tok = lax.broadcasted_iota(jnp.int32, (BLOCK, LANES), 1) // GROUP
 
-    def state(b):
-        _, ref = start_of(q_ref, b)
+    def state(b, high=None):
+        ref = start_of(q_ref, b)[1] if high is None else high
         s = jnp.where(sub > tok, MASKED, dot(mine_ref[pl.ds(pl.multiple_of(b * BLOCK, BLOCK), BLOCK), :], q_ref[b, :LANES, :], NT))
         diags[b] = jnp.broadcast_to(jnp.max(s, axis=0, keepdims=True), (8, LANES))
         e = jnp.exp2((s.reshape(BLOCK // 8, 8, LANES) - ref) * EXP2)
@@ -197,8 +203,8 @@
 
 
 def partner_first(q_ref, half, back, ahead, bm_ref, acc_ref, ref_ref):
-    def state(b):
-        return start_of(q_ref, b)[1], jnp.zeros((8, LANES), F32)
+    def state(b, high=None):
+        return start_of(q_ref, b)[1] if high is None else high, jnp.zeros((8, LANES), F32)
 
     sweep(([half, back, ahead], q_ref, state, bm_ref, acc_ref, ref_ref, None))
 

time: 79.7 us -> 79.6 us (level)
  no operation moved by 1% of the time
where the time goes in v6:
time: 79.6 us; the launch traced here: 79.4 us
  starting transfers between devices  31 us (39%)
  Pallas kernels  22.6 us (28%)
  blocking collectives  14.8 us (19%)
  waiting for transfers between devices  9.36 us (12%)
  between operations  0.83 us (1%)
    pallas_call x10, Pallas kernels, call(): pl.pallas_call(kernel, out_shape=out_shape, in_specs=[VMEM] * len(args),...  21.1 us
    all_to_all x1, blocking collectives, shards(): got = lax.all_to_all(spread, ('x', 'z'), 0, 0).astype(F32)  14.8 us
    all_to_all x1, starting transfers between devices, shards(): loss = lax.all_to_all(loss, ('y', 'core'), 0, 0)  11.6 us
    ppermute x7, starting transfers between devices, shift(): return lax.ppermute(a, 'z', [(i, (i + by) % NZ) for i in range(NZ)])  11.4 us
    ppermute x3, starting transfers between devices, partner(): return lax.ppermute(a, 'x', [(i, NX - 1 - i) for i in range(NX)])  5.94 us
    ppermute x7, waiting for transfers between devices, shift(): return lax.ppermute(a, 'z', [(i, (i + by) % NZ) for i in range(NZ)])  4.26 us
    ppermute x3, waiting for transfers between devices, partner(): return lax.ppermute(a, 'x', [(i, NX - 1 - i) for i in range(NX)])  3.03 us
    ppermute x1, starting transfers between devices, shards(): beside = lax.ppermute(mine, 'x', [(i, i ^ 1) for i in range(NX)])  2.13 us
  transfers between devices with their start and end apart: 12, of which 4 were waited for; matrix products, arithmetic and copies ran while one was open for 0% of the time, Pallas kernels for 23%

profile of v6, /device:TPU:1, one launch (start us, length us, event | category | flops | bytes accessed | tf_op | source)
XLA Modules:
  0.0 79.4 jit_solution(4785457345250097469)
XLA Ops:
  0.6 1.5 %prepare.1 = (bf16[304,128]{1,0:T(8,128)(2,1)S(1)}, bf16[4,528,128]{2,1,0:T(8,128)(2,1)S(1)}) custom-call(s32[4]{0:T(128)} %own_hbm.1, bf16[4,64,128]{2,1,0:T(8,128)(2,1)} %bitcast.13, bf16[4,512,128]{2,1,0:T(8,128)(2,1)} %bitcast.12), custom_call_target="tpu_custom_call" | custom-call | tf_op jit(solution)/shard_map/prepare/pallas_call | solution.py:365
  2.2 2.1 %collective-permute-start = (bf16[304,128]{1,0:T(8,128)(2,1)S(1)}, bf16[304,128]{1,0:T(8,128)(2,1)S(1)}, u32[]{:S(2)}, u32[]{:S(2)}) collective-permute-start(bf16[304,128]{1,0:T(8,128)(2,1)S(1)} %get-tuple-element.53.mine.mine_ref), channel_id=1, source_target_pairs={{0,64},{64,0},{128,192},{192,128},{1,65},{65,1},{129,193},{193,129... | collective-permute-start | bytes 233480 | tf_op jit(solution)/shard_map/ppermute | solution.py:391
  4.3 1.8 %collective-permute-start.5 = (bf16[4,528,128]{2,1,0:T(8,128)(2,1)S(1)}, bf16[4,528,128]{2,1,0:T(8,128)(2,1)S(1)}, u32[]{:S(2)}, u32[]{:S(2)}) collective-permute-start(bf16[4,528,128]{2,1,0:T(8,128)(2,1)S(1)} %get-tuple-element.52.q_ref.q0), channel_id=1, source_target_pairs={{0,192},{64,128},{128,64},{192,0},{1,193},{65,129},{129,65},{193,1... | collective-permute-start | bytes 1622024 | tf_op jit(solution)/shard_map/ppermute | solution.py:386
  6.2 5.9 %collective-permute-start.2 = (bf16[2,304,128]{2,1,0:T(8,128)(2,1)S(1)}, bf16[2,304,128]{2,1,0:T(8,128)(2,1)S(1)}, u32[]{:S(2)}, u32[]{:S(2)}) collective-permute-start(bf16[2,304,128]{2,1,0:T(8,128)(2,1)S(1)} %join.1.half), channel_id=1, source_target_pairs={{0,56},{8,0},{16,8},{24,16},{32,24},{40,32},{48,40},{56,48},{1,57}... | collective-permute-start | bytes 466952 | tf_op jit(solution)/shard_map/ppermute | solution.py:389
  12.0 1.3 %first.1 = (f32[4,8,512]{2,1,0:T(8,128)S(1)}, f32[4,8,512]{2,1,0:T(8,128)S(1)}, f32[4,8,512]{2,1,0:T(8,128)S(1)}) custom-call(bf16[4,528,128]{2,1,0:T(8,128)(2,1)S(1)} %get-tuple-element.52.q_ref.q0, bf16[304,128]{1,0:T(8,128)(2,1)S(1)} %get-tuple-element.53.mine.mine_ref, bf16[2,304,128]{2,1,0:T(8,128)(2,1)S(1)} %join.1.half), custom_call_target="tpu_custom_call" | custom-call | flops 268435456 | bytes 1048576 | tf_op jit(solution)/shard_map/first/pallas_call | solution.py:347
  13.3 0.8 %collective-permute-done.2.ahead = bf16[2,304,128]{2,1,0:T(8,128)(2,1)S(1)} collective-permute-done((bf16[2,304,128]{2,1,0:T(8,128)(2,1)S(1)}, bf16[2,304,128]{2,1,0:T(8,128)(2,1)S(1)}, u32[]{:S(2)}, u32[]{:S(2)}) %collective-permute-start.2) | collective-permute-done | bytes 155680 | tf_op jit(solution)/shard_map/ppermute | solution.py:389
  14.2 3.4 %collective-permute-done.1.back = bf16[2,304,128]{2,1,0:T(8,128)(2,1)S(1)} collective-permute-done((bf16[2,304,128]{2,1,0:T(8,128)(2,1)S(1)}, bf16[2,304,128]{2,1,0:T(8,128)(2,1)S(1)}, u32[]{:S(2)}, u32[]{:S(2)}) %collective-permute-start.1) | collective-permute-done | bytes 155680 | tf_op jit(solution)/shard_map/ppermute | solution.py:389
  17.6 2.7 %collective-permute-start.4 = (bf16[2,304,128]{2,1,0:T(8,128)(2,1)S(1)}, bf16[2,304,128]{2,1,0:T(8,128)(2,1)S(1)}, u32[]{:S(2)}, u32[]{:S(2)}) collective-permute-start(bf16[2,304,128]{2,1,0:T(8,128)(2,1)S(1)} %collective-permute-done.2.ahead), channel_id=1, source_target_pairs={{0,56},{8,0},{16,8},{24,16},{32,24},{40,32},{48,40},{56,48},{1,57}... | collective-permute-start | bytes 466952 | tf_op jit(solution)/shard_map/ppermute | solution.py:389
  20.3 2.0 %middle.1 = (f32[4,16,512]{2,1,0:T(8,128)S(1)}, f32[4,8,512]{2,1,0:T(8,128)S(1)}, f32[4,8,512]{2,1,0:T(8,128)S(1)}) custom-call(bf16[4,528,128]{2,1,0:T(8,128)(2,1)S(1)} %get-tuple-element.52.q_ref.q0, f32[4,8,512]{2,1,0:T(8,128)S(1)} %get-tuple-element.57.acc_in, f32[4,8,512]{2,1,0:T(8,128)S(1)} %get-tuple-element.58.ref_in, ...), custom_call_target="tpu_custom_call" | custom-call | flops 536870912 | bytes 1048576 | tf_op jit(solution)/shard_map/middle/pallas_call | solution.py:347
  22.3 2.8 %partner_first.1 = (f32[4,24,512]{2,1,0:T(8,128)S(1)}, f32[4,8,512]{2,1,0:T(8,128)S(1)}, f32[4,8,512]{2,1,0:T(8,128)S(1)}) custom-call(bf16[4,528,128]{2,1,0:T(8,128)(2,1)S(1)} %collective-permute-done.5.q_ref.q1, bf16[2,304,128]{2,1,0:T(8,128)(2,1)S(1)} %join.1.half, bf16[2,304,128]{2,1,0:T(8,128)(2,1)S(1)} %collective-permute-done.1.back, ...), custom_call_target="tpu_custom_call" | custom-call | flops 805306368 | bytes 1048576 | tf_op jit(solution)/shard_map/partner_first/pallas_call | solution.py:347
  25.2 2.7 %collective-permute-start.7 = (bf16[2,304,128]{2,1,0:T(8,128)(2,1)S(1)}, bf16[2,304,128]{2,1,0:T(8,128)(2,1)S(1)}, u32[]{:S(2)}, u32[]{:S(2)}) collective-permute-start(bf16[2,304,128]{2,1,0:T(8,128)(2,1)S(1)} %collective-permute-done.4.ahead), channel_id=1, source_target_pairs={{0,56},{8,0},{16,8},{24,16},{32,24},{40,32},{48,40},{56,48},{1,57}... | collective-permute-start | bytes 466952 | tf_op jit(solution)/shard_map/ppermute | solution.py:389
  27.9 3.6 %both.2 = (f32[4,16,512]{2,1,0:T(8,128)S(1)}, f32[4,8,512]{2,1,0:T(8,128)S(1)}, f32[4,8,512]{2,1,0:T(8,128)S(1)}, f32[4,16,512]{2,1,0:T(8,128)S(1)}, f32[4,8,512]{2,1,0:T(8,128)S(1)}, /*index=5*/f32[4,8,512]{2,1,0:T(8,128)S(1)}) custom-call(bf16[4,528,128]{2,1,0:T(8,128)(2,1)S(1)} %get-tuple-element.52.q_ref.q0, f32[4,8,512]{2,1,0:T(8,128)S(1)} %get-tuple-element.66.acc0, ...), custom_call_target="tpu_custom_call" | custom-call | flops 1073741824 | bytes 1048576 | tf_op jit(solution)/shard_map/both/pallas_call | solution.py:347
  31.7 2.6 %collective-permute-start.10 = (bf16[14,48,128]{2,1,0:T(8,128)(2,1)S(1)}, bf16[14,48,128]{2,1,0:T(8,128)(2,1)S(1)}, u32[]{:S(2)}, u32[]{:S(2)}) collective-permute-start(bf16[14,48,128]{2,1,0:T(8,128)(2,1)S(1)} %slice_dynamic-update-slice_fusion.1.mine), channel_id=1, source_target_pairs={{0,192},{64,128},{128,64},{192,0},{1,193},{65,129},{129,65},{193,1... | collective-permute-start | bytes 516104 | tf_op jit(solution)/shard_map/ppermute | solution.py:386
  34.2 3.7 %both.3 = (f32[4,16,512]{2,1,0:T(8,128)S(1)}, f32[4,8,512]{2,1,0:T(8,128)S(1)}, f32[4,8,512]{2,1,0:T(8,128)S(1)}, f32[4,16,512]{2,1,0:T(8,128)S(1)}, f32[4,8,512]{2,1,0:T(8,128)S(1)}, /*index=5*/f32[4,8,512]{2,1,0:T(8,128)S(1)}) custom-call(bf16[4,528,128]{2,1,0:T(8,128)(2,1)S(1)} %get-tuple-element.52.q_ref.q0, f32[4,8,512]{2,1,0:T(8,128)S(1)} %get-tuple-element.73.acc0, ...), custom_call_target="tpu_custom_call" | custom-call | flops 1073741824 | bytes 1048576 | tf_op jit(solution)/shard_map/both/pallas_call | solution.py:347
  37.9 2.2 %last_rows.1 = (f32[4,8,512]{2,1,0:T(8,128)S(1)}, f32[4,8,512]{2,1,0:T(8,128)S(1)}, f32[40,512]{1,0:T(8,128)S(1)}) custom-call(bf16[4,528,128]{2,1,0:T(8,128)(2,1)S(1)} %get-tuple-element.52.q_ref.q0, f32[4,8,512]{2,1,0:T(8,128)S(1)} %get-tuple-element.81.acc0, f32[4,8,512]{2,1,0:T(8,128)S(1)} %get-tuple-element.82.ref0, ...), custom_call_target="tpu_custom_call" | custom-call | flops 536870912 | bytes 1048576 | tf_op jit(solution)/shard_map/last_rows/pallas_call | solution.py:347
  40.2 1.6 %collective-permute-start.9 = (f32[40,512]{1,0:T(8,128)S(1)}, f32[40,512]{1,0:T(8,128)S(1)}, u32[]{:S(2)}, u32[]{:S(2)}) collective-permute-start(f32[40,512]{1,0:T(8,128)S(1)} %get-tuple-element.85.stat), channel_id=1, source_target_pairs={{0,192},{64,128},{128,64},{192,0},{1,193},{65,129},{129,65},{193,1... | collective-permute-start | bytes 245768 | tf_op jit(solution)/shard_map/ppermute | solution.py:386
  41.7 3.0 %collective-permute-done.9.other.stat = f32[40,512]{1,0:T(8,128)S(1)} collective-permute-done((f32[40,512]{1,0:T(8,128)S(1)}, f32[40,512]{1,0:T(8,128)S(1)}, u32[]{:S(2)}, u32[]{:S(2)}) %collective-permute-start.9) | collective-permute-done | bytes 81952 | tf_op jit(solution)/shard_map/ppermute | solution.py:386
  44.8 0.9 %pool.1 = f32[32,128]{1,0:T(8,128)S(1)} custom-call(f32[40,512]{1,0:T(8,128)S(1)} %get-tuple-element.85.stat, f32[40,512]{1,0:T(8,128)S(1)} %collective-permute-done.9.other.stat, f32[4,8,512]{2,1,0:T(8,128)S(1)} %get-tuple-element.87.refs_0_, f32[4,16,512]{2,1,0:T(8,128)S(1)} %get-tuple-element.88.refs_1_, f32[4,16,512]{2,1,0:T(8,128)S(1)} %get-tuple-element.89.refs_2_, ...), custom_call_target="tpu_custom_call" | custom-call | flops 67108864 | bytes 1048576 | tf_op jit(solution)/shard_map/pool/pallas_call | solution.py:347
  45.8 14.8 %all_to_all.10 = f16[32,32,128]{2,1,0:T(8,128)(2,1)S(1)} all-to-all(f16[32,32,128]{2,1,0:T(8,128)(2,1)S(1)} %broadcast_in_dim.12), channel_id=1, replica_groups=mesh['x'=4,'z'=8,'y'=4,'core'=2] {'x','z'}, dimensions={0} | all-to-all | bytes 524288 | tf_op jit(solution)/shard_map/all_to_all | solution.py:440
  60.7 1.9 %head_loss.1 = (f32[8,8,128]{2,1,0:T(8,128)}, f32[1024,128]{1,0:T(8,128)S(1)}) custom-call(f32[32,32,128]{2,1,0:T(8,128)S(1)} %convert_element_type.7.got_ref, bf16[14,48,128]{2,1,0:T(8,128)(2,1)S(1)} %slice_dynamic-update-slice_fusion.1.mine, bf16[14,48,128]{2,1,0:T(8,128)(2,1)S(1)} %collective-permute-done.10.other, ...), custom_call_target="tpu_custom_call" | custom-call | flops 268435456 | bytes 1048576 | tf_op jit(solution)/shard_map/head_loss/pallas_call | solution.py:347
  62.5 11.6 %all-to-all-start.1 = ((f32[8,8,128]{2,1,0:T(8,128)}), f32[8,8,128]{2,1,0:T(8,128)S(1)}, u32[]{:S(2)}, u32[]{:S(2)}) async-start(f32[8,8,128]{2,1,0:T(8,128)} %get-tuple-element.97), calls=%async_computation.1 | async-start | bytes 65536 | tf_op jit(solution)/shard_map/all_to_all | solution.py:446
  74.1 2.7 %finish.1 = (f32[128,128]{1,0:T(8,128)}, f32[384,128]{1,0:T(8,128)}) custom-call(f32[32,32,128]{2,1,0:T(8,128)S(1)} %convert_element_type.7.got_ref, f32[1024,128]{1,0:T(8,128)S(1)} %get-tuple-element.98.logp_ref, bf16[14,48,128]{2,1,0:T(8,128)(2,1)S(1)} %slice_dynamic-update-slice_fusion.1.mine, bf16[14,48,128]{2,1,0:T(8,128)(2,1)S(1)} %collective-permute-done.10.other, ...), custom_call_target="tpu_custom_call" | custom-call | flops 268435456 | bytes 1048576 | tf_op jit(solution)/shard_map/finish/pallas_call | solution.py:347
  76.7 2.1 %all-to-all-done.1 = f32[8,8,128]{2,1,0:T(8,128)S(1)} async-done(((f32[8,8,128]{2,1,0:T(8,128)}), f32[8,8,128]{2,1,0:T(8,128)S(1)}, u32[]{:S(2)}, u32[]{:S(2)}) %all-to-all-start.1) | async-done | bytes 32800 | tf_op jit(solution)/shard_map/all_to_all | solution.py:446
  78.8 0.6 slice_reduce_fusion
  (27 shorter events, 0.4 us)
Async XLA Ops:
  2.2 3.9 %collective-permute-start = (bf16[304,128]{1,0:T(8,128)(2,1)S(1)}, bf16[304,128]{1,0:T(8,128)(2,1)S(1)}, u32[]{:S(2)}, u32[]{:S(2)}) collective-permute-start(bf16[304,128]{1,0:T(8,128)(2,1)S(1)} %get-tuple-element.53.mine.mine_ref), channel_id=1, source_target_pairs={{0,64},{64,0},{128,192},{192,128},{1,65},{65,1},{129,193},{193,129... | collective-permute-start | bytes 233480 | tf_op jit(solution)/shard_map/ppermute | solution.py:391
  4.3 18.0 %collective-permute-start.5 = (bf16[4,528,128]{2,1,0:T(8,128)(2,1)S(1)}, bf16[4,528,128]{2,1,0:T(8,128)(2,1)S(1)}, u32[]{:S(2)}, u32[]{:S(2)}) collective-permute-start(bf16[4,528,128]{2,1,0:T(8,128)(2,1)S(1)} %get-tuple-element.52.q_ref.q0), channel_id=1, source_target_pairs={{0,192},{64,128},{128,64},{192,0},{1,193},{65,129},{129,65},{193,1... | collective-permute-start | bytes 1622024 | tf_op jit(solution)/shard_map/ppermute | solution.py:386
  6.2 8.0 %collective-permute-start.2 = (bf16[2,304,128]{2,1,0:T(8,128)(2,1)S(1)}, bf16[2,304,128]{2,1,0:T(8,128)(2,1)S(1)}, u32[]{:S(2)}, u32[]{:S(2)}) collective-permute-start(bf16[2,304,128]{2,1,0:T(8,128)(2,1)S(1)} %join.1.half), channel_id=1, source_target_pairs={{0,56},{8,0},{16,8},{24,16},{32,24},{40,32},{48,40},{56,48},{1,57}... | collective-permute-start | bytes 466952 | tf_op jit(solution)/shard_map/ppermute | solution.py:389
  12.0 5.6 %collective-permute-start.1 = (bf16[2,304,128]{2,1,0:T(8,128)(2,1)S(1)}, bf16[2,304,128]{2,1,0:T(8,128)(2,1)S(1)}, u32[]{:S(2)}, u32[]{:S(2)}) collective-permute-start(bf16[2,304,128]{2,1,0:T(8,128)(2,1)S(1)} %join.1.half), channel_id=1, source_target_pairs={{0,8},{8,16},{16,24},{24,32},{32,40},{40,48},{48,56},{56,0},{1,9},... | collective-permute-start | bytes 466952 | tf_op jit(solution)/shard_map/ppermute | solution.py:389
  17.6 7.5 %collective-permute-start.3 = (bf16[2,304,128]{2,1,0:T(8,128)(2,1)S(1)}, bf16[2,304,128]{2,1,0:T(8,128)(2,1)S(1)}, u32[]{:S(2)}, u32[]{:S(2)}) collective-permute-start(bf16[2,304,128]{2,1,0:T(8,128)(2,1)S(1)} %collective-permute-done.1.back), channel_id=1, source_target_pairs={{0,8},{8,16},{16,24},{24,32},{32,40},{40,48},{48,56},{56,0},{1,9},... | collective-permute-start | bytes 466952 | tf_op jit(solution)/shard_map/ppermute | solution.py:389
  17.6 7.5 %collective-permute-start.4 = (bf16[2,304,128]{2,1,0:T(8,128)(2,1)S(1)}, bf16[2,304,128]{2,1,0:T(8,128)(2,1)S(1)}, u32[]{:S(2)}, u32[]{:S(2)}) collective-permute-start(bf16[2,304,128]{2,1,0:T(8,128)(2,1)S(1)} %collective-permute-done.2.ahead), channel_id=1, source_target_pairs={{0,56},{8,0},{16,8},{24,16},{32,24},{40,32},{48,40},{56,48},{1,57}... | collective-permute-start | bytes 466952 | tf_op jit(solution)/shard_map/ppermute | solution.py:389
  25.1 6.4 %collective-permute-start.6 = (bf16[2,304,128]{2,1,0:T(8,128)(2,1)S(1)}, bf16[2,304,128]{2,1,0:T(8,128)(2,1)S(1)}, u32[]{:S(2)}, u32[]{:S(2)}) collective-permute-start(bf16[2,304,128]{2,1,0:T(8,128)(2,1)S(1)} %collective-permute-done.3.back), channel_id=1, source_target_pairs={{0,8},{8,16},{16,24},{24,32},{32,40},{40,48},{48,56},{56,0},{1,9},... | collective-permute-start | bytes 466952 | tf_op jit(solution)/shard_map/ppermute | solution.py:389
  25.2 6.3 %collective-permute-start.7 = (bf16[2,304,128]{2,1,0:T(8,128)(2,1)S(1)}, bf16[2,304,128]{2,1,0:T(8,128)(2,1)S(1)}, u32[]{:S(2)}, u32[]{:S(2)}) collective-permute-start(bf16[2,304,128]{2,1,0:T(8,128)(2,1)S(1)} %collective-permute-done.4.ahead), channel_id=1, source_target_pairs={{0,56},{8,0},{16,8},{24,16},{32,24},{40,32},{48,40},{56,48},{1,57}... | collective-permute-start | bytes 466952 | tf_op jit(solution)/shard_map/ppermute | solution.py:389
  31.5 6.3 %collective-permute-start.8 = (bf16[2,304,128]{2,1,0:T(8,128)(2,1)S(1)}, bf16[2,304,128]{2,1,0:T(8,128)(2,1)S(1)}, u32[]{:S(2)}, u32[]{:S(2)}) collective-permute-start(bf16[2,304,128]{2,1,0:T(8,128)(2,1)S(1)} %collective-permute-done.6.back), channel_id=1, source_target_pairs={{0,8},{8,16},{16,24},{24,32},{32,40},{40,48},{48,56},{56,0},{1,9},... | collective-permute-start | bytes 466952 | tf_op jit(solution)/shard_map/ppermute | solution.py:389
  31.7 10.0 %collective-permute-start.10 = (bf16[14,48,128]{2,1,0:T(8,128)(2,1)S(1)}, bf16[14,48,128]{2,1,0:T(8,128)(2,1)S(1)}, u32[]{:S(2)}, u32[]{:S(2)}) collective-permute-start(bf16[14,48,128]{2,1,0:T(8,128)(2,1)S(1)} %slice_dynamic-update-slice_fusion.1.mine), channel_id=1, source_target_pairs={{0,192},{64,128},{128,64},{192,0},{1,193},{65,129},{129,65},{193,1... | collective-permute-start | bytes 516104 | tf_op jit(solution)/shard_map/ppermute | solution.py:386
  37.9 6.8 %copy-start = (bf16[1,384,128]{2,1,0:T(8,128)(2,1)S(1)}, bf16[1,384,128]{2,1,0:T(8,128)(2,1)}, u32[]{:S(2)}) copy-start(bf16[1,384,128]{2,1,0:T(8,128)(2,1)} %param.9) | copy-start | bytes 294916
  37.9 6.8 %copy-start.1 = (bf16[1,128,128]{2,1,0:T(8,128)(2,1)S(1)}, bf16[1,128,128]{2,1,0:T(8,128)(2,1)}, u32[]{:S(2)}) copy-start(bf16[1,128,128]{2,1,0:T(8,128)(2,1)} %param.8) | copy-start | bytes 98308
  40.2 4.6 %collective-permute-start.9 = (f32[40,512]{1,0:T(8,128)S(1)}, f32[40,512]{1,0:T(8,128)S(1)}, u32[]{:S(2)}, u32[]{:S(2)}) collective-permute-start(f32[40,512]{1,0:T(8,128)S(1)} %get-tuple-element.85.stat), channel_id=1, source_target_pairs={{0,192},{64,128},{128,64},{192,0},{1,193},{65,129},{129,65},{193,1... | collective-permute-start | bytes 245768 | tf_op jit(solution)/shard_map/ppermute | solution.py:386
  62.5 16.3 %all-to-all-start.1 = ((f32[8,8,128]{2,1,0:T(8,128)}), f32[8,8,128]{2,1,0:T(8,128)S(1)}, u32[]{:S(2)}, u32[]{:S(2)}) async-start(f32[8,8,128]{2,1,0:T(8,128)} %get-tuple-element.97), calls=%async_computation.1 | async-start | bytes 65536 | tf_op jit(solution)/shard_map/all_to_all | solution.py:446
